TPU v7x, 256 devices: a whole 4x4x8 slice. The times are simulated.
256 devices in a mesh: clu: 64 (over z, y, core), row: 4 (over x).
Axes of the slice: x: 4, y: 4, z: 8, core: 2. Of those that a mesh axis runs over, the one named last changes fastest.
Arguments:
- embeddings: bfloat16 [131072, 1024], P(('clu', 'row')), may hold values from -400 to 400
- cluster: int32 [131072], P(('clu', 'row')), may hold values from 0 to 63, as said below
- doc_rank: int32 [131072], P(('clu', 'row')), may hold values from 0 to 131071, each once
Outputs:
- nearest_earlier: float32 [131072], P(('clu', 'row'))
Inputs may be any that keep to these rules, and one draw needn't show every extreme that they name: The 512 documents of one device name any one cluster at most 16 times; one cluster is named exactly 16 times by every device, so it holds 4096 documents. `doc_rank`: all ranks differ.
All inputs are finite; a program needn't handle non-finite values.
Results may differ from a plain program's by a relative error of at most 0.00056.
Values may be sent and summed in bfloat16 or wider, within the bound.
No kernel may reach another device: no remote copies, remote signals or barrier semaphores. Data moves between devices by JAX's collectives and lax.ppermute only.
A program may use at most 64 MiB of HBM per device.

v0:
```python
import jax
import jax.numpy as jnp
from jax import lax
from jax.sharding import PartitionSpec as P


def compare(queries, key_rows):
    return lax.dot_general(
        queries, key_rows, (((1,), (1,)), ((), ())), preferred_element_type=jnp.float32
    )


def per_device(embeddings, cluster, doc_rank):
    owners = lax.axis_size("clu")
    doc_count = embeddings.shape[0]
    features = embeddings.shape[1]
    capacity = 2 * doc_count // owners
    widened = embeddings.astype(jnp.float32)
    squares_eps = jnp.sum(widened * widened, axis=1, keepdims=True) + 1e-06
    unit_rows = (widened * lax.rsqrt(squares_eps)).astype(jnp.bfloat16)
    member = (cluster[:, None] == jnp.arange(owners, dtype=jnp.int32)[None, :]).astype(jnp.int32)
    before = jnp.cumsum(member, axis=0) - member
    within = jnp.sum(before * member, axis=1)
    position = cluster * capacity + within
    outgoing = jnp.zeros((owners * capacity, features), jnp.bfloat16).at[position].set(unit_rows)
    out_ranks = jnp.full((owners * capacity,), -1, jnp.int32).at[position].set(doc_rank)
    arrived, arrived_ranks = (
        lax.all_to_all(
            outgoing.reshape(owners, capacity, features),
            "clu",
            split_axis=0,
            concat_axis=0,
            tiled=True,
        ),
        lax.all_to_all(
            out_ranks.reshape(owners, capacity), "clu", split_axis=0, concat_axis=0, tiled=True
        ),
    )
    queries = arrived.reshape(owners * capacity, features)
    query_ranks = arrived_ranks.reshape(owners * capacity)
    best_sim = jnp.full((owners * capacity,), -1.0, jnp.float32)
    key_rows = lax.all_gather(queries, "row", axis=0, tiled=True)
    key_ranks = lax.all_gather(query_ranks, "row", axis=0, tiled=True)
    scores = compare(queries, key_rows)
    earlier = (key_ranks[None, :] >= 0) & (key_ranks[None, :] < query_ranks[:, None])
    best_sim = jnp.maximum(best_sim, jnp.max(jnp.where(earlier, scores, -1.0), axis=1))
    outcome = lax.all_to_all(
        best_sim.reshape(owners, capacity), "clu", split_axis=0, concat_axis=0, tiled=True
    )
    return outcome.reshape(owners * capacity)[position]


def solution(mesh):
    placed = (P(("clu", "row"), None), P(("clu", "row")), P(("clu", "row")))
    return jax.shard_map(
        per_device, mesh=mesh, in_specs=placed, out_specs=P(("clu", "row")), check_vma=False
    )
```

profile of v0, /device:TPU:1, one launch (start us, length us, event | category | flops | bytes accessed | tf_op | source)
XLA Modules:
  0.0 205.9 jit_solution(14560138137701401269)
XLA Ops:
  6.5 0.0 copy-start.1
  6.5 0.0 all-gather.2.cloned.1.call-start
  6.5 0.8 fusion.9
  7.3 1.2 reduce-window.6
  8.5 0.2 slice_reduce_fusion
  8.8 0.8 fusion.8
  9.6 0.7 compare_select_fusion
  10.3 1.5 fusion
  11.8 0.0 copy-done.1
  11.8 3.3 %scatter_custom_fusion.1 = bf16[1024,1024]{1,0:T(8,128)(2,1)S(1)} fusion(s32[512]{0:T(512)S(1)} %compare_select_fusion, bf16[512,1024]{1,0:T(8,128)(2,1)S(1)} %copy-done.1, f32[512]{0:T(512)S(1)} %add_rsqrt_fusion, bf16[]{:T(256)} %constant.3.clone.1), kind=kCustom, calls=%fused_computation.8 | custom fusion | flops 1572864 | bytes 3147778 | tf_op jit(solution)/shard_map/scatter | solution.py:25
  15.1 62.7 %all_to_all.20 = bf16[64,16,1024]{2,1,0:T(8,128)(2,1)} all-to-all(bf16[64,16,1024]{2,1,0:T(8,128)(2,1)S(1)} %bitcast.28), channel_id=1, replica_groups=mesh['clu'=64,'row'=4] {'clu'}, dimensions={0} | all-to-all | bytes 4194304 | tf_op jit(solution)/shard_map/all_to_all | solution.py:28
  77.9 0.0 copy-start
  77.9 0.0 all-gather.2.cloned.1.call-update
  77.9 2.7 %scatter_custom_fusion = s32[1024]{0:T(1024)S(1)} fusion(s32[512]{0:T(512)S(1)} %compare_select_fusion, s32[512]{0:T(512)} %param.5, s32[]{:T(128)} %constant.9.clone.1), kind=kCustom, calls=%fused_computation.25 | custom fusion | bytes 4608 | tf_op jit(solution)/shard_map/scatter | solution.py:26
  80.6 0.1 all_to_all.13
  80.7 16.2 %all_to_all.21 = s32[64,1,16]{2,1,0:T(1,128)S(1)} all-to-all(s32[64,1,16]{2,1,0:T(1,128)S(1)} %bitcast.29), channel_id=1, replica_groups=mesh['clu'=64,'row'=4] {'clu'}, dimensions={0} | all-to-all | bytes 8192 | tf_op jit(solution)/shard_map/all_to_all | solution.py:35
  96.9 0.5 broadcast.58
  97.4 0.7 reduce.8
  98.1 0.1 reshape.62
  98.2 10.3 %all_gather.6 = s32[4096]{0:T(1024)S(1)} all-gather(s32[1024]{0:T(1024)S(1)} %reshape.62), channel_id=1, replica_groups=mesh['clu'=64,'row'=4] {'row'}, dimensions={0}, use_global_device_ids=true | all-gather | bytes 20480 | tf_op jit(solution)/shard_map/all_gather | solution.py:43
  108.6 52.9 %all-gather.2.cloned.1.call-done = bf16[4096,1024]{1,0:T(8,128)(2,1)} async-done(((bf16[1024,1024]{1,0:T(8,128)(2,1)}), bf16[4096,1024]{1,0:T(8,128)(2,1)}) %all-gather.2.cloned.1.call-update) | async-done | bytes 8388624 | tf_op jit(solution)/shard_map/all_gather | solution.py:42
  161.5 0.0 copy-done
  161.5 12.0 %select_reduce_fusion = f32[1024]{0:T(1024)S(1)} fusion(s32[4096]{0:T(1024)S(1)} %all_gather.6, s32[1024]{0:T(1024)S(1)} %reshape.62, pred[4096]{0:T(1024)(128)(4,1)S(1)} %broadcast_compare_fusion, bf16[1024,1024]{1,0:T(8,128)(2,1)S(1)} %bitcast.27, bf16[4096,1024]{1,0:T(8,128)(2,1)} %all-gather.2.cloned.1.call-done), kind=kOutput, calls=%fused_computation.3 | convolution fusion | flops 8606710784 | bytes 10514432 | tf_op jit(solution)/shard_map/dot_general | solution.py:8
  173.5 0.7 max_broadcast_in_dim.15
  174.2 10.7 %all-to-all-start.2 = ((f32[64,1,16]{2,1,0:T(1,128)}), f32[64,1,16]{2,1,0:T(1,128)S(1)}, u32[]{:S(2)}, u32[]{:S(2)}) async-start(f32[64,1,16]{2,1,0:T(1,128)} %bitcast.5), calls=%async_computation.2 | async-start | bytes 65536 | tf_op jit(solution)/shard_map/all_to_all | solution.py:47
  184.9 9.4 %all-to-all-done.2 = f32[64,1,16]{2,1,0:T(1,128)S(1)} async-done(((f32[64,1,16]{2,1,0:T(1,128)}), f32[64,1,16]{2,1,0:T(1,128)S(1)}, u32[]{:S(2)}, u32[]{:S(2)}) %all-to-all-start.2) | async-done | bytes 4128 | tf_op jit(solution)/shard_map/all_to_all | solution.py:47
  194.3 0.5 broadcast.59
  194.8 0.7 reduce.9
  195.5 0.1 reshape.65
  195.6 3.4 %gather_fusion = f32[512]{0:T(512)} fusion(f32[1024]{0:T(1024)S(1)} %reshape.65, s32[1024]{0:T(1024)S(1)} %pad_clamp_fusion), kind=kCustom, calls=%fused_computation | custom fusion | bytes 6144 | tf_op jit(solution)/shard_map/gather | solution.py:50
  (6 shorter events, 0.1 us)
Async XLA Ops:
  6.5 5.3 %copy-start.1 = (bf16[512,1024]{1,0:T(8,128)(2,1)S(1)}, bf16[512,1024]{1,0:T(8,128)(2,1)}, u32[]{:S(2)}) copy-start(bf16[512,1024]{1,0:T(8,128)(2,1)} %param.3) | copy-start | bytes 3145732
  6.5 155.0 %all-gather.2.cloned.1.call-start = ((), (), s32[]{:S(2)}) async-start(), calls=%async_computation.3 | async-start | bytes 10485760 | tf_op jit(solution)/shard_map/all_gather | solution.py:42
  77.9 83.6 %copy-start = (bf16[64,16,1024]{2,1,0:T(8,128)(2,1)S(1)}, bf16[64,16,1024]{2,1,0:T(8,128)(2,1)}, u32[]{:S(2)}) copy-start(bf16[64,16,1024]{2,1,0:T(8,128)(2,1)} %all_to_all.20) | copy-start | bytes 6291460
  174.2 20.1 %all-to-all-start.2 = ((f32[64,1,16]{2,1,0:T(1,128)}), f32[64,1,16]{2,1,0:T(1,128)S(1)}, u32[]{:S(2)}, u32[]{:S(2)}) async-start(f32[64,1,16]{2,1,0:T(1,128)} %bitcast.5), calls=%async_computation.2 | async-start | bytes 65536 | tf_op jit(solution)/shard_map/all_to_all | solution.py:47
Sparse Core Ops, SparseCore 0:
  78.0 83.4 all-gather.1
where the time goes:
time: 206 us
  blocking collectives  89.3 us (43%)
  waiting for transfers between devices  62.3 us (30%)
  between operations  13.5 us (7%)
  matrix products  12 us (6%)
  starting transfers between devices  10.7 us (5%)
  other arithmetic  9.79 us (5%)
  local copies, waits for them, and re-layouts  8.31 us (4%)
    all_to_all x1, blocking collectives, per_device(): lax.all_to_all(outgoing.reshape(owners, capacity, features), 'clu', split...  62.7 us
    all_gather x1, waiting for transfers between devices, per_device(): key_rows = lax.all_gather(queries, 'row', axis=0, tiled=True)  52.9 us
    all_to_all x1, blocking collectives, per_device(): lax.all_to_all(out_ranks.reshape(owners, capacity), 'clu', split_axis=0,...  16.2 us
    dot_general x1, matrix products, compare(): lax.dot_general(queries, key_rows, (((1,), (1,)), ((), ())), preferred_el...  12 us
    all_to_all x1, starting transfers between devices, per_device(): lax.all_to_all(best_sim.reshape(owners, capacity), 'clu', split_axis=0, c...  10.7 us
    all_gather x1, blocking collectives, per_device(): key_ranks = lax.all_gather(query_ranks, 'row', axis=0, tiled=True)  10.3 us
    all_to_all x1, waiting for transfers between devices, per_device(): lax.all_to_all(best_sim.reshape(owners, capacity), 'clu', split_axis=0, c...  9.36 us
  transfers between devices with their start and end apart: 2, of which 2 were waited for; matrix products, arithmetic and copies ran while one was open for 2% of the time, Pallas kernels for 0%

commit v1 on v0

v1 whole, which is shorter than its diff:
```python
import functools

import jax
import jax.numpy as jnp
from jax import lax
from jax.experimental import pallas as pl
from jax.experimental.pallas import tpu as pltpu
from jax.sharding import Mesh, PartitionSpec as P

NZ, NY, NC, NX = 8, 4, 2, 4
CHIPS = NZ * NY * NX
SLOTS = 16
HALF = 8
NO_RANK = 1 << 20
STEPS = ((0, 1), (0, -1), (1, 0), (-1, 0))
TORUS = ("z", "y", "x")
ALL = ("z", "y", "core", "x")
MIB = 2**20


def dot(a, b, dims):
    return lax.dot_general(a, b, (dims, ((), ())), preferred_element_type=jnp.float32)


def pack_kernel(group_ref, emb_ref, clu_ref, rank_ref, rows_ref, ranks_ref, home_ref, slot_ref):
    docs = emb_ref.shape[0]
    wide = emb_ref[...].astype(jnp.float32)
    squares = jnp.sum(wide * wide, axis=1, keepdims=True) + 1e-06
    unit = (wide * lax.rsqrt(squares)).astype(jnp.bfloat16)
    clu = clu_ref[...]
    z, y, xh = clu // 8, (clu // 2) % 4, clu % 2
    x = 2 * xh + (y + z) % 2
    home = (z * NY + y) * NX + x
    on_home = lax.broadcasted_iota(jnp.int32, (CHIPS, docs), 0) == home
    member = on_home.astype(jnp.bfloat16)
    ahead = lax.broadcasted_iota(jnp.int32, (docs, docs), 0) < lax.broadcasted_iota(
        jnp.int32, (docs, docs), 1
    )
    before = dot(member, ahead.astype(jnp.bfloat16), ((1,), (0,)))
    slot = jnp.sum(jnp.where(on_home, before, 0.0), axis=0, keepdims=True).astype(jnp.int32)
    home_ref[...] = home
    slot_ref[...] = slot
    rank = rank_ref[...]
    in_slot = lax.broadcasted_iota(jnp.int32, (SLOTS, docs), 0) == slot
    digits = (rank & 255, (rank >> 8) & 255, rank >> 16, jnp.ones_like(rank))
    cols = jnp.concatenate(
        [jnp.where(in_slot, d.astype(jnp.float32), 0.0) for d in digits], axis=0
    ).astype(jnp.bfloat16)
    placed = dot(member, cols, ((1,), (1,))).astype(jnp.int32)
    low, mid, high, there = (placed[:, i * SLOTS : (i + 1) * SLOTS] for i in range(4))
    ranks_ref[...] = jnp.where(there > 0, low + 256 * mid + 65536 * high, NO_RANK)
    group = group_ref[0]
    dy = jnp.where(group == 2, -1, jnp.where(group == 3, 1, 0))
    dx = jnp.where(group == 0, -1, jnp.where(group == 1, 1, 0))
    via = (z * NY + ((y + dy) & 3)) * NX + ((x + dx) & 3)
    at = jnp.where(slot < HALF, home * HALF + slot, via * HALF + slot - HALF)
    total = CHIPS * HALF
    pick = lax.broadcasted_iota(jnp.int32, (total, docs), 0) == at
    rows_ref[...] = dot(
        jnp.where(pick, 1.0, 0.0).astype(jnp.bfloat16), unit, ((1,), (0,))
    ).astype(jnp.bfloat16)


def pack(group, embeddings, cluster, doc_rank):
    docs, features = embeddings.shape
    vmem = pl.BlockSpec(memory_space=pltpu.VMEM)
    return pl.pallas_call(
        pack_kernel,
        out_shape=(
            jax.ShapeDtypeStruct((CHIPS * HALF, features), jnp.bfloat16),
            jax.ShapeDtypeStruct((CHIPS, SLOTS), jnp.int32),
            jax.ShapeDtypeStruct((1, docs), jnp.int32),
            jax.ShapeDtypeStruct((1, docs), jnp.int32),
        ),
        in_specs=[pl.BlockSpec(memory_space=pltpu.SMEM), vmem, vmem, vmem],
        out_specs=(vmem,) * 4,
        compiler_params=pltpu.CompilerParams(vmem_limit_bytes=40 * MIB),
        name="pack",
    )(group, embeddings, cluster, doc_rank)


def compare_kernel(plan, nq, nk, *refs):
    queries, q_ranks = refs[:nq], refs[nq : 2 * nq]
    keys, k_ranks = refs[2 * nq : 2 * nq + nk], refs[2 * nq + nk : 2 * nq + 2 * nk]
    outs = refs[2 * nq + 2 * nk : 3 * nq + 2 * nk]
    best, q_cols = refs[-2:]
    tile = 512
    for q, against in enumerate(plan):
        rows = queries[q].shape[0]
        best[...] = jnp.full(best.shape, -1.0, jnp.float32)
        q_cols[...] = jnp.transpose(jnp.broadcast_to(q_ranks[q][...], (128, rows)))
        for k in against:

            @pl.loop(0, rows // tile)
            def _(t, q=q, k=k):
                here = pl.ds(t * tile, tile)
                scores = dot(queries[q][here, :], keys[k][...], ((1,), (1,)))
                top = best[here, :]
                for c in range(keys[k].shape[0] // 128):
                    cols = slice(c * 128, (c + 1) * 128)
                    earlier = k_ranks[k][:, cols] < q_cols[here, :]
                    top = jnp.maximum(top, jnp.where(earlier, scores[:, cols], -1.0))
                best[here, :] = top

        outs[q][...] = jnp.max(jnp.transpose(best[...]), axis=0, keepdims=True)


def compare(queries, q_ranks, keys, k_ranks, plan, name):
    rows, features = queries[0].shape
    vmem = pl.BlockSpec(memory_space=pltpu.VMEM)
    args = [*queries, *q_ranks, *keys, *k_ranks]
    pairs = sum(rows * keys[k].shape[0] for against in plan for k in against)
    return pl.pallas_call(
        functools.partial(compare_kernel, plan, len(queries), len(keys)),
        out_shape=tuple(jax.ShapeDtypeStruct((1, rows), jnp.float32) for _ in queries),
        in_specs=[vmem] * len(args),
        out_specs=(vmem,) * len(queries),
        scratch_shapes=[pltpu.VMEM((rows, 128), jnp.float32), pltpu.VMEM((rows, 128), jnp.int32)],
        compiler_params=pltpu.CompilerParams(vmem_limit_bytes=48 * MIB),
        cost_estimate=pl.CostEstimate(
            flops=2 * pairs * features, bytes_accessed=8 * MIB, transcendentals=0
        ),
        name=name,
    )(*args)


def unpack_kernel(back_ref, home_ref, slot_ref, out_ref):
    docs = home_ref.shape[1]
    on_home = lax.broadcasted_iota(jnp.int32, (CHIPS, docs), 0) == home_ref[...]
    found = lax.dot_general(
        back_ref[...],
        on_home.astype(jnp.float32),
        (((0,), (0,)), ((), ())),
        precision=lax.Precision.HIGHEST,
        preferred_element_type=jnp.float32,
    )
    in_slot = lax.broadcasted_iota(jnp.int32, (SLOTS, docs), 0) == slot_ref[...]
    out_ref[...] = jnp.sum(jnp.where(in_slot, found, 0.0), axis=0, keepdims=True)


def unpack(back, home, slot):
    vmem = pl.BlockSpec(memory_space=pltpu.VMEM)
    return pl.pallas_call(
        unpack_kernel,
        out_shape=jax.ShapeDtypeStruct(home.shape, jnp.float32),
        in_specs=[vmem] * 3,
        out_specs=vmem,
        name="unpack",
    )(back, home, slot)


def to_home(step):
    dy, dx = step
    place = lambda z, y, c, x: ((z * NY + y) * NC + c) * NX + x
    return [
        (place(z, y, c, x), place(z, (y + dy) % NY, c, (x + dx) % NX))
        for z in range(NZ)
        for y in range(NY)
        for c in range(NC)
        for x in range(NX)
        if (x + y + z) % 2
    ]


def other_core(a):
    return lax.ppermute(a, "core", [(0, 1), (1, 0)])


def exchange(a):
    return lax.all_to_all(a, TORUS, split_axis=0, concat_axis=0, tiled=True)


def per_device(embeddings, cluster, doc_rank):
    docs, features = embeddings.shape
    group = (lax.axis_index("z") // 2).reshape(1)
    rows, ranks, home, slot = pack(
        group, embeddings, cluster.reshape(1, docs), doc_rank.reshape(1, docs)
    )
    rows = exchange(rows.reshape(CHIPS, HALF, features)).reshape(CHIPS * HALF, features)
    ranks = exchange(ranks)
    both = (ranks, other_core(ranks))
    rank_first = [r[:, :HALF].reshape(1, -1) for r in both]
    rank_last = [r[:, HALF:].reshape(1, -1) for r in both]
    part = rows.shape[0] // 4
    passed = [
        lax.ppermute(rows[i * part : (i + 1) * part], ALL, to_home(step))
        for i, step in enumerate(STEPS)
    ]
    first = [rows, other_core(rows)]
    [near] = compare([rows], [rank_first[0]], first, rank_first, ((0, 1),), "compare_first")
    last = jnp.concatenate(passed, axis=0)
    lasts = [last, other_core(last)]
    near_more, far = compare(
        [rows, last],
        [rank_first[0], rank_last[0]],
        [*lasts, *first],
        [*rank_last, *rank_first],
        ((0, 1), (0, 1, 2, 3)),
        "compare_last",
    )
    near = jnp.maximum(near, near_more)
    result = jnp.concatenate([near.reshape(CHIPS, HALF), far.reshape(CHIPS, HALF)], axis=1)
    return unpack(exchange(result), home, slot).reshape(docs)


def solution(mesh):
    torus = Mesh(mesh.devices.reshape(NZ, NY, NC, NX), ALL)
    placed = (P(ALL, None), P(ALL), P(ALL))
    return jax.shard_map(
        per_device, mesh=torus, in_specs=placed, out_specs=P(ALL), check_vma=False
    )
```

time: 206 us -> 163 us (0.79)
  waiting for transfers between devices: 62.3 us -> 5.26 us
  Pallas kernels: 0 us -> 30.2 us
  blocking collectives: 89.3 us -> 103 us
  between operations: 13.5 us -> 0.14 us
  matrix products: 12 us -> 0 us
  other arithmetic: 9.79 us -> 0.76 us
  starting transfers between devices: 10.7 us -> 15.4 us
    all_gather x1 -> x0, waiting for transfers between devices: 52.9 us -> none  [per_device(): key_rows = lax.all_gather(queries, 'row', axis=0, tiled=True)]
    pallas_call x0 -> x4, Pallas kernels: none -> 30.2 us  [the longest x2 26.8 us: compare(): pl.pallas_call(functools.partial(compare_kernel, plan, len(queries), len(...]
    all_to_all x2 -> x3, blocking collectives: 78.9 us -> 103 us  [exchange(): return lax.all_to_all(a, TORUS, split_axis=0, concat_axis=0, tiled=True)]
    ppermute x0 -> x7, starting transfers between devices: none -> 15.4 us  [the longest x3 10.2 us: other_core(): return lax.ppermute(a, 'core', [(0, 1), (1, 0)])]
    dot_general x1 -> x0, matrix products: 12 us -> none  [compare(): lax.dot_general(queries, key_rows, (((1,), (1,)), ((), ())), preferred_el...]
    all_to_all x1 -> x0, starting transfers between devices: 10.7 us -> none  [per_device(): lax.all_to_all(best_sim.reshape(owners, capacity), 'clu', split_axis=0, c...]
    all_gather x1 -> x0, blocking collectives: 10.3 us -> none  [per_device(): key_ranks = lax.all_gather(query_ranks, 'row', axis=0, tiled=True)]
    all_to_all x1 -> x0, waiting for transfers between devices: 9.36 us -> none  [per_device(): lax.all_to_all(best_sim.reshape(owners, capacity), 'clu', split_axis=0, c...]
  transfers between devices with their start and end apart: 2 -> 7, of which waited for: 2 -> 3; matrix products, arithmetic and copies ran while one was open for 2% -> 2% of each run, Pallas kernels for 0% -> 4%
where the time goes in v1:
time: 163 us; the launch traced here: 162 us
  blocking collectives  103 us (63%)
  Pallas kernels  30.2 us (19%)
  starting transfers between devices  15.4 us (9%)
  local copies, waits for them, and re-layouts  7.34 us (5%)
  waiting for transfers between devices  5.26 us (3%)
    all_to_all x3, blocking collectives, exchange(): return lax.all_to_all(a, TORUS, split_axis=0, concat_axis=0, tiled=True)  103 us
    pallas_call x2, Pallas kernels, compare(): pl.pallas_call(functools.partial(compare_kernel, plan, len(queries), len(...  26.8 us
    ppermute x3, starting transfers between devices, other_core(): return lax.ppermute(a, 'core', [(0, 1), (1, 0)])  10.2 us
    ppermute x4, starting transfers between devices, per_device(): lax.ppermute(rows[i * part:(i + 1) * part], ALL, to_home(step))  5.17 us
    unnamed x13, local copies, waits for them, and re-layouts  5.12 us
    ppermute x4, waiting for transfers between devices, per_device(): lax.ppermute(rows[i * part:(i + 1) * part], ALL, to_home(step))  4.64 us
  transfers between devices with their start and end apart: 7, of which 3 were waited for; matrix products, arithmetic and copies ran while one was open for 2% of the time, Pallas kernels for 4%

profile of v1, /device:TPU:1, one launch (start us, length us, event | category | flops | bytes accessed | tf_op | source)
XLA Modules:
  0.0 162.5 jit_solution(9358726828173564963)
XLA Ops:
  0.0 1.2 copy-done
  1.2 0.7 copy-done.1
  1.9 0.7 copy-done.2
  2.6 1.6 %pack.1 = (bf16[1024,1024]{1,0:T(8,128)(2,1)S(1)}, s32[128,16]{1,0:T(8,128)S(1)}, s32[1,512]{1,0:T(1,128)S(1)}, s32[1,512]{1,0:T(1,128)S(1)}) custom-call(s32[1]{0:T(128)} %bitcast.group_ref, bf16[512,1024]{1,0:T(8,128)(2,1)S(1)} %copy-done, s32[1,512]{1,0:T(1,128)S(1)} %bitcast.29, s32[1,512]{1,0:T(1,128)S(1)} %bitcast.30), custom_call_target="tpu_custom_call" | custom-call | tf_op jit(solution)/shard_map/pack/pallas_call | solution.py:67
  4.3 65.9 %all_to_all.28 = bf16[128,8,1024]{2,1,0:T(8,128)(2,1)S(1)} all-to-all(bf16[128,8,1024]{2,1,0:T(8,128)(2,1)S(1)} %bitcast.27), channel_id=1, replica_groups=mesh['z'=8,'y'=4,'core'=2,'x'=4] {'z','y','x'}, dimensions={0} | all-to-all | bytes 4194304 | tf_op jit(solution)/shard_map/all_to_all | solution.py:170
  70.1 0.2 slice_bitcast_fusion
  70.3 1.3 collective-permute-start.2
  71.6 1.3 collective-permute-start.3
  72.9 1.3 collective-permute-start.4
  74.2 1.3 collective-permute-start.5
  75.5 4.1 %collective-permute-start = (bf16[1024,1024]{1,0:T(8,128)(2,1)S(1)}, bf16[1024,1024]{1,0:T(8,128)(2,1)}, u32[]{:S(2)}, u32[]{:S(2)}) collective-permute-start(bf16[1024,1024]{1,0:T(8,128)(2,1)S(1)} %bitcast.22), channel_id=1, source_target_pairs={{0,4},{4,0},{1,5},{5,1},{2,6},{6,2},{3,7},{7,3},{8,12},{12,8},{9,1... | collective-permute-start | bytes 6291464 | tf_op jit(solution)/shard_map/ppermute | solution.py:166
  79.6 3.2 %collective-permute-done.2 = bf16[256,1024]{1,0:T(8,128)(2,1)S(1)} collective-permute-done((bf16[256,1024]{1,0:T(8,128)(2,1)S(1)}, bf16[256,1024]{1,0:T(8,128)(2,1)S(1)}, u32[]{:S(2)}, u32[]{:S(2)}) %collective-permute-start.2) | collective-permute-done | bytes 524320 | tf_op jit(solution)/shard_map/ppermute | solution.py:186
  82.8 0.8 constant_dynamic-update-slice_fusion.3
  83.6 0.8 constant_dynamic-update-slice_fusion.2
  84.5 1.4 collective-permute-done.4
  85.9 0.9 constant_dynamic-update-slice_fusion.1
  86.8 0.8 constant_dynamic-update-slice_fusion.refs_1_.refs_4_
  87.6 4.7 %collective-permute-start.6 = (bf16[1024,1024]{1,0:T(8,128)(2,1)}, bf16[1024,1024]{1,0:T(8,128)(2,1)}, u32[]{:S(2)}, u32[]{:S(2)}) collective-permute-start(bf16[1024,1024]{1,0:T(8,128)(2,1)} %constant_dynamic-update-slice_fusion.refs_1_.refs_4_), channel_id=1, source_target_pairs={{0,4},{4,0},{1,5},{5,1},{2,6},{6,2},{3,7},{7,3},{8,12},{12,8},{9,1... | collective-permute-start | bytes 6291464 | tf_op jit(solution)/shard_map/ppermute | solution.py:166
  92.3 20.4 %all_to_all.29 = s32[128,1,16]{2,1,0:T(1,128)S(1)} all-to-all(s32[128,1,16]{2,1,0:T(1,128)S(1)} %bitcast.28), channel_id=1, replica_groups=mesh['z'=8,'y'=4,'core'=2,'x'=4] {'z','y','x'}, dimensions={0} | all-to-all | bytes 16384 | tf_op jit(solution)/shard_map/all_to_all | solution.py:170
  112.7 1.4 collective-permute-start.1
  114.2 0.1 reshape.51.refs_3_.refs_8_
  114.3 0.1 reshape.49.refs_1_.refs_4_.refs_2_.refs_10_
  114.4 0.6 collective-permute-done.1
  115.1 0.1 reshape.50.refs_5_.refs_11_
  115.2 0.1 reshape.52.refs_9_
  115.3 7.2 %compare_first.1 = f32[1,1024]{1,0:T(1,128)S(1)} custom-call(bf16[1024,1024]{1,0:T(8,128)(2,1)S(1)} %bitcast.23, s32[1,1024]{1,0:T(1,128)S(1)} %reshape.49.refs_1_.refs_4_.refs_2_.refs_10_, bf16[1024,1024]{1,0:T(8,128)(2,1)S(1)} %bitcast.24, bf16[1024,1024]{1,0:T(8,128)(2,1)} %collective-permute-done.refs_3_.refs_7_, ...), custom_call_target="tpu_custom_call" | custom-call | flops 4294967296 | bytes 8388608 | tf_op jit(solution)/shard_map/compare_first/pallas_call | solution.py:113
  122.5 19.7 %compare_last.1 = (f32[1,1024]{1,0:T(1,128)S(1)}, f32[1,1024]{1,0:T(1,128)S(1)}) custom-call(bf16[1024,1024]{1,0:T(8,128)(2,1)S(1)} %bitcast.25, bf16[1024,1024]{1,0:T(8,128)(2,1)} %constant_dynamic-update-slice_fusion.refs_1_.refs_4_, s32[1,1024]{1,0:T(1,128)S(1)} %reshape.49.refs_1_.refs_4_.refs_2_.refs_10_, s32[1,1024]{1,0:T(1,128)S(1)} %reshape.51.refs_3_.refs_8_, ...), custom_call_target="tpu_custom_call" | custom-call | flops 12884901888 | bytes 8388608 | tf_op jit(solution)/shard_map/compare_last/pallas_call | solution.py:113
  142.1 0.5 broadcast.7
  142.7 0.7 reduce.7
  143.5 0.1 pad_maximum_fusion
  143.6 17.2 %all_to_all.30 = f32[128,1,16]{2,1,0:T(1,128)} all-to-all(f32[128,1,16]{2,1,0:T(1,128)S(1)} %bitcast.33), channel_id=1, replica_groups=mesh['z'=8,'y'=4,'core'=2,'x'=4] {'z','y','x'}, dimensions={0} | all-to-all | bytes 16384 | tf_op jit(solution)/shard_map/all_to_all | solution.py:170
  160.8 1.7 %unpack.1 = f32[1,512]{1,0:T(1,128)} custom-call(f32[128,16]{1,0:T(8,128)} %bitcast.34, s32[1,512]{1,0:T(1,128)} %copy-done.3, s32[1,512]{1,0:T(1,128)} %copy-done.4), custom_call_target="tpu_custom_call" | custom-call | tf_op jit(solution)/shard_map/unpack/pallas_call | solution.py:143
  (16 shorter events, 0.4 us)
Async XLA Ops:
  0.0 1.2 copy-start
  1.2 0.7 copy-start.1
  1.9 0.7 copy-start.2
  4.2 65.9 %copy-start.3 = (s32[1,512]{1,0:T(1,128)}, s32[1,512]{1,0:T(1,128)S(1)}, u32[]{:S(2)}) copy-start(s32[1,512]{1,0:T(1,128)S(1)} %get-tuple-element.15.home_ref) | copy-start | bytes 6148
  4.2 65.9 %copy-start.4 = (s32[1,512]{1,0:T(1,128)}, s32[1,512]{1,0:T(1,128)S(1)}, u32[]{:S(2)}) copy-start(s32[1,512]{1,0:T(1,128)S(1)} %get-tuple-element.16.slot_ref) | copy-start | bytes 6148
  70.3 12.5 %collective-permute-start.2 = (bf16[256,1024]{1,0:T(8,128)(2,1)S(1)}, bf16[256,1024]{1,0:T(8,128)(2,1)S(1)}, u32[]{:S(2)}, u32[]{:S(2)}) collective-permute-start(bf16[256,1024]{1,0:T(8,128)(2,1)S(1)} %get-tuple-element.20), channel_id=1, source_target_pairs={{1,2},{3,0},{5,6},{7,4},{8,9},{10,11},{12,13},{14,15},{17,18},{19,... | collective-permute-start | bytes 1572872 | tf_op jit(solution)/shard_map/ppermute | solution.py:186
  71.6 12.0 %collective-permute-start.3 = (bf16[256,1024]{1,0:T(8,128)(2,1)S(1)}, bf16[256,1024]{1,0:T(8,128)(2,1)S(1)}, u32[]{:S(2)}, u32[]{:S(2)}) collective-permute-start(bf16[256,1024]{1,0:T(8,128)(2,1)S(1)} %get-tuple-element.19), channel_id=1, source_target_pairs={{1,0},{3,2},{5,4},{7,6},{8,11},{10,9},{12,15},{14,13},{17,16},{19,... | collective-permute-start | bytes 1572872 | tf_op jit(solution)/shard_map/ppermute | solution.py:186
  72.9 13.0 %collective-permute-start.4 = (bf16[256,1024]{1,0:T(8,128)(2,1)S(1)}, bf16[256,1024]{1,0:T(8,128)(2,1)S(1)}, u32[]{:S(2)}, u32[]{:S(2)}) collective-permute-start(bf16[256,1024]{1,0:T(8,128)(2,1)S(1)} %get-tuple-element.18), channel_id=1, source_target_pairs={{1,9},{3,11},{5,13},{7,15},{8,16},{10,18},{12,20},{14,22},{17,25},... | collective-permute-start | bytes 1572872 | tf_op jit(solution)/shard_map/ppermute | solution.py:186
  74.2 12.6 %collective-permute-start.5 = (bf16[256,1024]{1,0:T(8,128)(2,1)S(1)}, bf16[256,1024]{1,0:T(8,128)(2,1)S(1)}, u32[]{:S(2)}, u32[]{:S(2)}) collective-permute-start(bf16[256,1024]{1,0:T(8,128)(2,1)S(1)} %get-tuple-element.17), channel_id=1, source_target_pairs={{1,25},{3,27},{5,29},{7,31},{8,0},{10,2},{12,4},{14,6},{17,9},{19,... | collective-permute-start | bytes 1572872 | tf_op jit(solution)/shard_map/ppermute | solution.py:186
  75.5 39.8 %collective-permute-start = (bf16[1024,1024]{1,0:T(8,128)(2,1)S(1)}, bf16[1024,1024]{1,0:T(8,128)(2,1)}, u32[]{:S(2)}, u32[]{:S(2)}) collective-permute-start(bf16[1024,1024]{1,0:T(8,128)(2,1)S(1)} %bitcast.22), channel_id=1, source_target_pairs={{0,4},{4,0},{1,5},{5,1},{2,6},{6,2},{3,7},{7,3},{8,12},{12,8},{9,1... | collective-permute-start | bytes 6291464 | tf_op jit(solution)/shard_map/ppermute | solution.py:166
  87.6 34.9 %collective-permute-start.6 = (bf16[1024,1024]{1,0:T(8,128)(2,1)}, bf16[1024,1024]{1,0:T(8,128)(2,1)}, u32[]{:S(2)}, u32[]{:S(2)}) collective-permute-start(bf16[1024,1024]{1,0:T(8,128)(2,1)} %constant_dynamic-update-slice_fusion.refs_1_.refs_4_), channel_id=1, source_target_pairs={{0,4},{4,0},{1,5},{5,1},{2,6},{6,2},{3,7},{7,3},{8,12},{12,8},{9,1... | collective-permute-start | bytes 6291464 | tf_op jit(solution)/shard_map/ppermute | solution.py:166
  112.7 2.3 %collective-permute-start.1 = (s32[128,16]{1,0:T(8,128)S(1)}, s32[128,16]{1,0:T(8,128)S(1)}, u32[]{:S(2)}, u32[]{:S(2)}) collective-permute-start(s32[128,16]{1,0:T(8,128)S(1)} %bitcast.31), channel_id=1, source_target_pairs={{0,4},{4,0},{1,5},{5,1},{2,6},{6,2},{3,7},{7,3},{8,12},{12,8},{9,1... | collective-permute-start | bytes 24584 | tf_op jit(solution)/shard_map/ppermute | solution.py:166

commit v2 on v1

v2 whole, which is shorter than its diff:
```python
import functools

import jax
import jax.numpy as jnp
from jax import lax
from jax.experimental import pallas as pl
from jax.experimental.pallas import tpu as pltpu
from jax.sharding import Mesh, PartitionSpec as P

NZ, NY, NC, NX = 8, 4, 2, 4
CHIPS = NZ * NY * NX
SLOTS = 16
HALF = 8
NO_RANK = 1 << 20
STEPS = ((0, 1), (0, -1), (1, 0), (-1, 0))
TORUS = ("z", "y", "x")
ALL = ("z", "y", "core", "x")
MIB = 2**20
TILE = 512


def dot(a, b, dims):
    return lax.dot_general(a, b, (dims, ((), ())), preferred_element_type=jnp.float32)


def digit_weights():
    which = lax.broadcasted_iota(jnp.int32, (128, 128), 0)
    weight = jnp.where(
        which == 0, 1, jnp.where(which == 1, 256, jnp.where(which == 2, 65536, -NO_RANK))
    )
    return jnp.where(which < 4, weight, 0).astype(jnp.float32).astype(jnp.bfloat16)


def pack_kernel(group_ref, emb_ref, clu_ref, rank_ref, rows_ref, home_ref, slot_ref):
    docs, features = emb_ref.shape
    wide = emb_ref[...].astype(jnp.float32)
    squares = jnp.sum(wide * wide, axis=1, keepdims=True) + 1e-06
    unit = (wide * lax.rsqrt(squares)).astype(jnp.bfloat16)
    clu = clu_ref[...]
    z, y, xh = clu // 8, (clu // 2) % 4, clu % 2
    x = 2 * xh + (y + z) % 2
    home = (z * NY + y) * NX + x
    on_home = lax.broadcasted_iota(jnp.int32, (CHIPS, docs), 0) == home
    member = on_home.astype(jnp.bfloat16)
    ahead = lax.broadcasted_iota(jnp.int32, (docs, docs), 0) < lax.broadcasted_iota(
        jnp.int32, (docs, docs), 1
    )
    before = dot(member, ahead.astype(jnp.bfloat16), ((1,), (0,)))
    slot = jnp.sum(jnp.where(on_home, before, 0.0), axis=0, keepdims=True).astype(jnp.int32)
    home_ref[...] = home
    slot_ref[...] = slot
    rank = rank_ref[...]
    which = lax.broadcasted_iota(jnp.int32, (128, docs), 0)
    digits = jnp.where(
        which == 0,
        rank & 255,
        jnp.where(which == 1, (rank >> 8) & 255, jnp.where(which == 2, rank >> 16, 1)),
    )
    digits = jnp.where(which < 4, digits, 0).astype(jnp.float32).astype(jnp.bfloat16)
    group = group_ref[0]
    dy = jnp.where(group == 2, -1, jnp.where(group == 3, 1, 0))
    dx = jnp.where(group == 0, -1, jnp.where(group == 1, 1, 0))
    via = (z * NY + ((y + dy) & 3)) * NX + ((x + dx) & 3)
    at = jnp.where(slot < HALF, home * HALF + slot, via * HALF + slot - HALF)
    pick = lax.broadcasted_iota(jnp.int32, (CHIPS * HALF, docs), 0) == at
    pick = jnp.where(pick, 1.0, 0.0).astype(jnp.bfloat16)
    rows_ref[:, :features] = dot(pick, unit, ((1,), (0,))).astype(jnp.bfloat16)
    rows_ref[:, features:] = dot(pick, digits, ((1,), (1,))).astype(jnp.bfloat16)


def pack(group, embeddings, cluster, doc_rank):
    docs, features = embeddings.shape
    vmem = pl.BlockSpec(memory_space=pltpu.VMEM)
    return pl.pallas_call(
        pack_kernel,
        out_shape=(
            jax.ShapeDtypeStruct((CHIPS * HALF, features + 128), jnp.bfloat16),
            jax.ShapeDtypeStruct((1, docs), jnp.int32),
            jax.ShapeDtypeStruct((1, docs), jnp.int32),
        ),
        in_specs=[pl.BlockSpec(memory_space=pltpu.SMEM), vmem, vmem, vmem],
        out_specs=(vmem,) * 3,
        compiler_params=pltpu.CompilerParams(vmem_limit_bytes=40 * MIB),
        name="pack",
    )(group, embeddings, cluster, doc_rank)


def compare_kernel(plan, sets, *refs):
    core_ref, refs = refs[0], list(refs[1:])
    pieces, start, outs, by_row, by_col, row_rank, col_rank, joined = ([] for _ in range(8))
    for n, _, _ in sets:
        pieces.append([refs.pop(0) for _ in range(n)])
    for _, has, _ in sets:
        start.append(refs.pop(0) if has else None)
    for _, _, wanted in sets:
        outs.append(refs.pop(0) if wanted else None)
    for _ in sets:
        by_row.append(refs.pop(0))
        by_col.append(refs.pop(0))
        row_rank.append(refs.pop(0))
        col_rank.append(refs.pop(0))
    weights = digit_weights()
    features = pieces[0][0].shape[1] - 128
    for i, (n, _, _) in enumerate(sets):
        if n > 1:
            whole = refs.pop(0)
            part = pieces[i][0].shape[0]
            for p, piece in enumerate(pieces[i]):
                whole[p * part : (p + 1) * part, :] = piece[...]
        else:
            whole = pieces[i][0]
        joined.append(whole)
        tail = whole[:, features:]
        row_rank[i][...] = dot(tail, weights, ((1,), (0,))) + float(NO_RANK)
        col_rank[i][...] = dot(weights[:, :8], tail, ((0,), (1,))) + float(NO_RANK)
        by_row[i][...] = jnp.full(by_row[i].shape, -1.0, jnp.float32)
        by_col[i][...] = jnp.full(by_col[i].shape, -1.0, jnp.float32)
    core = core_ref[0]
    for (q, qb), (k, kb), both in plan:
        q_at = pl.ds(pl.multiple_of((core if qb is None else qb) * TILE, TILE), TILE)
        k_at = pl.ds(pl.multiple_of((core if kb is None else kb) * TILE, TILE), TILE)
        scores = dot(joined[q][q_at, :features], joined[k][k_at, :features], ((1,), (1,)))
        q_rank = row_rank[q][q_at, :]
        top = by_row[q][q_at, :]
        k_rank = col_rank[k][0:1, k_at]
        side = []
        for c in range(TILE // 128):
            cols = slice(c * 128, (c + 1) * 128)
            part = scores[:, cols]
            earlier = k_rank[:, cols] < q_rank
            top = jnp.maximum(top, jnp.where(earlier, part, -1.0))
            if both:
                other = jnp.where(earlier, -1.0, part)
                side.append(jnp.max(other.reshape(TILE // 8, 8, 128), axis=0))
        by_row[q][q_at, :] = top
        if both:
            by_col[k][:, k_at] = jnp.maximum(by_col[k][:, k_at], jnp.concatenate(side, axis=1))
    for i, out in enumerate(outs):
        if out is not None:
            best = jnp.max(jnp.transpose(by_row[i][...]), axis=0, keepdims=True)
            best = jnp.maximum(best, jnp.max(by_col[i][...], axis=0, keepdims=True))
            if start[i] is not None:
                best = jnp.maximum(best, start[i][...])
            out[...] = best


def compare(core, sets, plan, name):
    wide = sets[0][0][0].shape[1]
    rows = [sum(a.shape[0] for a in arrays) for arrays, _, _ in sets]
    vmem = pl.BlockSpec(memory_space=pltpu.VMEM)
    args = [a for arrays, _, _ in sets for a in arrays]
    args += [best for _, best, _ in sets if best is not None]
    wanted = [n for n, (_, _, want) in zip(rows, sets) if want]
    scratch = []
    for n in rows:
        scratch += [
            pltpu.VMEM((n, 128), jnp.float32),
            pltpu.VMEM((8, n), jnp.float32),
            pltpu.VMEM((n, 128), jnp.float32),
            pltpu.VMEM((8, n), jnp.float32),
        ]
    scratch += [
        pltpu.VMEM((n, wide), jnp.bfloat16)
        for n, (arrays, _, _) in zip(rows, sets)
        if len(arrays) > 1
    ]
    return pl.pallas_call(
        functools.partial(
            compare_kernel,
            plan,
            [(len(arrays), best is not None, want) for arrays, best, want in sets],
        ),
        out_shape=tuple(jax.ShapeDtypeStruct((1, n), jnp.float32) for n in wanted),
        in_specs=[pl.BlockSpec(memory_space=pltpu.SMEM)] + [vmem] * len(args),
        out_specs=(vmem,) * len(wanted),
        scratch_shapes=scratch,
        compiler_params=pltpu.CompilerParams(vmem_limit_bytes=48 * MIB),
        cost_estimate=pl.CostEstimate(
            flops=2 * len(plan) * TILE * TILE * wide,
            bytes_accessed=2 * wide * sum(rows),
            transcendentals=0,
        ),
        name=name,
    )(core, *args)


def unpack_kernel(back_ref, home_ref, slot_ref, out_ref):
    docs = home_ref.shape[1]
    on_home = lax.broadcasted_iota(jnp.int32, (CHIPS, docs), 0) == home_ref[...]
    found = lax.dot_general(
        back_ref[...],
        on_home.astype(jnp.float32),
        (((0,), (0,)), ((), ())),
        precision=lax.Precision.HIGHEST,
        preferred_element_type=jnp.float32,
    )
    in_slot = lax.broadcasted_iota(jnp.int32, (SLOTS, docs), 0) == slot_ref[...]
    out_ref[...] = jnp.sum(jnp.where(in_slot, found, 0.0), axis=0, keepdims=True)


def unpack(back, home, slot):
    vmem = pl.BlockSpec(memory_space=pltpu.VMEM)
    return pl.pallas_call(
        unpack_kernel,
        out_shape=jax.ShapeDtypeStruct(home.shape, jnp.float32),
        in_specs=[vmem] * 3,
        out_specs=vmem,
        name="unpack",
    )(back, home, slot)


def to_home(step):
    dy, dx = step
    place = lambda z, y, c, x: ((z * NY + y) * NC + c) * NX + x
    return [
        (place(z, y, c, x), place(z, (y + dy) % NY, c, (x + dx) % NX))
        for z in range(NZ)
        for y in range(NY)
        for c in range(NC)
        for x in range(NX)
        if (x + y + z) % 2
    ]


def other_core(a):
    return lax.ppermute(a, "core", [(0, 1), (1, 0)])


def exchange(a):
    return lax.all_to_all(a, TORUS, split_axis=0, concat_axis=0, tiled=True)


def per_device(embeddings, cluster, doc_rank):
    docs, features = embeddings.shape
    group = (lax.axis_index("z") // 2).reshape(1)
    core = lax.axis_index("core").reshape(1)
    rows, home, slot = pack(group, embeddings, cluster.reshape(1, docs), doc_rank.reshape(1, docs))
    wide = features + 128
    near = exchange(rows.reshape(CHIPS, HALF, wide)).reshape(CHIPS * HALF, wide)
    part = near.shape[0] // 4
    far = [
        lax.ppermute(near[i * part : (i + 1) * part], ALL, to_home(step))
        for i, step in enumerate(STEPS)
    ]
    near_there = other_core(near)
    plan = (
        ((0, 0), (0, 0), False),
        ((0, 1), (0, 1), False),
        ((0, 0), (0, 1), True),
        ((0, 0), (1, 1), True),
        ((0, None), (1, None), True),
    )
    best_near, best_near_there = compare(
        core, [([near], None, True), ([near_there], None, True)], plan, "compare_near"
    )
    far_there = [other_core(a) for a in far]
    plan = (
        ((0, 0), (0, 0), False),
        ((0, 1), (0, 1), False),
        ((0, 0), (0, 1), True),
        *(((0, q), (k, b), True) for q in (0, 1) for k in (1, 2) for b in (0, 1)),
    )
    best_far, best_near, best_near_there = compare(
        core,
        [(far, None, True), ([near], best_near, True), ([near_there], best_near_there, True)],
        plan,
        "compare_far",
    )
    plan = (((0, 0), (1, 1), True), ((0, None), (1, None), True))
    best_far, best_far_there = compare(
        core, [(far, best_far, True), (far_there, None, True)], plan, "compare_cores"
    )
    mine = jnp.concatenate([best_near, best_far], axis=0)
    theirs = other_core(jnp.concatenate([best_near_there, best_far_there], axis=0))
    result = jnp.maximum(mine, theirs).reshape(2, CHIPS, HALF)
    result = jnp.concatenate([result[0], result[1]], axis=1)
    return unpack(exchange(result), home, slot).reshape(docs)


def solution(mesh):
    torus = Mesh(mesh.devices.reshape(NZ, NY, NC, NX), ALL)
    placed = (P(ALL, None), P(ALL), P(ALL))
    return jax.shard_map(
        per_device, mesh=torus, in_specs=placed, out_specs=P(ALL), check_vma=False
    )
```

time: 163 us -> 145 us (0.89)
  blocking collectives: 103 us -> 90.1 us
  waiting for transfers between devices: 5.26 us -> 16.3 us
  Pallas kernels: 30.2 us -> 21.2 us
  starting transfers between devices: 15.4 us -> 12.1 us
  local copies, waits for them, and re-layouts: 7.34 us -> 4.25 us
    all_to_all x3 -> x2, blocking collectives: 103 us -> 90.1 us  [exchange(): return lax.all_to_all(a, TORUS, split_axis=0, concat_axis=0, tiled=True)]
    ppermute x4, waiting for transfers between devices: 4.64 us -> 15.1 us  [per_device(): lax.ppermute(near[i * part:(i + 1) * part], ALL, to_home(step))]
    pallas_call x2 -> x3, Pallas kernels: 26.8 us -> 17.5 us  [compare(): pl.pallas_call(functools.partial(compare_kernel, plan, [(len(arrays), bes...]
    ppermute x3 -> x6, starting transfers between devices: 10.2 us -> 6.9 us  [other_core(): return lax.ppermute(a, 'core', [(0, 1), (1, 0)])]
    unnamed x13 -> x10, local copies, waits for them, and re-layouts: 5.12 us -> 2.59 us
  transfers between devices with their start and end apart: 7 -> 10, of which waited for: 3 -> 4; matrix products, arithmetic and copies ran while one was open for 2% -> 1% of each run, Pallas kernels for 4% -> 10%
where the time goes in v2:
time: 145 us; the launch traced here: 144 us
  blocking collectives  90.1 us (62%)
  Pallas kernels  21.2 us (15%)
  waiting for transfers between devices  16.3 us (11%)
  starting transfers between devices  12.1 us (8%)
  local copies, waits for them, and re-layouts  4.25 us (3%)
    all_to_all x2, blocking collectives, exchange(): return lax.all_to_all(a, TORUS, split_axis=0, concat_axis=0, tiled=True)  90.1 us
    pallas_call x3, Pallas kernels, compare(): pl.pallas_call(functools.partial(compare_kernel, plan, [(len(arrays), bes...  17.5 us
    ppermute x4, waiting for transfers between devices, per_device(): lax.ppermute(near[i * part:(i + 1) * part], ALL, to_home(step))  15.1 us
    ppermute x6, starting transfers between devices, other_core(): return lax.ppermute(a, 'core', [(0, 1), (1, 0)])  6.9 us
    ppermute x4, starting transfers between devices, per_device(): lax.ppermute(near[i * part:(i + 1) * part], ALL, to_home(step))  5.16 us
  transfers between devices with their start and end apart: 10, of which 4 were waited for; matrix products, arithmetic and copies ran while one was open for 1% of the time, Pallas kernels for 10%

profile of v2, /device:TPU:1, one launch (start us, length us, event | category | flops | bytes accessed | tf_op | source)
XLA Modules:
  0.0 144.2 jit_solution(15382133140375425986)
XLA Ops:
  0.0 1.2 copy-done
  1.2 0.7 copy-done.1
  1.9 0.7 copy-done.2
  2.6 1.9 %pack.1 = (bf16[1024,1152]{1,0:T(8,128)(2,1)S(1)}, s32[1,512]{1,0:T(1,128)S(1)}, s32[1,512]{1,0:T(1,128)S(1)}) custom-call(s32[1]{0:T(128)} %bitcast.1.group_ref, bf16[512,1024]{1,0:T(8,128)(2,1)S(1)} %copy-done, s32[1,512]{1,0:T(1,128)S(1)} %bitcast.23, s32[1,512]{1,0:T(1,128)S(1)} %bitcast.24), custom_call_target="tpu_custom_call" | custom-call | tf_op jit(solution)/shard_map/pack/pallas_call | solution.py:74
  4.5 70.9 %all_to_all.16 = bf16[128,8,1152]{2,1,0:T(8,128)(2,1)S(1)} all-to-all(bf16[128,8,1152]{2,1,0:T(8,128)(2,1)S(1)} %bitcast.22), channel_id=1, replica_groups=mesh['z'=8,'y'=4,'core'=2,'x'=4] {'z','y','x'}, dimensions={0} | all-to-all | bytes 4718592 | tf_op jit(solution)/shard_map/all_to_all | solution.py:230
  75.5 4.5 %collective-permute-start.4 = (bf16[1024,1152]{1,0:T(8,128)(2,1)S(1)}, bf16[1024,1152]{1,0:T(8,128)(2,1)}, u32[]{:S(2)}, u32[]{:S(2)}) collective-permute-start(bf16[1024,1152]{1,0:T(8,128)(2,1)S(1)} %bitcast.19), channel_id=1, source_target_pairs={{0,4},{4,0},{1,5},{5,1},{2,6},{6,2},{3,7},{7,3},{8,12},{12,8},{9,1... | collective-permute-start | bytes 7077896 | tf_op jit(solution)/shard_map/ppermute | solution.py:226
  79.9 1.5 %slice_bitcast_fusion = (bf16[256,1152]{1,0:T(8,128)(2,1)}, bf16[256,1152]{1,0:T(8,128)(2,1)}, bf16[256,1152]{1,0:T(8,128)(2,1)}, bf16[256,1152]{1,0:T(8,128)(2,1)}) fusion(bf16[128,8,1152]{2,1,0:T(8,128)(2,1)S(1)} %all_to_all.16), kind=kLoop, calls=%fused_computation | loop fusion | bytes 4718592 | tf_op jit(solution)/shard_map/slice | solution.py:242
  81.4 1.3 collective-permute-start
  82.7 1.3 collective-permute-start.1
  84.0 1.3 collective-permute-start.2
  85.3 1.3 collective-permute-start.3
  86.6 13.2 %collective-permute-done.refs_1_ = bf16[256,1152]{1,0:T(8,128)(2,1)S(1)} collective-permute-done((bf16[256,1152]{1,0:T(8,128)(2,1)}, bf16[256,1152]{1,0:T(8,128)(2,1)S(1)}, u32[]{:S(2)}, u32[]{:S(2)}) %collective-permute-start) | collective-permute-done | bytes 589856 | tf_op jit(solution)/shard_map/ppermute | solution.py:242
  99.8 0.7 collective-permute-start.5
  100.5 0.0 collective-permute-done.1.refs_2_
  100.5 0.1 collective-permute-start.6
  100.5 1.8 %collective-permute-done.2.refs_3_ = bf16[256,1152]{1,0:T(8,128)(2,1)} collective-permute-done((bf16[256,1152]{1,0:T(8,128)(2,1)}, bf16[256,1152]{1,0:T(8,128)(2,1)}, u32[]{:S(2)}, u32[]{:S(2)}) %collective-permute-start.2) | collective-permute-done | bytes 589856 | tf_op jit(solution)/shard_map/ppermute | solution.py:242
  102.4 0.8 collective-permute-start.7
  103.2 0.1 collective-permute-done.3.refs_4_
  103.3 0.8 collective-permute-start.8
  104.1 0.0 collective-permute-done.4.refs_2_.refs_6_
  104.1 5.1 %compare_near.1 = (f32[1,1024]{1,0:T(1,128)S(1)}, f32[1,1024]{1,0:T(1,128)S(1)}) custom-call(s32[1]{0:T(128)} %bitcast.refs_0_, bf16[1024,1152]{1,0:T(8,128)(2,1)S(1)} %bitcast.20, bf16[1024,1152]{1,0:T(8,128)(2,1)} %collective-permute-done.4.refs_2_.refs_6_), custom_call_target="tpu_custom_call" | custom-call | flops 3019898880 | bytes 4718592 | tf_op jit(solution)/shard_map/compare_near/pallas_call | solution.py:167
  109.2 9.3 %compare_far.1 = (f32[1,1024]{1,0:T(1,128)S(1)}, f32[1,1024]{1,0:T(1,128)S(1)}, f32[1,1024]{1,0:T(1,128)S(1)}) custom-call(s32[1]{0:T(128)} %bitcast.refs_0_, bf16[256,1152]{1,0:T(8,128)(2,1)S(1)} %collective-permute-done.refs_1_, bf16[256,1152]{1,0:T(8,128)(2,1)S(1)} %collective-permute-done.1.refs_2_, bf16[256,1152]{1,0:T(8,128)(2,1)} %collective-permute-done.2.refs_3_, ...), custom_call_target="tpu_custom_call" | custom-call | flops 6643777536 | bytes 7077888 | tf_op jit(solution)/shard_map/compare_far/pallas_call | solution.py:167
  118.5 0.0 collective-permute-done.6.refs_6_
  118.5 0.0 collective-permute-done.8.refs_8_
  118.5 3.1 %compare_cores.1 = (f32[1,1024]{1,0:T(1,128)S(1)}, f32[1,1024]{1,0:T(1,128)S(1)}) custom-call(s32[1]{0:T(128)} %bitcast.refs_0_, bf16[256,1152]{1,0:T(8,128)(2,1)S(1)} %collective-permute-done.refs_1_, bf16[256,1152]{1,0:T(8,128)(2,1)S(1)} %collective-permute-done.1.refs_2_, bf16[256,1152]{1,0:T(8,128)(2,1)} %collective-permute-done.2.refs_3_, ...), custom_call_target="tpu_custom_call" | custom-call | flops 1207959552 | bytes 4718592 | tf_op jit(solution)/shard_map/compare_cores/pallas_call | solution.py:167
  121.7 0.1 collective-permute-start.9
  121.8 1.2 collective-permute-done.9
  123.0 0.1 squeeze.6
  123.1 0.1 squeeze.7
  123.2 0.1 pad_maximum_fusion
  123.3 19.2 %all_to_all.17 = f32[128,1,16]{2,1,0:T(1,128)} all-to-all(f32[128,1,16]{2,1,0:T(1,128)S(1)} %bitcast.25), channel_id=1, replica_groups=mesh['z'=8,'y'=4,'core'=2,'x'=4] {'z','y','x'}, dimensions={0} | all-to-all | bytes 16384 | tf_op jit(solution)/shard_map/all_to_all | solution.py:230
  142.5 1.7 %unpack.1 = f32[1,512]{1,0:T(1,128)} custom-call(f32[128,16]{1,0:T(8,128)} %bitcast.26, s32[1,512]{1,0:T(1,128)} %copy-done.3, s32[1,512]{1,0:T(1,128)} %copy-done.4), custom_call_target="tpu_custom_call" | custom-call | tf_op jit(solution)/shard_map/unpack/pallas_call | solution.py:203
  (12 shorter events, 0.1 us)
Async XLA Ops:
  0.0 1.2 copy-start
  1.2 0.7 copy-start.1
  1.9 0.7 copy-start.2
  4.5 71.0 %copy-start.3 = (s32[1,512]{1,0:T(1,128)}, s32[1,512]{1,0:T(1,128)S(1)}, u32[]{:S(2)}) copy-start(s32[1,512]{1,0:T(1,128)S(1)} %get-tuple-element.23.home_ref) | copy-start | bytes 6148
  4.5 71.0 %copy-start.4 = (s32[1,512]{1,0:T(1,128)}, s32[1,512]{1,0:T(1,128)S(1)}, u32[]{:S(2)}) copy-start(s32[1,512]{1,0:T(1,128)S(1)} %get-tuple-element.24.slot_ref) | copy-start | bytes 6148
  75.5 28.6 %collective-permute-start.4 = (bf16[1024,1152]{1,0:T(8,128)(2,1)S(1)}, bf16[1024,1152]{1,0:T(8,128)(2,1)}, u32[]{:S(2)}, u32[]{:S(2)}) collective-permute-start(bf16[1024,1152]{1,0:T(8,128)(2,1)S(1)} %bitcast.19), channel_id=1, source_target_pairs={{0,4},{4,0},{1,5},{5,1},{2,6},{6,2},{3,7},{7,3},{8,12},{12,8},{9,1... | collective-permute-start | bytes 7077896 | tf_op jit(solution)/shard_map/ppermute | solution.py:226
  81.4 18.4 %collective-permute-start = (bf16[256,1152]{1,0:T(8,128)(2,1)}, bf16[256,1152]{1,0:T(8,128)(2,1)S(1)}, u32[]{:S(2)}, u32[]{:S(2)}) collective-permute-start(bf16[256,1152]{1,0:T(8,128)(2,1)} %get-tuple-element.30), channel_id=1, source_target_pairs={{1,2},{3,0},{5,6},{7,4},{8,9},{10,11},{12,13},{14,15},{17,18},{19,... | collective-permute-start | bytes 1769480 | tf_op jit(solution)/shard_map/ppermute | solution.py:242
  82.7 17.8 %collective-permute-start.1 = (bf16[256,1152]{1,0:T(8,128)(2,1)}, bf16[256,1152]{1,0:T(8,128)(2,1)S(1)}, u32[]{:S(2)}, u32[]{:S(2)}) collective-permute-start(bf16[256,1152]{1,0:T(8,128)(2,1)} %get-tuple-element.29), channel_id=1, source_target_pairs={{1,0},{3,2},{5,4},{7,6},{8,11},{10,9},{12,15},{14,13},{17,16},{19,... | collective-permute-start | bytes 1769480 | tf_op jit(solution)/shard_map/ppermute | solution.py:242
  84.0 18.4 %collective-permute-start.2 = (bf16[256,1152]{1,0:T(8,128)(2,1)}, bf16[256,1152]{1,0:T(8,128)(2,1)}, u32[]{:S(2)}, u32[]{:S(2)}) collective-permute-start(bf16[256,1152]{1,0:T(8,128)(2,1)} %get-tuple-element.28), channel_id=1, source_target_pairs={{1,9},{3,11},{5,13},{7,15},{8,16},{10,18},{12,20},{14,22},{17,25},... | collective-permute-start | bytes 1769480 | tf_op jit(solution)/shard_map/ppermute | solution.py:242
  85.3 18.0 %collective-permute-start.3 = (bf16[256,1152]{1,0:T(8,128)(2,1)}, bf16[256,1152]{1,0:T(8,128)(2,1)}, u32[]{:S(2)}, u32[]{:S(2)}) collective-permute-start(bf16[256,1152]{1,0:T(8,128)(2,1)} %get-tuple-element.27), channel_id=1, source_target_pairs={{1,25},{3,27},{5,29},{7,31},{8,0},{10,2},{12,4},{14,6},{17,9},{19,... | collective-permute-start | bytes 1769480 | tf_op jit(solution)/shard_map/ppermute | solution.py:242
  99.8 18.7 %collective-permute-start.5 = (bf16[256,1152]{1,0:T(8,128)(2,1)S(1)}, bf16[256,1152]{1,0:T(8,128)(2,1)S(1)}, u32[]{:S(2)}, u32[]{:S(2)}) collective-permute-start(bf16[256,1152]{1,0:T(8,128)(2,1)S(1)} %collective-permute-done.refs_1_), channel_id=1, source_target_pairs={{0,4},{4,0},{1,5},{5,1},{2,6},{6,2},{3,7},{7,3},{8,12},{12,8},{9,1... | collective-permute-start | bytes 1769480 | tf_op jit(solution)/shard_map/ppermute | solution.py:226
  100.5 18.0 %collective-permute-start.6 = (bf16[256,1152]{1,0:T(8,128)(2,1)S(1)}, bf16[256,1152]{1,0:T(8,128)(2,1)S(1)}, u32[]{:S(2)}, u32[]{:S(2)}) collective-permute-start(bf16[256,1152]{1,0:T(8,128)(2,1)S(1)} %collective-permute-done.1.refs_2_), channel_id=1, source_target_pairs={{0,4},{4,0},{1,5},{5,1},{2,6},{6,2},{3,7},{7,3},{8,12},{12,8},{9,1... | collective-permute-start | bytes 1769480 | tf_op jit(solution)/shard_map/ppermute | solution.py:226
  102.4 16.1 %collective-permute-start.7 = (bf16[256,1152]{1,0:T(8,128)(2,1)}, bf16[256,1152]{1,0:T(8,128)(2,1)S(1)}, u32[]{:S(2)}, u32[]{:S(2)}) collective-permute-start(bf16[256,1152]{1,0:T(8,128)(2,1)} %collective-permute-done.2.refs_3_), channel_id=1, source_target_pairs={{0,4},{4,0},{1,5},{5,1},{2,6},{6,2},{3,7},{7,3},{8,12},{12,8},{9,1... | collective-permute-start | bytes 1769480 | tf_op jit(solution)/shard_map/ppermute | solution.py:226
  103.3 15.2 %collective-permute-start.8 = (bf16[256,1152]{1,0:T(8,128)(2,1)}, bf16[256,1152]{1,0:T(8,128)(2,1)S(1)}, u32[]{:S(2)}, u32[]{:S(2)}) collective-permute-start(bf16[256,1152]{1,0:T(8,128)(2,1)} %collective-permute-done.3.refs_4_), channel_id=1, source_target_pairs={{0,4},{4,0},{1,5},{5,1},{2,6},{6,2},{3,7},{7,3},{8,12},{12,8},{9,1... | collective-permute-start | bytes 1769480 | tf_op jit(solution)/shard_map/ppermute | solution.py:226
  121.7 1.3 collective-permute-start.9

commit v3 on v2

v3 whole, which is shorter than its diff:
```python
import functools

import jax
import jax.numpy as jnp
from jax import lax
from jax.experimental import pallas as pl
from jax.experimental.pallas import tpu as pltpu
from jax.sharding import Mesh, PartitionSpec as P

NZ, NY, NC, NX = 8, 4, 2, 4
CHIPS, COLUMNS, HOMES = NZ * NY * NX, NY * NX, NZ // 2
SLOTS = 16
NO_RANK = 1 << 20
NEAR, FAR = (0, 1, 7, 2), (6, 3, 5, 4)
TORUS = ("z", "y", "x")
PLANE = ("y", "x")
ALL = ("z", "y", "core", "x")
MIB = 2**20
TILE = 512
PIECE = COLUMNS * SLOTS


def dot(a, b, dims):
    return lax.dot_general(a, b, (dims, ((), ())), preferred_element_type=jnp.float32)


def digit_weights():
    which = lax.broadcasted_iota(jnp.int32, (128, 128), 0)
    weight = jnp.where(
        which == 0, 1, jnp.where(which == 1, 256, jnp.where(which == 2, 65536, -NO_RANK))
    )
    return jnp.where(which < 4, weight, 0).astype(jnp.float32).astype(jnp.bfloat16)


def pack_kernel(place_ref, emb_ref, clu_ref, rank_ref, rows_ref, home_ref, slot_ref):
    docs, features = emb_ref.shape
    wide = emb_ref[...].astype(jnp.float32)
    squares = jnp.sum(wide * wide, axis=1, keepdims=True) + 1e-06
    unit = (wide * lax.rsqrt(squares)).astype(jnp.bfloat16)
    clu = clu_ref[...]
    column, which_home = clu // HOMES, clu % HOMES
    home = which_home * 2 * COLUMNS + column
    on_home = lax.broadcasted_iota(jnp.int32, (CHIPS, docs), 0) == home
    member = on_home.astype(jnp.bfloat16)
    ahead = lax.broadcasted_iota(jnp.int32, (docs, docs), 0) < lax.broadcasted_iota(
        jnp.int32, (docs, docs), 1
    )
    before = dot(member, ahead.astype(jnp.bfloat16), ((1,), (0,)))
    slot = jnp.sum(jnp.where(on_home, before, 0.0), axis=0, keepdims=True).astype(jnp.int32)
    home_ref[...] = home
    slot_ref[...] = slot
    rank = rank_ref[...]
    which = lax.broadcasted_iota(jnp.int32, (128, docs), 0)
    digits = jnp.where(
        which == 0,
        rank & 255,
        jnp.where(which == 1, (rank >> 8) & 255, jnp.where(which == 2, rank >> 16, 1)),
    )
    digits = jnp.where(which < 4, digits, 0).astype(jnp.float32).astype(jnp.bfloat16)
    ahead_of_z = (which_home - (place_ref[1] + 1) // 2) & (HOMES - 1)
    at = (column * HOMES + ahead_of_z) * SLOTS + slot
    pick = lax.broadcasted_iota(jnp.int32, (rows_ref.shape[0], docs), 0) == at
    pick = jnp.where(pick, 1.0, 0.0).astype(jnp.bfloat16)
    rows_ref[:, :features] = dot(pick, unit, ((1,), (0,))).astype(jnp.bfloat16)
    rows_ref[:, features:] = dot(pick, digits, ((1,), (1,))).astype(jnp.bfloat16)


def pack(place, embeddings, cluster, doc_rank):
    docs, features = embeddings.shape
    vmem = pl.BlockSpec(memory_space=pltpu.VMEM)
    return pl.pallas_call(
        pack_kernel,
        out_shape=(
            jax.ShapeDtypeStruct((COLUMNS * HOMES * SLOTS, features + 128), jnp.bfloat16),
            jax.ShapeDtypeStruct((1, docs), jnp.int32),
            jax.ShapeDtypeStruct((1, docs), jnp.int32),
        ),
        in_specs=[pl.BlockSpec(memory_space=pltpu.SMEM), vmem, vmem, vmem],
        out_specs=(vmem,) * 3,
        compiler_params=pltpu.CompilerParams(vmem_limit_bytes=40 * MIB),
        name="pack",
    )(place, embeddings, cluster, doc_rank)


def compare_kernel(plan, sets, order, *refs):
    place_ref, refs = refs[0], list(refs[1:])
    pieces, start, outs = [], [], []
    for n, _ in sets:
        pieces.append([refs.pop(0) for _ in range(n)])
    for _, has in sets:
        start.append(refs.pop(0) if has else None)
    if order is None:
        outs = [refs.pop(0) for _ in sets]
    else:
        outs = [refs.pop(0) for _ in range(2)]
    scratch = [None if n == 0 else [refs.pop(0) for _ in range(5)] for n, _ in sets]
    weights = digit_weights()
    for held, buffers in zip(pieces, scratch):
        if not held:
            continue
        whole, by_row, by_col, row_rank, col_rank = buffers
        features = whole.shape[1] - 128
        part = held[0].shape[0]
        for p, piece in enumerate(held):
            whole[p * part : (p + 1) * part, :] = piece[...]
        tail = whole[:, features:]
        row_rank[...] = dot(tail, weights, ((1,), (0,))) + float(NO_RANK)
        col_rank[...] = dot(weights[:, :8], tail, ((0,), (1,))) + float(NO_RANK)
        by_row[...] = jnp.full(by_row.shape, -1.0, jnp.float32)
        by_col[...] = jnp.full(by_col.shape, -1.0, jnp.float32)
    core = place_ref[0]
    for (q, qb), (k, kb), both in plan:
        q_rows, by_row, _, row_rank, _ = scratch[q]
        k_rows, _, by_col, _, col_rank = scratch[k]
        q_at = pl.ds(pl.multiple_of((core if qb is None else qb) * TILE, TILE), TILE)
        k_at = pl.ds(pl.multiple_of((core if kb is None else kb) * TILE, TILE), TILE)
        scores = dot(q_rows[q_at, :features], k_rows[k_at, :features], ((1,), (1,)))
        q_rank = row_rank[q_at, :]
        top = by_row[q_at, :]
        k_rank = col_rank[0:1, k_at]
        side = []
        for c in range(TILE // 128):
            cols = slice(c * 128, (c + 1) * 128)
            part = scores[:, cols]
            earlier = k_rank[:, cols] < q_rank
            top = jnp.maximum(top, jnp.where(earlier, part, -1.0))
            if both:
                other = jnp.where(earlier, -1.0, part)
                side.append(jnp.max(other.reshape(TILE // 8, 8, 128), axis=0))
        by_row[q_at, :] = top
        if both:
            by_col[:, k_at] = jnp.maximum(by_col[:, k_at], jnp.concatenate(side, axis=1))
    for i, buffers in enumerate(scratch):
        best = None if start[i] is None else start[i][...]
        if buffers is not None:
            _, by_row, by_col, _, _ = buffers
            found = jnp.max(jnp.transpose(by_row[...]), axis=0, keepdims=True)
            found = jnp.maximum(found, jnp.max(by_col[...], axis=0, keepdims=True))
            best = found if best is None else jnp.maximum(best, found)
        if order is None:
            outs[i][...] = best
        else:
            which, steps = order[i]
            for p, step in enumerate(steps):
                came = (place_ref[1] - step) & (NZ - 1)
                outs[which][pl.ds(came, 1), :] = best[:, p * PIECE : (p + 1) * PIECE]


def compare(place, sets, plan, order, name):
    wide = sets[0][0][0].shape[1]
    rows = [sum(a.shape[0] for a in arrays) for arrays, _ in sets]
    vmem = pl.BlockSpec(memory_space=pltpu.VMEM)
    args = [a for arrays, _ in sets for a in arrays]
    args += [best for _, best in sets if best is not None]
    shapes = [(1, n) for n in rows] if order is None else [(NZ, PIECE)] * 2
    scratch = []
    for n in rows:
        if n:
            scratch += [
                pltpu.VMEM((n, wide), jnp.bfloat16),
                pltpu.VMEM((n, 128), jnp.float32),
                pltpu.VMEM((8, n), jnp.float32),
                pltpu.VMEM((n, 128), jnp.float32),
                pltpu.VMEM((8, n), jnp.float32),
            ]
    return pl.pallas_call(
        functools.partial(
            compare_kernel, plan, [(len(arrays), best is not None) for arrays, best in sets], order
        ),
        out_shape=tuple(jax.ShapeDtypeStruct(shape, jnp.float32) for shape in shapes),
        in_specs=[pl.BlockSpec(memory_space=pltpu.SMEM)] + [vmem] * len(args),
        out_specs=(vmem,) * len(shapes),
        scratch_shapes=scratch,
        compiler_params=pltpu.CompilerParams(vmem_limit_bytes=48 * MIB),
        cost_estimate=pl.CostEstimate(
            flops=2 * len(plan) * TILE * TILE * wide,
            bytes_accessed=2 * wide * sum(rows),
            transcendentals=0,
        ),
        name=name,
    )(place, *args)


def unpack_kernel(back_ref, home_ref, slot_ref, out_ref):
    docs = home_ref.shape[1]
    on_home = lax.broadcasted_iota(jnp.int32, (CHIPS, docs), 0) == home_ref[...]
    found = lax.dot_general(
        back_ref[...],
        on_home.astype(jnp.float32),
        (((0,), (0,)), ((), ())),
        precision=lax.Precision.HIGHEST,
        preferred_element_type=jnp.float32,
    )
    in_slot = lax.broadcasted_iota(jnp.int32, (SLOTS, docs), 0) == slot_ref[...]
    out_ref[...] = jnp.sum(jnp.where(in_slot, found, 0.0), axis=0, keepdims=True)


def unpack(back, home, slot):
    vmem = pl.BlockSpec(memory_space=pltpu.VMEM)
    return pl.pallas_call(
        unpack_kernel,
        out_shape=jax.ShapeDtypeStruct(home.shape, jnp.float32),
        in_specs=[vmem] * 3,
        out_specs=vmem,
        name="unpack",
    )(back, home, slot)


def up_z(a, step):
    pairs = [(z, (z + step) % NZ) for z in range(NZ) if (z + step) % 2 == 0]
    return lax.ppermute(a, "z", pairs)


def other_core(a):
    return lax.ppermute(a, "core", [(0, 1), (1, 0)])


def exchange(a, axes):
    return lax.all_to_all(a, axes, split_axis=0, concat_axis=0, tiled=True)


def per_device(embeddings, cluster, doc_rank):
    docs, features = embeddings.shape
    wide = features + 128
    place = jnp.stack([lax.axis_index("core"), lax.axis_index("z")]).astype(jnp.int32)
    rows, home, slot = pack(place, embeddings, cluster.reshape(1, docs), doc_rank.reshape(1, docs))
    rows = exchange(rows.reshape(COLUMNS, HOMES * SLOTS, wide), PLANE)
    rows = rows.reshape(COLUMNS, HOMES, SLOTS, wide)
    parts = [rows[:, h].reshape(PIECE, wide) for h in range(HOMES)]
    arrive = lambda steps: [up_z(parts[s // 2], s) if s else parts[0] for s in steps]
    near, far = arrive(NEAR), arrive(FAR)
    near_there = [other_core(a) for a in near]
    plan = (
        ((0, 0), (0, 0), False),
        ((0, 1), (0, 1), False),
        ((0, 0), (0, 1), True),
        ((0, 0), (1, 1), True),
        ((0, None), (1, None), True),
    )
    best_near, best_near_there = compare(
        place, [(near, None), (near_there, None)], plan, None, "compare_near"
    )
    far_there = [other_core(a) for a in far]
    plan = (
        ((0, 0), (0, 0), False),
        ((0, 1), (0, 1), False),
        ((0, 0), (0, 1), True),
        *(((0, q), (k, b), True) for q in (0, 1) for k in (1, 2) for b in (0, 1)),
    )
    best_far, best_near, best_near_there = compare(
        place,
        [(far, None), (near, best_near), (near_there, best_near_there)],
        plan,
        None,
        "compare_far",
    )
    plan = (((0, 0), (1, 1), True), ((0, None), (1, None), True))
    mine, theirs = compare(
        place,
        [(far, best_far), (far_there, None), ([], best_near), ([], best_near_there)],
        plan,
        ((0, FAR), (1, FAR), (0, NEAR), (1, NEAR)),
        "compare_cores",
    )
    result = jnp.maximum(mine, other_core(theirs)).reshape(CHIPS, SLOTS)
    return unpack(exchange(result, TORUS), home, slot).reshape(docs)


def solution(mesh):
    torus = Mesh(mesh.devices.reshape(NZ, NY, NC, NX), ALL)
    placed = (P(ALL, None), P(ALL), P(ALL))
    return jax.shard_map(
        per_device, mesh=torus, in_specs=placed, out_specs=P(ALL), check_vma=False
    )
```

time: 145 us -> 172 us (1.19)
  waiting for transfers between devices: 16.3 us -> 62.5 us
  blocking collectives: 90.1 us -> 56.5 us
  starting transfers between devices: 12.1 us -> 30.4 us
  Pallas kernels: 21.2 us -> 19.3 us
    ppermute x4 -> x7, waiting for transfers between devices: 15.1 us -> 61.1 us  [up_z(): return lax.ppermute(a, 'z', pairs)]
    all_to_all x2, blocking collectives: 90.1 us -> 56.5 us  [exchange(): return lax.all_to_all(a, axes, split_axis=0, concat_axis=0, tiled=True)]
    ppermute x4 -> x7, starting transfers between devices: 5.16 us -> 21 us  [up_z(): return lax.ppermute(a, 'z', pairs)]
    ppermute x6 -> x9, starting transfers between devices: 6.9 us -> 9.38 us  [other_core(): return lax.ppermute(a, 'core', [(0, 1), (1, 0)])]
    pallas_call x3, Pallas kernels: 17.5 us -> 15.1 us  [compare(): pl.pallas_call(functools.partial(compare_kernel, plan, [(len(arrays), bes...]
  transfers between devices with their start and end apart: 10 -> 16, of which waited for: 4 -> 4; matrix products, arithmetic and copies ran while one was open for 1% -> 0% of each run, Pallas kernels for 10% -> 7%
where the time goes in v3:
time: 172 us
  waiting for transfers between devices  62.5 us (36%)
  blocking collectives  56.5 us (33%)
  starting transfers between devices  30.4 us (18%)
  Pallas kernels  19.3 us (11%)
  local copies, waits for them, and re-layouts  2.86 us (2%)
    ppermute x7, waiting for transfers between devices, up_z(): return lax.ppermute(a, 'z', pairs)  61.1 us
    all_to_all x2, blocking collectives, exchange(): return lax.all_to_all(a, axes, split_axis=0, concat_axis=0, tiled=True)  56.5 us
    ppermute x7, starting transfers between devices, up_z(): return lax.ppermute(a, 'z', pairs)  21 us
    pallas_call x3, Pallas kernels, compare(): pl.pallas_call(functools.partial(compare_kernel, plan, [(len(arrays), bes...  15.1 us
    ppermute x9, starting transfers between devices, other_core(): return lax.ppermute(a, 'core', [(0, 1), (1, 0)])  9.38 us
  transfers between devices with their start and end apart: 16, of which 4 were waited for; matrix products, arithmetic and copies ran while one was open for 0% of the time, Pallas kernels for 7%

profile of v3, /device:TPU:1, one launch (start us, length us, event | category | flops | bytes accessed | tf_op | source)
XLA Modules:
  0.0 171.8 jit_solution(8433106698841694813)
XLA Ops:
  0.0 0.1 pad_add_fusion.place_ref.refs_0_
  0.1 1.2 copy-done
  1.3 0.7 copy-done.1
  2.0 0.7 copy-done.2
  2.7 2.5 %pack.1 = (bf16[1024,1152]{1,0:T(8,128)(2,1)S(1)}, s32[1,512]{1,0:T(1,128)S(1)}, s32[1,512]{1,0:T(1,128)S(1)}) custom-call(s32[2]{0:T(128)S(1)} %pad_add_fusion.place_ref.refs_0_, bf16[512,1024]{1,0:T(8,128)(2,1)S(1)} %copy-done, s32[1,512]{1,0:T(1,128)S(1)} %bitcast.18, s32[1,512]{1,0:T(1,128)S(1)} %bitcast.19), custom_call_target="tpu_custom_call" | custom-call | tf_op jit(solution)/shard_map/pack/pallas_call | solution.py:71
  5.1 37.7 %all_to_all.16 = bf16[16,64,1152]{2,1,0:T(8,128)(2,1)S(1)} all-to-all(bf16[16,64,1152]{2,1,0:T(8,128)(2,1)S(1)} %bitcast.13), channel_id=1, replica_groups=mesh['z'=8,'y'=4,'core'=2,'x'=4] {'y','x'}, dimensions={0} | all-to-all | bytes 4718592 | tf_op jit(solution)/shard_map/all_to_all | solution.py:219
  42.9 0.2 fusion
  43.1 1.3 collective-permute-start.8
  44.4 1.3 collective-permute-start.9
  45.7 4.9 %collective-permute-start.10 = (bf16[256,1152]{1,0:T(8,128)(2,1)S(1)}, bf16[256,1152]{1,0:T(8,128)(2,1)S(1)}, u32[]{:S(2)}, u32[]{:S(2)}) collective-permute-start(bf16[256,1152]{1,0:T(8,128)(2,1)S(1)} %bitcast.23), channel_id=1, source_target_pairs={{0,64},{64,128},{128,192},{192,0},{1,65},{65,129},{129,193},{193,1... | collective-permute-start | bytes 1769480 | tf_op jit(solution)/shard_map/ppermute | solution.py:211
  50.6 2.2 %collective-permute-start.11 = (bf16[256,1152]{1,0:T(8,128)(2,1)S(1)}, bf16[256,1152]{1,0:T(8,128)(2,1)S(1)}, u32[]{:S(2)}, u32[]{:S(2)}) collective-permute-start(bf16[256,1152]{1,0:T(8,128)(2,1)S(1)} %bitcast.15), channel_id=1, source_target_pairs={{0,4},{4,0},{1,5},{5,1},{2,6},{6,2},{3,7},{7,3},{8,12},{12,8},{9,1... | collective-permute-start | bytes 1769480 | tf_op jit(solution)/shard_map/ppermute | solution.py:215
  52.8 4.7 %collective-permute-start = (bf16[256,1152]{1,0:T(8,128)(2,1)S(1)}, bf16[256,1152]{1,0:T(8,128)(2,1)S(1)}, u32[]{:S(2)}, u32[]{:S(2)}) collective-permute-start(bf16[256,1152]{1,0:T(8,128)(2,1)S(1)} %bitcast.26), channel_id=1, source_target_pairs={{0,192},{64,0},{128,64},{192,128},{1,193},{65,1},{129,65},{193,129... | collective-permute-start | bytes 1769480 | tf_op jit(solution)/shard_map/ppermute | solution.py:211
  57.4 17.0 %collective-permute-done.8.refs_2_.refs_6_ = bf16[256,1152]{1,0:T(8,128)(2,1)S(1)} collective-permute-done((bf16[256,1152]{1,0:T(8,128)(2,1)S(1)}, bf16[256,1152]{1,0:T(8,128)(2,1)S(1)}, u32[]{:S(2)}, u32[]{:S(2)}) %collective-permute-start.8) | collective-permute-done | bytes 589856 | tf_op jit(solution)/shard_map/ppermute | solution.py:211
  74.4 1.3 collective-permute-start.1
  75.7 1.3 collective-permute-start.2
  77.0 6.3 %collective-permute-start.3 = (bf16[256,1152]{1,0:T(8,128)(2,1)S(1)}, bf16[256,1152]{1,0:T(8,128)(2,1)S(1)}, u32[]{:S(2)}, u32[]{:S(2)}) collective-permute-start(bf16[256,1152]{1,0:T(8,128)(2,1)S(1)} %bitcast.22), channel_id=1, source_target_pairs={{0,128},{64,192},{128,0},{192,64},{1,129},{65,193},{129,1},{193,65... | collective-permute-start | bytes 1769480 | tf_op jit(solution)/shard_map/ppermute | solution.py:211
  83.3 3.1 %collective-permute-start.12 = (bf16[256,1152]{1,0:T(8,128)(2,1)S(1)}, bf16[256,1152]{1,0:T(8,128)(2,1)S(1)}, u32[]{:S(2)}, u32[]{:S(2)}) collective-permute-start(bf16[256,1152]{1,0:T(8,128)(2,1)S(1)} %collective-permute-done.8.refs_2_.refs_6_), channel_id=1, source_target_pairs={{0,4},{4,0},{1,5},{5,1},{2,6},{6,2},{3,7},{7,3},{8,12},{12,8},{9,1... | collective-permute-start | bytes 1769480 | tf_op jit(solution)/shard_map/ppermute | solution.py:215
  86.4 0.1 collective-permute-start.13
  86.5 44.1 %collective-permute-done.1.refs_2_ = bf16[256,1152]{1,0:T(8,128)(2,1)S(1)} collective-permute-done((bf16[256,1152]{1,0:T(8,128)(2,1)S(1)}, bf16[256,1152]{1,0:T(8,128)(2,1)S(1)}, u32[]{:S(2)}, u32[]{:S(2)}) %collective-permute-start.1) | collective-permute-done | bytes 589856 | tf_op jit(solution)/shard_map/ppermute | solution.py:211
  130.6 2.5 %collective-permute-start.14 = (bf16[256,1152]{1,0:T(8,128)(2,1)S(1)}, bf16[256,1152]{1,0:T(8,128)(2,1)S(1)}, u32[]{:S(2)}, u32[]{:S(2)}) collective-permute-start(bf16[256,1152]{1,0:T(8,128)(2,1)S(1)} %collective-permute-done.10.refs_4_.refs_8_), channel_id=1, source_target_pairs={{0,4},{4,0},{1,5},{5,1},{2,6},{6,2},{3,7},{7,3},{8,12},{12,8},{9,1... | collective-permute-start | bytes 1769480 | tf_op jit(solution)/shard_map/ppermute | solution.py:215
  133.2 0.5 collective-permute-start.5
  133.7 0.1 collective-permute-start.6
  133.8 0.4 collective-permute-start.7
  134.2 0.6 collective-permute-done.14.refs_8_.refs_12_
  134.8 4.1 %compare_near.1 = (f32[1,1024]{1,0:T(1,128)S(1)}, f32[1,1024]{1,0:T(1,128)S(1)}) custom-call(s32[2]{0:T(128)S(1)} %pad_add_fusion.place_ref.refs_0_, bf16[256,1152]{1,0:T(8,128)(2,1)S(1)} %bitcast.16, bf16[256,1152]{1,0:T(8,128)(2,1)S(1)} %collective-permute-done.8.refs_2_.refs_6_, bf16[256,1152]{1,0:T(8,128)(2,1)S(1)} %collective-permute-done.9.refs_3_.refs_7_, ...), custom_call_target="tpu_custom_call" | custom-call | flops 3019898880 | bytes 4718592 | tf_op jit(solution)/shard_map/compare_near/pallas_call | solution.py:166
  138.9 8.6 %compare_far.1 = (f32[1,1024]{1,0:T(1,128)S(1)}, f32[1,1024]{1,0:T(1,128)S(1)}, f32[1,1024]{1,0:T(1,128)S(1)}) custom-call(s32[2]{0:T(128)S(1)} %pad_add_fusion.place_ref.refs_0_, bf16[256,1152]{1,0:T(8,128)(2,1)S(1)} %collective-permute-done.refs_1_, bf16[256,1152]{1,0:T(8,128)(2,1)S(1)} %collective-permute-done.1.refs_2_, ...), custom_call_target="tpu_custom_call" | custom-call | flops 6643777536 | bytes 7077888 | tf_op jit(solution)/shard_map/compare_far/pallas_call | solution.py:166
  147.5 2.4 %compare_cores.1 = (f32[8,256]{1,0:T(8,128)S(1)}, f32[8,256]{1,0:T(8,128)S(1)}) custom-call(s32[2]{0:T(128)S(1)} %pad_add_fusion.place_ref.refs_0_, bf16[256,1152]{1,0:T(8,128)(2,1)S(1)} %collective-permute-done.refs_1_, bf16[256,1152]{1,0:T(8,128)(2,1)S(1)} %collective-permute-done.1.refs_2_, bf16[256,1152]{1,0:T(8,128)(2,1)S(1)} %collective-permute-done.2.refs_3_, ...), custom_call_target="tpu_custom_call" | custom-call | flops 1207959552 | bytes 4718592 | tf_op jit(solution)/shard_map/compare_cores/pallas_call | solution.py:166
  150.0 0.5 collective-permute-start.15
  150.4 0.8 collective-permute-done.15
  151.3 0.1 all_to_all.11
  151.4 18.7 %all_to_all.17 = f32[128,1,16]{2,1,0:T(1,128)} all-to-all(f32[128,1,16]{2,1,0:T(1,128)S(1)} %bitcast.28), channel_id=1, replica_groups=mesh['z'=8,'y'=4,'core'=2,'x'=4] {'z','y','x'}, dimensions={0} | all-to-all | bytes 16384 | tf_op jit(solution)/shard_map/all_to_all | solution.py:219
  170.1 1.7 unpack.1
  (25 shorter events, 0.1 us)
Async XLA Ops:
  0.1 1.2 copy-start
  1.3 0.7 copy-start.1
  2.0 0.7 copy-start.2
  5.1 37.8 %copy-start.3 = (s32[1,512]{1,0:T(1,128)}, s32[1,512]{1,0:T(1,128)S(1)}, u32[]{:S(2)}) copy-start(s32[1,512]{1,0:T(1,128)S(1)} %get-tuple-element.23.home_ref) | copy-start | bytes 6148
  5.1 37.8 %copy-start.4 = (s32[1,512]{1,0:T(1,128)}, s32[1,512]{1,0:T(1,128)S(1)}, u32[]{:S(2)}) copy-start(s32[1,512]{1,0:T(1,128)S(1)} %get-tuple-element.24.slot_ref) | copy-start | bytes 6148
  43.1 31.3 %collective-permute-start.8 = (bf16[256,1152]{1,0:T(8,128)(2,1)S(1)}, bf16[256,1152]{1,0:T(8,128)(2,1)S(1)}, u32[]{:S(2)}, u32[]{:S(2)}) collective-permute-start(bf16[256,1152]{1,0:T(8,128)(2,1)S(1)} %bitcast.14), channel_id=1, source_target_pairs={{32,64},{96,128},{160,192},{224,0},{33,65},{97,129},{161,193},{225... | collective-permute-start | bytes 1769480 | tf_op jit(solution)/shard_map/ppermute | solution.py:211
  44.4 31.3 %collective-permute-start.9 = (bf16[256,1152]{1,0:T(8,128)(2,1)S(1)}, bf16[256,1152]{1,0:T(8,128)(2,1)S(1)}, u32[]{:S(2)}, u32[]{:S(2)}) collective-permute-start(bf16[256,1152]{1,0:T(8,128)(2,1)S(1)} %bitcast.25), channel_id=1, source_target_pairs={{32,0},{96,64},{160,128},{224,192},{33,1},{97,65},{161,129},{225,1... | collective-permute-start | bytes 1769480 | tf_op jit(solution)/shard_map/ppermute | solution.py:211
  45.7 31.3 %collective-permute-start.10 = (bf16[256,1152]{1,0:T(8,128)(2,1)S(1)}, bf16[256,1152]{1,0:T(8,128)(2,1)S(1)}, u32[]{:S(2)}, u32[]{:S(2)}) collective-permute-start(bf16[256,1152]{1,0:T(8,128)(2,1)S(1)} %bitcast.23), channel_id=1, source_target_pairs={{0,64},{64,128},{128,192},{192,0},{1,65},{65,129},{129,193},{193,1... | collective-permute-start | bytes 1769480 | tf_op jit(solution)/shard_map/ppermute | solution.py:211
  50.6 32.7 %collective-permute-start.11 = (bf16[256,1152]{1,0:T(8,128)(2,1)S(1)}, bf16[256,1152]{1,0:T(8,128)(2,1)S(1)}, u32[]{:S(2)}, u32[]{:S(2)}) collective-permute-start(bf16[256,1152]{1,0:T(8,128)(2,1)S(1)} %bitcast.15), channel_id=1, source_target_pairs={{0,4},{4,0},{1,5},{5,1},{2,6},{6,2},{3,7},{7,3},{8,12},{12,8},{9,1... | collective-permute-start | bytes 1769480 | tf_op jit(solution)/shard_map/ppermute | solution.py:215
  52.8 33.6 %collective-permute-start = (bf16[256,1152]{1,0:T(8,128)(2,1)S(1)}, bf16[256,1152]{1,0:T(8,128)(2,1)S(1)}, u32[]{:S(2)}, u32[]{:S(2)}) collective-permute-start(bf16[256,1152]{1,0:T(8,128)(2,1)S(1)} %bitcast.26), channel_id=1, source_target_pairs={{0,192},{64,0},{128,64},{192,128},{1,193},{65,1},{129,65},{193,129... | collective-permute-start | bytes 1769480 | tf_op jit(solution)/shard_map/ppermute | solution.py:211
  74.4 56.2 %collective-permute-start.1 = (bf16[256,1152]{1,0:T(8,128)(2,1)S(1)}, bf16[256,1152]{1,0:T(8,128)(2,1)S(1)}, u32[]{:S(2)}, u32[]{:S(2)}) collective-permute-start(bf16[256,1152]{1,0:T(8,128)(2,1)S(1)} %bitcast.24), channel_id=1, source_target_pairs={{32,128},{96,192},{160,0},{224,64},{33,129},{97,193},{161,1},{225,... | collective-permute-start | bytes 1769480 | tf_op jit(solution)/shard_map/ppermute | solution.py:211
  75.7 57.4 %collective-permute-start.2 = (bf16[256,1152]{1,0:T(8,128)(2,1)S(1)}, bf16[256,1152]{1,0:T(8,128)(2,1)S(1)}, u32[]{:S(2)}, u32[]{:S(2)}) collective-permute-start(bf16[256,1152]{1,0:T(8,128)(2,1)S(1)} %bitcast.21), channel_id=1, source_target_pairs={{32,192},{96,0},{160,64},{224,128},{33,193},{97,1},{161,65},{225,1... | collective-permute-start | bytes 1769480 | tf_op jit(solution)/shard_map/ppermute | solution.py:211
  77.0 56.1 %collective-permute-start.3 = (bf16[256,1152]{1,0:T(8,128)(2,1)S(1)}, bf16[256,1152]{1,0:T(8,128)(2,1)S(1)}, u32[]{:S(2)}, u32[]{:S(2)}) collective-permute-start(bf16[256,1152]{1,0:T(8,128)(2,1)S(1)} %bitcast.22), channel_id=1, source_target_pairs={{0,128},{64,192},{128,0},{192,64},{1,129},{65,193},{129,1},{193,65... | collective-permute-start | bytes 1769480 | tf_op jit(solution)/shard_map/ppermute | solution.py:211
  83.3 50.4 %collective-permute-start.12 = (bf16[256,1152]{1,0:T(8,128)(2,1)S(1)}, bf16[256,1152]{1,0:T(8,128)(2,1)S(1)}, u32[]{:S(2)}, u32[]{:S(2)}) collective-permute-start(bf16[256,1152]{1,0:T(8,128)(2,1)S(1)} %collective-permute-done.8.refs_2_.refs_6_), channel_id=1, source_target_pairs={{0,4},{4,0},{1,5},{5,1},{2,6},{6,2},{3,7},{7,3},{8,12},{12,8},{9,1... | collective-permute-start | bytes 1769480 | tf_op jit(solution)/shard_map/ppermute | solution.py:215
  86.4 47.4 %collective-permute-start.13 = (bf16[256,1152]{1,0:T(8,128)(2,1)S(1)}, bf16[256,1152]{1,0:T(8,128)(2,1)S(1)}, u32[]{:S(2)}, u32[]{:S(2)}) collective-permute-start(bf16[256,1152]{1,0:T(8,128)(2,1)S(1)} %collective-permute-done.9.refs_3_.refs_7_), channel_id=1, source_target_pairs={{0,4},{4,0},{1,5},{5,1},{2,6},{6,2},{3,7},{7,3},{8,12},{12,8},{9,1... | collective-permute-start | bytes 1769480 | tf_op jit(solution)/shard_map/ppermute | solution.py:215
  130.6 4.2 %collective-permute-start.14 = (bf16[256,1152]{1,0:T(8,128)(2,1)S(1)}, bf16[256,1152]{1,0:T(8,128)(2,1)S(1)}, u32[]{:S(2)}, u32[]{:S(2)}) collective-permute-start(bf16[256,1152]{1,0:T(8,128)(2,1)S(1)} %collective-permute-done.10.refs_4_.refs_8_), channel_id=1, source_target_pairs={{0,4},{4,0},{1,5},{5,1},{2,6},{6,2},{3,7},{7,3},{8,12},{12,8},{9,1... | collective-permute-start | bytes 1769480 | tf_op jit(solution)/shard_map/ppermute | solution.py:215
  133.1 14.4 %collective-permute-start.4 = (bf16[256,1152]{1,0:T(8,128)(2,1)S(1)}, bf16[256,1152]{1,0:T(8,128)(2,1)S(1)}, u32[]{:S(2)}, u32[]{:S(2)}) collective-permute-start(bf16[256,1152]{1,0:T(8,128)(2,1)S(1)} %collective-permute-done.refs_1_), channel_id=1, source_target_pairs={{0,4},{4,0},{1,5},{5,1},{2,6},{6,2},{3,7},{7,3},{8,12},{12,8},{9,1... | collective-permute-start | bytes 1769480 | tf_op jit(solution)/shard_map/ppermute | solution.py:215
  133.2 14.4 %collective-permute-start.5 = (bf16[256,1152]{1,0:T(8,128)(2,1)S(1)}, bf16[256,1152]{1,0:T(8,128)(2,1)S(1)}, u32[]{:S(2)}, u32[]{:S(2)}) collective-permute-start(bf16[256,1152]{1,0:T(8,128)(2,1)S(1)} %collective-permute-done.1.refs_2_), channel_id=1, source_target_pairs={{0,4},{4,0},{1,5},{5,1},{2,6},{6,2},{3,7},{7,3},{8,12},{12,8},{9,1... | collective-permute-start | bytes 1769480 | tf_op jit(solution)/shard_map/ppermute | solution.py:215
  133.7 13.9 %collective-permute-start.6 = (bf16[256,1152]{1,0:T(8,128)(2,1)S(1)}, bf16[256,1152]{1,0:T(8,128)(2,1)S(1)}, u32[]{:S(2)}, u32[]{:S(2)}) collective-permute-start(bf16[256,1152]{1,0:T(8,128)(2,1)S(1)} %collective-permute-done.2.refs_3_), channel_id=1, source_target_pairs={{0,4},{4,0},{1,5},{5,1},{2,6},{6,2},{3,7},{7,3},{8,12},{12,8},{9,1... | collective-permute-start | bytes 1769480 | tf_op jit(solution)/shard_map/ppermute | solution.py:215
  133.8 5.1 %copy-start.5 = (bf16[256,1152]{1,0:T(8,128)(2,1)}, bf16[256,1152]{1,0:T(8,128)(2,1)S(1)}, u32[]{:S(2)}) copy-start(bf16[256,1152]{1,0:T(8,128)(2,1)S(1)} %collective-permute-done.13.refs_7_.refs_11_) | copy-start | bytes 1769476
  133.8 13.8 %collective-permute-start.7 = (bf16[256,1152]{1,0:T(8,128)(2,1)S(1)}, bf16[256,1152]{1,0:T(8,128)(2,1)S(1)}, u32[]{:S(2)}, u32[]{:S(2)}) collective-permute-start(bf16[256,1152]{1,0:T(8,128)(2,1)S(1)} %collective-permute-done.3.refs_4_), channel_id=1, source_target_pairs={{0,4},{4,0},{1,5},{5,1},{2,6},{6,2},{3,7},{7,3},{8,12},{12,8},{9,1... | collective-permute-start | bytes 1769480 | tf_op jit(solution)/shard_map/ppermute | solution.py:215
  134.8 4.1 %copy-start.6 = (bf16[256,1152]{1,0:T(8,128)(2,1)}, bf16[256,1152]{1,0:T(8,128)(2,1)S(1)}, u32[]{:S(2)}) copy-start(bf16[256,1152]{1,0:T(8,128)(2,1)S(1)} %collective-permute-done.14.refs_8_.refs_12_) | copy-start | bytes 1769476
  150.0 1.3 collective-permute-start.15

commit v4 on v2

--- a/solution.py
+++ b/solution.py
@@ -31,12 +31,12 @@
     return jnp.where(which < 4, weight, 0).astype(jnp.float32).astype(jnp.bfloat16)
 
 
-def pack_kernel(group_ref, emb_ref, clu_ref, rank_ref, rows_ref, home_ref, slot_ref):
+def pack_kernel(group_ref, emb_ref, labels_ref, rows_ref, home_ref, slot_ref):
     docs, features = emb_ref.shape
     wide = emb_ref[...].astype(jnp.float32)
     squares = jnp.sum(wide * wide, axis=1, keepdims=True) + 1e-06
     unit = (wide * lax.rsqrt(squares)).astype(jnp.bfloat16)
-    clu = clu_ref[...]
+    clu = labels_ref[0:1, :]
     z, y, xh = clu // 8, (clu // 2) % 4, clu % 2
     x = 2 * xh + (y + z) % 2
     home = (z * NY + y) * NX + x
@@ -49,7 +49,7 @@
     slot = jnp.sum(jnp.where(on_home, before, 0.0), axis=0, keepdims=True).astype(jnp.int32)
     home_ref[...] = home
     slot_ref[...] = slot
-    rank = rank_ref[...]
+    rank = labels_ref[1:2, :]
     which = lax.broadcasted_iota(jnp.int32, (128, docs), 0)
     digits = jnp.where(
         which == 0,
@@ -68,7 +68,7 @@
     rows_ref[:, features:] = dot(pick, digits, ((1,), (1,))).astype(jnp.bfloat16)
 
 
-def pack(group, embeddings, cluster, doc_rank):
+def pack(group, embeddings, labels):
     docs, features = embeddings.shape
     vmem = pl.BlockSpec(memory_space=pltpu.VMEM)
     return pl.pallas_call(
@@ -78,11 +78,11 @@
             jax.ShapeDtypeStruct((1, docs), jnp.int32),
             jax.ShapeDtypeStruct((1, docs), jnp.int32),
         ),
-        in_specs=[pl.BlockSpec(memory_space=pltpu.SMEM), vmem, vmem, vmem],
+        in_specs=[pl.BlockSpec(memory_space=pltpu.SMEM), vmem, vmem],
         out_specs=(vmem,) * 3,
-        compiler_params=pltpu.CompilerParams(vmem_limit_bytes=40 * MIB),
+        compiler_params=pltpu.CompilerParams(vmem_limit_bytes=24 * MIB),
         name="pack",
-    )(group, embeddings, cluster, doc_rank)
+    )(group, embeddings, labels)
 
 
 def compare_kernel(plan, sets, *refs):
@@ -174,7 +174,7 @@
         in_specs=[pl.BlockSpec(memory_space=pltpu.SMEM)] + [vmem] * len(args),
         out_specs=(vmem,) * len(wanted),
         scratch_shapes=scratch,
-        compiler_params=pltpu.CompilerParams(vmem_limit_bytes=48 * MIB),
+        compiler_params=pltpu.CompilerParams(vmem_limit_bytes=24 * MIB),
         cost_estimate=pl.CostEstimate(
             flops=2 * len(plan) * TILE * TILE * wide,
             bytes_accessed=2 * wide * sum(rows),
@@ -234,7 +234,7 @@
     docs, features = embeddings.shape
     group = (lax.axis_index("z") // 2).reshape(1)
     core = lax.axis_index("core").reshape(1)
-    rows, home, slot = pack(group, embeddings, cluster.reshape(1, docs), doc_rank.reshape(1, docs))
+    rows, home, slot = pack(group, embeddings, jnp.stack([cluster, doc_rank]))
     wide = features + 128
     near = exchange(rows.reshape(CHIPS, HALF, wide)).reshape(CHIPS * HALF, wide)
     part = near.shape[0] // 4
@@ -253,6 +253,7 @@
     best_near, best_near_there = compare(
         core, [([near], None, True), ([near_there], None, True)], plan, "compare_near"
     )
+    far, best_near, best_near_there = lax.optimization_barrier((far, best_near, best_near_there))
     far_there = [other_core(a) for a in far]
     plan = (
         ((0, 0), (0, 0), False),

time: 145 us -> 139 us (0.959)
  waiting for transfers between devices: 16.3 us -> 12.8 us
    ppermute x4, waiting for transfers between devices: 15.1 us -> 12 us  [per_device(): lax.ppermute(near[i * part:(i + 1) * part], ALL, to_home(step))]
  transfers between devices with their start and end apart: 10 -> 10, of which waited for: 4 -> 5; matrix products, arithmetic and copies ran while one was open for 1% -> 1% of each run, Pallas kernels for 10% -> 10%
where the time goes in v4:
time: 139 us
  blocking collectives  89.4 us (64%)
  Pallas kernels  21.2 us (15%)
  waiting for transfers between devices  12.8 us (9%)
  starting transfers between devices  11.5 us (8%)
  local copies, waits for them, and re-layouts  2.89 us (2%)
    all_to_all x2, blocking collectives, exchange(): return lax.all_to_all(a, TORUS, split_axis=0, concat_axis=0, tiled=True)  89.4 us
    pallas_call x3, Pallas kernels, compare(): pl.pallas_call(functools.partial(compare_kernel, plan, [(len(arrays), bes...  17.5 us
    ppermute x4, waiting for transfers between devices, per_device(): lax.ppermute(near[i * part:(i + 1) * part], ALL, to_home(step))  12 us
    ppermute x6, starting transfers between devices, other_core(): return lax.ppermute(a, 'core', [(0, 1), (1, 0)])  6.34 us
    ppermute x4, starting transfers between devices, per_device(): lax.ppermute(near[i * part:(i + 1) * part], ALL, to_home(step))  5.16 us
  transfers between devices with their start and end apart: 10, of which 5 were waited for; matrix products, arithmetic and copies ran while one was open for 1% of the time, Pallas kernels for 10%

profile of v4, /device:TPU:1, one launch (start us, length us, event | category | flops | bytes accessed | tf_op | source)
XLA Modules:
  0.0 138.7 jit_solution(11770369851835898454)
XLA Ops:
  0.0 0.7 pad_add_fusion.labels_ref
  0.7 1.2 copy-done
  1.9 1.9 %pack.1 = (bf16[1024,1152]{1,0:T(8,128)(2,1)S(1)}, s32[1,512]{1,0:T(1,128)S(1)}, s32[1,512]{1,0:T(1,128)S(1)}) custom-call(s32[1]{0:T(128)} %bitcast.1.group_ref, bf16[512,1024]{1,0:T(8,128)(2,1)S(1)} %copy-done, s32[2,512]{1,0:T(2,128)S(1)} %pad_add_fusion.labels_ref), custom_call_target="tpu_custom_call" | custom-call | tf_op jit(solution)/shard_map/pack/pallas_call | solution.py:74
  3.9 70.9 %all_to_all.16 = bf16[128,8,1152]{2,1,0:T(8,128)(2,1)S(1)} all-to-all(bf16[128,8,1152]{2,1,0:T(8,128)(2,1)S(1)} %bitcast.22), channel_id=1, replica_groups=mesh['z'=8,'y'=4,'core'=2,'x'=4] {'z','y','x'}, dimensions={0} | all-to-all | bytes 4718592 | tf_op jit(solution)/shard_map/all_to_all | solution.py:230
  74.8 4.4 %collective-permute-start.4 = (bf16[1024,1152]{1,0:T(8,128)(2,1)S(1)}, bf16[1024,1152]{1,0:T(8,128)(2,1)}, u32[]{:S(2)}, u32[]{:S(2)}) collective-permute-start(bf16[1024,1152]{1,0:T(8,128)(2,1)S(1)} %bitcast.19), channel_id=1, source_target_pairs={{0,4},{4,0},{1,5},{5,1},{2,6},{6,2},{3,7},{7,3},{8,12},{12,8},{9,1... | collective-permute-start | bytes 7077896 | tf_op jit(solution)/shard_map/ppermute | solution.py:226
  79.3 1.5 %slice_bitcast_fusion = (bf16[256,1152]{1,0:T(8,128)(2,1)}, bf16[256,1152]{1,0:T(8,128)(2,1)}, bf16[256,1152]{1,0:T(8,128)(2,1)}, bf16[256,1152]{1,0:T(8,128)(2,1)}) fusion(bf16[128,8,1152]{2,1,0:T(8,128)(2,1)S(1)} %all_to_all.16), kind=kLoop, calls=%fused_computation | loop fusion | bytes 4718592 | tf_op jit(solution)/shard_map/slice | solution.py:242
  80.8 1.3 collective-permute-start.3
  82.1 1.3 collective-permute-start.2
  83.4 1.3 collective-permute-start.1
  84.7 1.3 collective-permute-start
  86.0 0.0 collective-permute-done.4.refs_2_.refs_6_
  86.0 5.1 %compare_near.1 = (f32[1,1024]{1,0:T(1,128)S(1)}, f32[1,1024]{1,0:T(1,128)S(1)}) custom-call(s32[1]{0:T(128)} %bitcast.refs_0_, bf16[1024,1152]{1,0:T(8,128)(2,1)S(1)} %bitcast.20, bf16[1024,1152]{1,0:T(8,128)(2,1)} %collective-permute-done.4.refs_2_.refs_6_), custom_call_target="tpu_custom_call" | custom-call | flops 3019898880 | bytes 4718592 | tf_op jit(solution)/shard_map/compare_near/pallas_call | solution.py:167
  91.1 6.8 %collective-permute-done.3.refs_4_ = bf16[256,1152]{1,0:T(8,128)(2,1)S(1)} collective-permute-done((bf16[256,1152]{1,0:T(8,128)(2,1)}, bf16[256,1152]{1,0:T(8,128)(2,1)S(1)}, u32[]{:S(2)}, u32[]{:S(2)}) %collective-permute-start.3) | collective-permute-done | bytes 589856 | tf_op jit(solution)/shard_map/ppermute | solution.py:242
  97.9 2.5 %collective-permute-done.2.refs_3_ = bf16[256,1152]{1,0:T(8,128)(2,1)S(1)} collective-permute-done((bf16[256,1152]{1,0:T(8,128)(2,1)}, bf16[256,1152]{1,0:T(8,128)(2,1)S(1)}, u32[]{:S(2)}, u32[]{:S(2)}) %collective-permute-start.2) | collective-permute-done | bytes 589856 | tf_op jit(solution)/shard_map/ppermute | solution.py:242
  100.4 0.1 collective-permute-done.1.refs_2_
  100.5 2.6 %collective-permute-done.refs_1_ = bf16[256,1152]{1,0:T(8,128)(2,1)} collective-permute-done((bf16[256,1152]{1,0:T(8,128)(2,1)}, bf16[256,1152]{1,0:T(8,128)(2,1)}, u32[]{:S(2)}, u32[]{:S(2)}) %collective-permute-start) | collective-permute-done | bytes 589856 | tf_op jit(solution)/shard_map/ppermute | solution.py:242
  103.1 0.8 collective-permute-start.5
  103.9 0.0 collective-permute-start.6
  103.9 0.5 collective-permute-start.7
  104.4 0.0 collective-permute-start.8
  104.4 9.3 %compare_far.1 = (f32[1,1024]{1,0:T(1,128)S(1)}, f32[1,1024]{1,0:T(1,128)S(1)}, f32[1,1024]{1,0:T(1,128)S(1)}) custom-call(s32[1]{0:T(128)} %bitcast.refs_0_, bf16[256,1152]{1,0:T(8,128)(2,1)} %collective-permute-done.refs_1_, bf16[256,1152]{1,0:T(8,128)(2,1)} %collective-permute-done.1.refs_2_, bf16[256,1152]{1,0:T(8,128)(2,1)S(1)} %collective-permute-done.2.refs_3_, ...), custom_call_target="tpu_custom_call" | custom-call | flops 6643777536 | bytes 7077888 | tf_op jit(solution)/shard_map/compare_far/pallas_call | solution.py:167
  113.7 0.0 collective-permute-done.5.refs_5_
  113.7 0.0 collective-permute-done.7.refs_7_
  113.7 0.0 collective-permute-done.8.refs_8_
  113.7 3.1 %compare_cores.1 = (f32[1,1024]{1,0:T(1,128)S(1)}, f32[1,1024]{1,0:T(1,128)S(1)}) custom-call(s32[1]{0:T(128)} %bitcast.refs_0_, bf16[256,1152]{1,0:T(8,128)(2,1)} %collective-permute-done.refs_1_, bf16[256,1152]{1,0:T(8,128)(2,1)} %collective-permute-done.1.refs_2_, bf16[256,1152]{1,0:T(8,128)(2,1)S(1)} %collective-permute-done.2.refs_3_, ...), custom_call_target="tpu_custom_call" | custom-call | flops 1207959552 | bytes 4718592 | tf_op jit(solution)/shard_map/compare_cores/pallas_call | solution.py:167
  116.8 0.6 collective-permute-start.9
  117.4 0.8 collective-permute-done.9
  118.3 0.1 squeeze.6
  118.4 0.1 squeeze.7
  118.5 0.1 pad_maximum_fusion
  118.6 18.4 %all_to_all.17 = f32[128,1,16]{2,1,0:T(1,128)} all-to-all(f32[128,1,16]{2,1,0:T(1,128)S(1)} %bitcast.23), channel_id=1, replica_groups=mesh['z'=8,'y'=4,'core'=2,'x'=4] {'z','y','x'}, dimensions={0} | all-to-all | bytes 16384 | tf_op jit(solution)/shard_map/all_to_all | solution.py:230
  137.0 1.7 %unpack.1 = f32[1,512]{1,0:T(1,128)} custom-call(f32[128,16]{1,0:T(8,128)} %bitcast.24, s32[1,512]{1,0:T(1,128)} %copy-done.1, s32[1,512]{1,0:T(1,128)} %copy-done.2), custom_call_target="tpu_custom_call" | custom-call | tf_op jit(solution)/shard_map/unpack/pallas_call | solution.py:203
  (9 shorter events, 0.1 us)
Async XLA Ops:
  0.7 1.2 copy-start
  3.9 71.0 %copy-start.1 = (s32[1,512]{1,0:T(1,128)}, s32[1,512]{1,0:T(1,128)S(1)}, u32[]{:S(2)}) copy-start(s32[1,512]{1,0:T(1,128)S(1)} %get-tuple-element.35.home_ref) | copy-start | bytes 6148
  3.9 71.0 %copy-start.2 = (s32[1,512]{1,0:T(1,128)}, s32[1,512]{1,0:T(1,128)S(1)}, u32[]{:S(2)}) copy-start(s32[1,512]{1,0:T(1,128)S(1)} %get-tuple-element.36.slot_ref) | copy-start | bytes 6148
  74.8 11.1 %collective-permute-start.4 = (bf16[1024,1152]{1,0:T(8,128)(2,1)S(1)}, bf16[1024,1152]{1,0:T(8,128)(2,1)}, u32[]{:S(2)}, u32[]{:S(2)}) collective-permute-start(bf16[1024,1152]{1,0:T(8,128)(2,1)S(1)} %bitcast.19), channel_id=1, source_target_pairs={{0,4},{4,0},{1,5},{5,1},{2,6},{6,2},{3,7},{7,3},{8,12},{12,8},{9,1... | collective-permute-start | bytes 7077896 | tf_op jit(solution)/shard_map/ppermute | solution.py:226
  80.8 17.2 %collective-permute-start.3 = (bf16[256,1152]{1,0:T(8,128)(2,1)}, bf16[256,1152]{1,0:T(8,128)(2,1)S(1)}, u32[]{:S(2)}, u32[]{:S(2)}) collective-permute-start(bf16[256,1152]{1,0:T(8,128)(2,1)} %get-tuple-element.39), channel_id=1, source_target_pairs={{1,25},{3,27},{5,29},{7,31},{8,0},{10,2},{12,4},{14,6},{17,9},{19,... | collective-permute-start | bytes 1769480 | tf_op jit(solution)/shard_map/ppermute | solution.py:242
  82.1 18.4 %collective-permute-start.2 = (bf16[256,1152]{1,0:T(8,128)(2,1)}, bf16[256,1152]{1,0:T(8,128)(2,1)S(1)}, u32[]{:S(2)}, u32[]{:S(2)}) collective-permute-start(bf16[256,1152]{1,0:T(8,128)(2,1)} %get-tuple-element.40), channel_id=1, source_target_pairs={{1,9},{3,11},{5,13},{7,15},{8,16},{10,18},{12,20},{14,22},{17,25},... | collective-permute-start | bytes 1769480 | tf_op jit(solution)/shard_map/ppermute | solution.py:242
  83.4 17.2 %collective-permute-start.1 = (bf16[256,1152]{1,0:T(8,128)(2,1)}, bf16[256,1152]{1,0:T(8,128)(2,1)}, u32[]{:S(2)}, u32[]{:S(2)}) collective-permute-start(bf16[256,1152]{1,0:T(8,128)(2,1)} %get-tuple-element.41), channel_id=1, source_target_pairs={{1,0},{3,2},{5,4},{7,6},{8,11},{10,9},{12,15},{14,13},{17,16},{19,... | collective-permute-start | bytes 1769480 | tf_op jit(solution)/shard_map/ppermute | solution.py:242
  84.7 18.4 %collective-permute-start = (bf16[256,1152]{1,0:T(8,128)(2,1)}, bf16[256,1152]{1,0:T(8,128)(2,1)}, u32[]{:S(2)}, u32[]{:S(2)}) collective-permute-start(bf16[256,1152]{1,0:T(8,128)(2,1)} %get-tuple-element.42), channel_id=1, source_target_pairs={{1,2},{3,0},{5,6},{7,4},{8,9},{10,11},{12,13},{14,15},{17,18},{19,... | collective-permute-start | bytes 1769480 | tf_op jit(solution)/shard_map/ppermute | solution.py:242
  103.1 10.6 %collective-permute-start.5 = (bf16[256,1152]{1,0:T(8,128)(2,1)}, bf16[256,1152]{1,0:T(8,128)(2,1)S(1)}, u32[]{:S(2)}, u32[]{:S(2)}) collective-permute-start(bf16[256,1152]{1,0:T(8,128)(2,1)} %collective-permute-done.refs_1_), channel_id=1, source_target_pairs={{0,4},{4,0},{1,5},{5,1},{2,6},{6,2},{3,7},{7,3},{8,12},{12,8},{9,1... | collective-permute-start | bytes 1769480 | tf_op jit(solution)/shard_map/ppermute | solution.py:226
  103.9 9.8 %collective-permute-start.6 = (bf16[256,1152]{1,0:T(8,128)(2,1)}, bf16[256,1152]{1,0:T(8,128)(2,1)S(1)}, u32[]{:S(2)}, u32[]{:S(2)}) collective-permute-start(bf16[256,1152]{1,0:T(8,128)(2,1)} %collective-permute-done.1.refs_2_), channel_id=1, source_target_pairs={{0,4},{4,0},{1,5},{5,1},{2,6},{6,2},{3,7},{7,3},{8,12},{12,8},{9,1... | collective-permute-start | bytes 1769480 | tf_op jit(solution)/shard_map/ppermute | solution.py:226
  103.9 9.8 %collective-permute-start.7 = (bf16[256,1152]{1,0:T(8,128)(2,1)S(1)}, bf16[256,1152]{1,0:T(8,128)(2,1)S(1)}, u32[]{:S(2)}, u32[]{:S(2)}) collective-permute-start(bf16[256,1152]{1,0:T(8,128)(2,1)S(1)} %collective-permute-done.2.refs_3_), channel_id=1, source_target_pairs={{0,4},{4,0},{1,5},{5,1},{2,6},{6,2},{3,7},{7,3},{8,12},{12,8},{9,1... | collective-permute-start | bytes 1769480 | tf_op jit(solution)/shard_map/ppermute | solution.py:226
  104.4 9.3 %collective-permute-start.8 = (bf16[256,1152]{1,0:T(8,128)(2,1)S(1)}, bf16[256,1152]{1,0:T(8,128)(2,1)S(1)}, u32[]{:S(2)}, u32[]{:S(2)}) collective-permute-start(bf16[256,1152]{1,0:T(8,128)(2,1)S(1)} %collective-permute-done.3.refs_4_), channel_id=1, source_target_pairs={{0,4},{4,0},{1,5},{5,1},{2,6},{6,2},{3,7},{7,3},{8,12},{12,8},{9,1... | collective-permute-start | bytes 1769480 | tf_op jit(solution)/shard_map/ppermute | solution.py:226
  116.8 1.4 %collective-permute-start.9 = (f32[2,1024]{1,0:T(2,128)S(1)}, f32[2,1024]{1,0:T(2,128)S(1)}, u32[]{:S(2)}, u32[]{:S(2)}) collective-permute-start(f32[2,1024]{1,0:T(2,128)S(1)} %pad_maximum_fusion.1), channel_id=1, source_target_pairs={{0,4},{4,0},{1,5},{5,1},{2,6},{6,2},{3,7},{7,3},{8,12},{12,8},{9,1... | collective-permute-start | bytes 24584 | tf_op jit(solution)/shard_map/ppermute | solution.py:226

commit v5 on v4

--- a/solution.py
+++ b/solution.py
@@ -12,7 +12,6 @@
 SLOTS = 16
 HALF = 8
 NO_RANK = 1 << 20
-STEPS = ((0, 1), (0, -1), (1, 0), (-1, 0))
 TORUS = ("z", "y", "x")
 ALL = ("z", "y", "core", "x")
 MIB = 2**20
@@ -31,7 +30,7 @@
     return jnp.where(which < 4, weight, 0).astype(jnp.float32).astype(jnp.bfloat16)
 
 
-def pack_kernel(group_ref, emb_ref, labels_ref, rows_ref, home_ref, slot_ref):
+def pack_kernel(place_ref, emb_ref, labels_ref, rows_ref, home_ref, slot_ref):
     docs, features = emb_ref.shape
     wide = emb_ref[...].astype(jnp.float32)
     squares = jnp.sum(wide * wide, axis=1, keepdims=True) + 1e-06
@@ -57,9 +56,9 @@
         jnp.where(which == 1, (rank >> 8) & 255, jnp.where(which == 2, rank >> 16, 1)),
     )
     digits = jnp.where(which < 4, digits, 0).astype(jnp.float32).astype(jnp.bfloat16)
-    group = group_ref[0]
-    dy = jnp.where(group == 2, -1, jnp.where(group == 3, 1, 0))
-    dx = jnp.where(group == 0, -1, jnp.where(group == 1, 1, 0))
+    core, upper = place_ref[0], place_ref[1]
+    side = jnp.where(upper == 0, -1, 1)
+    dy, dx = side * core, side * (1 - core)
     via = (z * NY + ((y + dy) & 3)) * NX + ((x + dx) & 3)
     at = jnp.where(slot < HALF, home * HALF + slot, via * HALF + slot - HALF)
     pick = lax.broadcasted_iota(jnp.int32, (CHIPS * HALF, docs), 0) == at
@@ -68,7 +67,7 @@
     rows_ref[:, features:] = dot(pick, digits, ((1,), (1,))).astype(jnp.bfloat16)
 
 
-def pack(group, embeddings, labels):
+def pack(place, embeddings, labels):
     docs, features = embeddings.shape
     vmem = pl.BlockSpec(memory_space=pltpu.VMEM)
     return pl.pallas_call(
@@ -82,7 +81,7 @@
         out_specs=(vmem,) * 3,
         compiler_params=pltpu.CompilerParams(vmem_limit_bytes=24 * MIB),
         name="pack",
-    )(group, embeddings, labels)
+    )(place, embeddings, labels)
 
 
 def compare_kernel(plan, sets, *refs):
@@ -209,17 +208,17 @@
     )(back, home, slot)
 
 
-def to_home(step):
-    dy, dx = step
+def to_home(a, step):
     place = lambda z, y, c, x: ((z * NY + y) * NC + c) * NX + x
-    return [
-        (place(z, y, c, x), place(z, (y + dy) % NY, c, (x + dx) % NX))
+    pairs = [
+        (place(z, y, c, x), place(z, (y + step * c) % NY, c, (x + step * (1 - c)) % NX))
         for z in range(NZ)
         for y in range(NY)
         for c in range(NC)
         for x in range(NX)
         if (x + y + z) % 2
     ]
+    return lax.ppermute(a, ALL, pairs)
 
 
 def other_core(a):
@@ -232,16 +231,14 @@
 
 def per_device(embeddings, cluster, doc_rank):
     docs, features = embeddings.shape
-    group = (lax.axis_index("z") // 2).reshape(1)
-    core = lax.axis_index("core").reshape(1)
-    rows, home, slot = pack(group, embeddings, jnp.stack([cluster, doc_rank]))
+    place = jnp.stack([lax.axis_index("core"), lax.axis_index("z") // (NZ // 2)]).astype(jnp.int32)
+    core = place[:1]
+    rows, home, slot = pack(place, embeddings, jnp.stack([cluster, doc_rank]))
     wide = features + 128
     near = exchange(rows.reshape(CHIPS, HALF, wide)).reshape(CHIPS * HALF, wide)
     part = near.shape[0] // 4
-    far = [
-        lax.ppermute(near[i * part : (i + 1) * part], ALL, to_home(step))
-        for i, step in enumerate(STEPS)
-    ]
+    quarter = [near[i * part : (i + 1) * part] for i in range(4)]
+    far = [[to_home(quarter[i], 1), to_home(quarter[i + 2], -1)] for i in (0, 1)]
     near_there = other_core(near)
     plan = (
         ((0, 0), (0, 0), False),
@@ -250,32 +247,56 @@
         ((0, 0), (1, 1), True),
         ((0, None), (1, None), True),
     )
-    best_near, best_near_there = compare(
-        core, [([near], None, True), ([near_there], None, True)], plan, "compare_near"
-    )
-    far, best_near, best_near_there = lax.optimization_barrier((far, best_near, best_near_there))
-    far_there = [other_core(a) for a in far]
+    best = compare(core, [([near], None, True), ([near_there], None, True)], plan, "compare_near")
+    far[0], best = lax.optimization_barrier((far[0], best))
+    far_there = [[other_core(a) for a in far[0]]]
     plan = (
         ((0, 0), (0, 0), False),
-        ((0, 1), (0, 1), False),
-        ((0, 0), (0, 1), True),
-        *(((0, q), (k, b), True) for q in (0, 1) for k in (1, 2) for b in (0, 1)),
-    )
-    best_far, best_near, best_near_there = compare(
+        *(((0, 0), (k, b), True) for k in (1, 2) for b in (0, 1)),
+    )
+    best_first, *best = compare(
         core,
-        [(far, None, True), ([near], best_near, True), ([near_there], best_near_there, True)],
+        [(far[0], None, True), ([near], best[0], True), ([near_there], best[1], True)],
         plan,
-        "compare_far",
-    )
-    plan = (((0, 0), (1, 1), True), ((0, None), (1, None), True))
-    best_far, best_far_there = compare(
-        core, [(far, best_far, True), (far_there, None, True)], plan, "compare_cores"
-    )
-    mine = jnp.concatenate([best_near, best_far], axis=0)
-    theirs = other_core(jnp.concatenate([best_near_there, best_far_there], axis=0))
-    result = jnp.maximum(mine, theirs).reshape(2, CHIPS, HALF)
-    result = jnp.concatenate([result[0], result[1]], axis=1)
-    return unpack(exchange(result), home, slot).reshape(docs)
+        "compare_first",
+    )
+    far[1], best_first, best = lax.optimization_barrier((far[1], best_first, best))
+    far_there.append([other_core(a) for a in far[1]])
+    plan = (
+        ((0, 0), (0, 0), False),
+        *(((0, 0), (k, b), True) for k, b in ((1, 0), (2, 0), (3, 0), (3, 1), (4, 0), (4, 1))),
+    )
+    best_second, best_first, best_first_there, *best = compare(
+        core,
+        [
+            (far[1], None, True),
+            (far[0], best_first, True),
+            (far_there[0], None, True),
+            ([near], best[0], True),
+            ([near_there], best[1], True),
+        ],
+        plan,
+        "compare_second",
+    )
+    theirs = other_core(jnp.concatenate([best[1], best_first_there], axis=1))
+    best_first, best_second = compare(
+        core,
+        [
+            (far[0], best_first, True),
+            (far[1], best_second, True),
+            (far_there[0], None, False),
+            (far_there[1], None, False),
+        ],
+        (((0, 0), (2, 0), False), ((1, 0), (3, 0), False)),
+        "compare_cores",
+    )
+    count = near.shape[0]
+    best_near = jnp.maximum(best[0], theirs[:, :count])
+    best_first = jnp.maximum(best_first, theirs[:, count:])
+    best_far = [b[:, i : i + part] for i in (0, part) for b in (best_first, best_second)]
+    best_far = jnp.concatenate(best_far, axis=1)
+    result = [b.reshape(CHIPS, HALF) for b in (best_near, best_far)]
+    return unpack(exchange(jnp.concatenate(result, axis=1)), home, slot).reshape(docs)
 
 
 def solution(mesh):

time: 139 us -> 128 us (0.921)
  waiting for transfers between devices: 12.8 us -> 5.28 us
  Pallas kernels: 21.2 us -> 18.1 us
    ppermute x4, waiting for transfers between devices: 12 us -> 5.26 us  [to_home(): return lax.ppermute(a, ALL, pairs)]
    pallas_call x3 -> x4, Pallas kernels: 17.5 us -> 13.9 us  [compare(): pl.pallas_call(functools.partial(compare_kernel, plan, [(len(arrays), bes...]
  transfers between devices with their start and end apart: 10 -> 10, of which waited for: 5 -> 4; matrix products, arithmetic and copies ran while one was open for 1% -> 0% of each run, Pallas kernels for 10% -> 11%
where the time goes in v5:
time: 128 us
  blocking collectives  90.1 us (70%)
  Pallas kernels  18.1 us (14%)
  starting transfers between devices  11.9 us (9%)
  waiting for transfers between devices  5.28 us (4%)
  local copies, waits for them, and re-layouts  1.58 us (1%)
    all_to_all x2, blocking collectives, exchange(): return lax.all_to_all(a, TORUS, split_axis=0, concat_axis=0, tiled=True)  90.1 us
    pallas_call x4, Pallas kernels, compare(): pl.pallas_call(functools.partial(compare_kernel, plan, [(len(arrays), bes...  13.9 us
    ppermute x6, starting transfers between devices, other_core(): return lax.ppermute(a, 'core', [(0, 1), (1, 0)])  6.77 us
    ppermute x4, waiting for transfers between devices, to_home(): return lax.ppermute(a, ALL, pairs)  5.26 us
    ppermute x4, starting transfers between devices, to_home(): return lax.ppermute(a, ALL, pairs)  5.17 us
  transfers between devices with their start and end apart: 10, of which 4 were waited for; matrix products, arithmetic and copies ran while one was open for 0% of the time, Pallas kernels for 11%

profile of v5, /device:TPU:1, one launch (start us, length us, event | category | flops | bytes accessed | tf_op | source)
XLA Modules:
  0.0 128.0 jit_solution(1905393355060722846)
XLA Ops:
  0.0 0.1 pad_add_fusion.1.place_ref
  0.1 0.7 pad_add_fusion.labels_ref
  0.8 1.2 copy-done
  2.0 2.5 %pack.1 = (bf16[1024,1152]{1,0:T(8,128)(2,1)S(1)}, s32[1,512]{1,0:T(1,128)S(1)}, s32[1,512]{1,0:T(1,128)S(1)}) custom-call(s32[2]{0:T(128)S(1)} %pad_add_fusion.1.place_ref, bf16[512,1024]{1,0:T(8,128)(2,1)S(1)} %copy-done, s32[2,512]{1,0:T(2,128)S(1)} %pad_add_fusion.labels_ref), custom_call_target="tpu_custom_call" | custom-call | tf_op jit(solution)/shard_map/pack/pallas_call | solution.py:73
  4.5 71.0 %all_to_all.16 = bf16[128,8,1152]{2,1,0:T(8,128)(2,1)S(1)} all-to-all(bf16[128,8,1152]{2,1,0:T(8,128)(2,1)S(1)} %bitcast.23), channel_id=1, replica_groups=mesh['z'=8,'y'=4,'core'=2,'x'=4] {'z','y','x'}, dimensions={0} | all-to-all | bytes 4718592 | tf_op jit(solution)/shard_map/all_to_all | solution.py:229
  75.5 4.4 %collective-permute-start.4 = (bf16[1024,1152]{1,0:T(8,128)(2,1)S(1)}, bf16[1024,1152]{1,0:T(8,128)(2,1)S(1)}, u32[]{:S(2)}, u32[]{:S(2)}) collective-permute-start(bf16[1024,1152]{1,0:T(8,128)(2,1)S(1)} %bitcast.19), channel_id=1, source_target_pairs={{0,4},{4,0},{1,5},{5,1},{2,6},{6,2},{3,7},{7,3},{8,12},{12,8},{9,1... | collective-permute-start | bytes 7077896 | tf_op jit(solution)/shard_map/ppermute | solution.py:225
  79.9 0.2 slice_bitcast_fusion.2
  80.1 1.3 %collective-permute-start.2 = (bf16[256,1152]{1,0:T(8,128)(2,1)S(1)}, bf16[256,1152]{1,0:T(8,128)(2,1)S(1)}, u32[]{:S(2)}, u32[]{:S(2)}) collective-permute-start(bf16[256,1152]{1,0:T(8,128)(2,1)S(1)} %get-tuple-element.55), channel_id=1, source_target_pairs={{1,2},{3,0},{5,13},{7,15},{8,9},{10,11},{12,20},{14,22},{17,18},{1... | collective-permute-start | bytes 1769480 | tf_op jit(solution)/shard_map/ppermute | solution.py:221
  81.4 1.3 %collective-permute-start.3 = (bf16[256,1152]{1,0:T(8,128)(2,1)S(1)}, bf16[256,1152]{1,0:T(8,128)(2,1)S(1)}, u32[]{:S(2)}, u32[]{:S(2)}) collective-permute-start(bf16[256,1152]{1,0:T(8,128)(2,1)S(1)} %get-tuple-element.54), channel_id=1, source_target_pairs={{1,0},{3,2},{5,29},{7,31},{8,11},{10,9},{12,4},{14,6},{17,16},{19,... | collective-permute-start | bytes 1769480 | tf_op jit(solution)/shard_map/ppermute | solution.py:221
  82.7 1.3 %collective-permute-start = (bf16[256,1152]{1,0:T(8,128)(2,1)S(1)}, bf16[256,1152]{1,0:T(8,128)(2,1)S(1)}, u32[]{:S(2)}, u32[]{:S(2)}) collective-permute-start(bf16[256,1152]{1,0:T(8,128)(2,1)S(1)} %get-tuple-element.56), channel_id=1, source_target_pairs={{1,2},{3,0},{5,13},{7,15},{8,9},{10,11},{12,20},{14,22},{17,18},{1... | collective-permute-start | bytes 1769480 | tf_op jit(solution)/shard_map/ppermute | solution.py:221
  84.0 1.3 %collective-permute-start.1 = (bf16[256,1152]{1,0:T(8,128)(2,1)S(1)}, bf16[256,1152]{1,0:T(8,128)(2,1)S(1)}, u32[]{:S(2)}, u32[]{:S(2)}) collective-permute-start(bf16[256,1152]{1,0:T(8,128)(2,1)S(1)} %get-tuple-element.53), channel_id=1, source_target_pairs={{1,0},{3,2},{5,29},{7,31},{8,11},{10,9},{12,4},{14,6},{17,16},{19,... | collective-permute-start | bytes 1769480 | tf_op jit(solution)/shard_map/ppermute | solution.py:221
  85.3 0.0 collective-permute-done.4.refs_2_.refs_4_.refs_8_
  85.3 3.5 %compare_near.1 = (f32[1,1024]{1,0:T(1,128)S(1)}, f32[1,1024]{1,0:T(1,128)S(1)}) custom-call(s32[1]{0:T(128)} %bitcast.refs_0_, bf16[1024,1152]{1,0:T(8,128)(2,1)S(1)} %bitcast.20, bf16[1024,1152]{1,0:T(8,128)(2,1)S(1)} %collective-permute-done.4.refs_2_.refs_4_.refs_8_), custom_call_target="tpu_custom_call" | custom-call | flops 3019898880 | bytes 4718592 | tf_op jit(solution)/shard_map/compare_near/pallas_call | solution.py:166
  88.8 3.4 %collective-permute-done.2.refs_1_.refs_3_ = bf16[256,1152]{1,0:T(8,128)(2,1)S(1)} collective-permute-done((bf16[256,1152]{1,0:T(8,128)(2,1)S(1)}, bf16[256,1152]{1,0:T(8,128)(2,1)S(1)}, u32[]{:S(2)}, u32[]{:S(2)}) %collective-permute-start.2) | collective-permute-done | bytes 589856 | tf_op jit(solution)/shard_map/ppermute | solution.py:221
  92.2 0.1 collective-permute-done.3.refs_2_.refs_4_
  92.3 0.9 collective-permute-start.5
  93.2 0.0 collective-permute-start.6
  93.2 3.7 %compare_first.1 = (f32[1,512]{1,0:T(1,128)S(1)}, f32[1,1024]{1,0:T(1,128)S(1)}, f32[1,1024]{1,0:T(1,128)S(1)}) custom-call(s32[1]{0:T(128)} %bitcast.refs_0_, bf16[256,1152]{1,0:T(8,128)(2,1)S(1)} %collective-permute-done.2.refs_1_.refs_3_, bf16[256,1152]{1,0:T(8,128)(2,1)S(1)} %collective-permute-done.3.refs_2_.refs_4_, bf16[1024,1152]{1,0:T(8,128)(2,1)S(1)} %bitcast.21, ...), custom_call_target="tpu_custom_call" | custom-call | flops 3019898880 | bytes 5898240 | tf_op jit(solution)/shard_map/compare_first/pallas_call | solution.py:166
  96.9 1.7 %collective-permute-done.refs_1_.refs_3_ = bf16[256,1152]{1,0:T(8,128)(2,1)S(1)} collective-permute-done((bf16[256,1152]{1,0:T(8,128)(2,1)S(1)}, bf16[256,1152]{1,0:T(8,128)(2,1)S(1)}, u32[]{:S(2)}, u32[]{:S(2)}) %collective-permute-start) | collective-permute-done | bytes 589856 | tf_op jit(solution)/shard_map/ppermute | solution.py:221
  98.5 0.1 collective-permute-done.1.refs_2_.refs_4_
  98.6 0.9 collective-permute-start.8
  99.5 0.0 collective-permute-start.9
  99.5 0.0 collective-permute-done.5.refs_5_
  99.5 0.0 collective-permute-done.6.refs_6_
  99.5 5.0 %compare_second.1 = (f32[1,512]{1,0:T(1,128)S(1)}, f32[1,512]{1,0:T(1,128)S(1)}, f32[1,512]{1,0:T(1,128)S(1)}, f32[1,1024]{1,0:T(1,128)S(1)}, f32[1,1024]{1,0:T(1,128)S(1)}) custom-call(s32[1]{0:T(128)} %bitcast.refs_0_, bf16[256,1152]{1,0:T(8,128)(2,1)S(1)} %collective-permute-done.refs_1_.refs_3_, ...), custom_call_target="tpu_custom_call" | custom-call | flops 4227858432 | bytes 8257536 | tf_op jit(solution)/shard_map/compare_second/pallas_call | solution.py:166
  104.5 0.6 collective-permute-start.7
  105.1 1.7 %compare_cores.1 = (f32[1,512]{1,0:T(1,128)S(1)}, f32[1,512]{1,0:T(1,128)S(1)}) custom-call(s32[1]{0:T(128)} %bitcast.refs_0_, bf16[256,1152]{1,0:T(8,128)(2,1)S(1)} %collective-permute-done.2.refs_1_.refs_3_, bf16[256,1152]{1,0:T(8,128)(2,1)S(1)} %collective-permute-done.3.refs_2_.refs_4_, bf16[256,1152]{1,0:T(8,128)(2,1)S(1)} %collective-permute-done.refs_1_.refs_3_, ...), custom_call_target="tpu_custom_call" | custom-call | flops 1207959552 | bytes 4718592 | tf_op jit(solution)/shard_map/compare_cores/pallas_call | solution.py:166
  106.9 0.1 reshape.24
  107.0 0.1 reshape.23
  107.1 0.1 pad_maximum_fusion
  107.2 19.1 %all_to_all.17 = f32[128,1,16]{2,1,0:T(1,128)} all-to-all(f32[128,1,16]{2,1,0:T(1,128)S(1)} %bitcast.24), channel_id=1, replica_groups=mesh['z'=8,'y'=4,'core'=2,'x'=4] {'z','y','x'}, dimensions={0} | all-to-all | bytes 16384 | tf_op jit(solution)/shard_map/all_to_all | solution.py:229
  126.3 1.7 %unpack.1 = f32[1,512]{1,0:T(1,128)} custom-call(f32[128,16]{1,0:T(8,128)} %bitcast.25, s32[1,512]{1,0:T(1,128)} %copy-done.1, s32[1,512]{1,0:T(1,128)} %copy-done.2), custom_call_target="tpu_custom_call" | custom-call | tf_op jit(solution)/shard_map/unpack/pallas_call | solution.py:202
  (13 shorter events, 0.1 us)
Async XLA Ops:
  0.8 1.2 copy-start
  4.5 71.0 %copy-start.1 = (s32[1,512]{1,0:T(1,128)}, s32[1,512]{1,0:T(1,128)S(1)}, u32[]{:S(2)}) copy-start(s32[1,512]{1,0:T(1,128)S(1)} %get-tuple-element.51.home_ref) | copy-start | bytes 6148
  4.5 71.0 %copy-start.2 = (s32[1,512]{1,0:T(1,128)}, s32[1,512]{1,0:T(1,128)S(1)}, u32[]{:S(2)}) copy-start(s32[1,512]{1,0:T(1,128)S(1)} %get-tuple-element.52.slot_ref) | copy-start | bytes 6148
  75.5 9.8 %collective-permute-start.4 = (bf16[1024,1152]{1,0:T(8,128)(2,1)S(1)}, bf16[1024,1152]{1,0:T(8,128)(2,1)S(1)}, u32[]{:S(2)}, u32[]{:S(2)}) collective-permute-start(bf16[1024,1152]{1,0:T(8,128)(2,1)S(1)} %bitcast.19), channel_id=1, source_target_pairs={{0,4},{4,0},{1,5},{5,1},{2,6},{6,2},{3,7},{7,3},{8,12},{12,8},{9,1... | collective-permute-start | bytes 7077896 | tf_op jit(solution)/shard_map/ppermute | solution.py:225
  80.1 12.1 %collective-permute-start.2 = (bf16[256,1152]{1,0:T(8,128)(2,1)S(1)}, bf16[256,1152]{1,0:T(8,128)(2,1)S(1)}, u32[]{:S(2)}, u32[]{:S(2)}) collective-permute-start(bf16[256,1152]{1,0:T(8,128)(2,1)S(1)} %get-tuple-element.55), channel_id=1, source_target_pairs={{1,2},{3,0},{5,13},{7,15},{8,9},{10,11},{12,20},{14,22},{17,18},{1... | collective-permute-start | bytes 1769480 | tf_op jit(solution)/shard_map/ppermute | solution.py:221
  81.4 10.9 %collective-permute-start.3 = (bf16[256,1152]{1,0:T(8,128)(2,1)S(1)}, bf16[256,1152]{1,0:T(8,128)(2,1)S(1)}, u32[]{:S(2)}, u32[]{:S(2)}) collective-permute-start(bf16[256,1152]{1,0:T(8,128)(2,1)S(1)} %get-tuple-element.54), channel_id=1, source_target_pairs={{1,0},{3,2},{5,29},{7,31},{8,11},{10,9},{12,4},{14,6},{17,16},{19,... | collective-permute-start | bytes 1769480 | tf_op jit(solution)/shard_map/ppermute | solution.py:221
  82.7 15.9 %collective-permute-start = (bf16[256,1152]{1,0:T(8,128)(2,1)S(1)}, bf16[256,1152]{1,0:T(8,128)(2,1)S(1)}, u32[]{:S(2)}, u32[]{:S(2)}) collective-permute-start(bf16[256,1152]{1,0:T(8,128)(2,1)S(1)} %get-tuple-element.56), channel_id=1, source_target_pairs={{1,2},{3,0},{5,13},{7,15},{8,9},{10,11},{12,20},{14,22},{17,18},{1... | collective-permute-start | bytes 1769480 | tf_op jit(solution)/shard_map/ppermute | solution.py:221
  84.0 14.6 %collective-permute-start.1 = (bf16[256,1152]{1,0:T(8,128)(2,1)S(1)}, bf16[256,1152]{1,0:T(8,128)(2,1)S(1)}, u32[]{:S(2)}, u32[]{:S(2)}) collective-permute-start(bf16[256,1152]{1,0:T(8,128)(2,1)S(1)} %get-tuple-element.53), channel_id=1, source_target_pairs={{1,0},{3,2},{5,29},{7,31},{8,11},{10,9},{12,4},{14,6},{17,16},{19,... | collective-permute-start | bytes 1769480 | tf_op jit(solution)/shard_map/ppermute | solution.py:221
  92.3 7.2 %collective-permute-start.5 = (bf16[256,1152]{1,0:T(8,128)(2,1)S(1)}, bf16[256,1152]{1,0:T(8,128)(2,1)S(1)}, u32[]{:S(2)}, u32[]{:S(2)}) collective-permute-start(bf16[256,1152]{1,0:T(8,128)(2,1)S(1)} %collective-permute-done.2.refs_1_.refs_3_), channel_id=1, source_target_pairs={{0,4},{4,0},{1,5},{5,1},{2,6},{6,2},{3,7},{7,3},{8,12},{12,8},{9,1... | collective-permute-start | bytes 1769480 | tf_op jit(solution)/shard_map/ppermute | solution.py:225
  93.2 6.3 %collective-permute-start.6 = (bf16[256,1152]{1,0:T(8,128)(2,1)S(1)}, bf16[256,1152]{1,0:T(8,128)(2,1)S(1)}, u32[]{:S(2)}, u32[]{:S(2)}) collective-permute-start(bf16[256,1152]{1,0:T(8,128)(2,1)S(1)} %collective-permute-done.3.refs_2_.refs_4_), channel_id=1, source_target_pairs={{0,4},{4,0},{1,5},{5,1},{2,6},{6,2},{3,7},{7,3},{8,12},{12,8},{9,1... | collective-permute-start | bytes 1769480 | tf_op jit(solution)/shard_map/ppermute | solution.py:225
  98.6 6.5 %collective-permute-start.8 = (bf16[256,1152]{1,0:T(8,128)(2,1)S(1)}, bf16[256,1152]{1,0:T(8,128)(2,1)S(1)}, u32[]{:S(2)}, u32[]{:S(2)}) collective-permute-start(bf16[256,1152]{1,0:T(8,128)(2,1)S(1)} %collective-permute-done.refs_1_.refs_3_), channel_id=1, source_target_pairs={{0,4},{4,0},{1,5},{5,1},{2,6},{6,2},{3,7},{7,3},{8,12},{12,8},{9,1... | collective-permute-start | bytes 1769480 | tf_op jit(solution)/shard_map/ppermute | solution.py:225
  99.5 5.6 %collective-permute-start.9 = (bf16[256,1152]{1,0:T(8,128)(2,1)S(1)}, bf16[256,1152]{1,0:T(8,128)(2,1)S(1)}, u32[]{:S(2)}, u32[]{:S(2)}) collective-permute-start(bf16[256,1152]{1,0:T(8,128)(2,1)S(1)} %collective-permute-done.1.refs_2_.refs_4_), channel_id=1, source_target_pairs={{0,4},{4,0},{1,5},{5,1},{2,6},{6,2},{3,7},{7,3},{8,12},{12,8},{9,1... | collective-permute-start | bytes 1769480 | tf_op jit(solution)/shard_map/ppermute | solution.py:225
  104.5 2.3 %collective-permute-start.7 = (f32[1,1536]{1,0:T(1,128)S(1)}, f32[1,1536]{1,0:T(1,128)S(1)}, u32[]{:S(2)}, u32[]{:S(2)}) collective-permute-start(f32[1,1536]{1,0:T(1,128)S(1)} %pad_maximum_fusion.1), channel_id=1, source_target_pairs={{0,4},{4,0},{1,5},{5,1},{2,6},{6,2},{3,7},{7,3},{8,12},{12,8},{9,1... | collective-permute-start | bytes 18440 | tf_op jit(solution)/shard_map/ppermute | solution.py:225

commit v6 on v5

--- a/solution.py
+++ b/solution.py
@@ -238,7 +238,7 @@
     near = exchange(rows.reshape(CHIPS, HALF, wide)).reshape(CHIPS * HALF, wide)
     part = near.shape[0] // 4
     quarter = [near[i * part : (i + 1) * part] for i in range(4)]
-    far = [[to_home(quarter[i], 1), to_home(quarter[i + 2], -1)] for i in (0, 1)]
+    far = [[to_home(quarter[0], 1), to_home(quarter[2], -1)]]
     near_there = other_core(near)
     plan = (
         ((0, 0), (0, 0), False),
@@ -248,6 +248,8 @@
         ((0, None), (1, None), True),
     )
     best = compare(core, [([near], None, True), ([near_there], None, True)], plan, "compare_near")
+    later, best = lax.optimization_barrier(((quarter[1], quarter[3]), best))
+    far.append([to_home(later[0], 1), to_home(later[1], -1)])
     far[0], best = lax.optimization_barrier((far[0], best))
     far_there = [[other_core(a) for a in far[0]]]
     plan = (

time: 128 us -> 130 us (1.016)
    ppermute x6, waiting for transfers between devices: 0.02 us -> 1.39 us  [other_core(): return lax.ppermute(a, 'core', [(0, 1), (1, 0)])]
  transfers between devices with their start and end apart: 10 -> 10, of which waited for: 4 -> 5; matrix products, arithmetic and copies ran while one was open for 0% -> 0% of each run, Pallas kernels for 11% -> 11%
where the time goes in v6:
time: 130 us
  blocking collectives  90.1 us (69%)
  Pallas kernels  18.1 us (14%)
  starting transfers between devices  12.3 us (9%)
  waiting for transfers between devices  6.47 us (5%)
  local copies, waits for them, and re-layouts  1.58 us (1%)
    all_to_all x2, blocking collectives, exchange(): return lax.all_to_all(a, TORUS, split_axis=0, concat_axis=0, tiled=True)  90.1 us
    pallas_call x4, Pallas kernels, compare(): pl.pallas_call(functools.partial(compare_kernel, plan, [(len(arrays), bes...  13.9 us
    ppermute x6, starting transfers between devices, other_core(): return lax.ppermute(a, 'core', [(0, 1), (1, 0)])  7.14 us
    ppermute x4, starting transfers between devices, to_home(): return lax.ppermute(a, ALL, pairs)  5.17 us
    ppermute x4, waiting for transfers between devices, to_home(): return lax.ppermute(a, ALL, pairs)  5.08 us
  transfers between devices with their start and end apart: 10, of which 5 were waited for; matrix products, arithmetic and copies ran while one was open for 0% of the time, Pallas kernels for 11%

profile of v6, /device:TPU:1, one launch (start us, length us, event | category | flops | bytes accessed | tf_op | source)
XLA Modules:
  0.0 129.6 jit_solution(12199533793775886365)
XLA Ops:
  0.0 0.1 pad_add_fusion.1.place_ref
  0.1 0.7 pad_add_fusion.labels_ref
  0.8 1.2 copy-done
  2.0 2.5 %pack.1 = (bf16[1024,1152]{1,0:T(8,128)(2,1)S(1)}, s32[1,512]{1,0:T(1,128)S(1)}, s32[1,512]{1,0:T(1,128)S(1)}) custom-call(s32[2]{0:T(128)S(1)} %pad_add_fusion.1.place_ref, bf16[512,1024]{1,0:T(8,128)(2,1)S(1)} %copy-done, s32[2,512]{1,0:T(2,128)S(1)} %pad_add_fusion.labels_ref), custom_call_target="tpu_custom_call" | custom-call | tf_op jit(solution)/shard_map/pack/pallas_call | solution.py:73
  4.5 71.0 %all_to_all.16 = bf16[128,8,1152]{2,1,0:T(8,128)(2,1)S(1)} all-to-all(bf16[128,8,1152]{2,1,0:T(8,128)(2,1)S(1)} %bitcast.23), channel_id=1, replica_groups=mesh['z'=8,'y'=4,'core'=2,'x'=4] {'z','y','x'}, dimensions={0} | all-to-all | bytes 4718592 | tf_op jit(solution)/shard_map/all_to_all | solution.py:229
  75.5 4.4 %collective-permute-start = (bf16[1024,1152]{1,0:T(8,128)(2,1)S(1)}, bf16[1024,1152]{1,0:T(8,128)(2,1)S(1)}, u32[]{:S(2)}, u32[]{:S(2)}) collective-permute-start(bf16[1024,1152]{1,0:T(8,128)(2,1)S(1)} %bitcast.19), channel_id=1, source_target_pairs={{0,4},{4,0},{1,5},{5,1},{2,6},{6,2},{3,7},{7,3},{8,12},{12,8},{9,1... | collective-permute-start | bytes 7077896 | tf_op jit(solution)/shard_map/ppermute | solution.py:225
  79.9 0.2 slice_bitcast_fusion.2
  80.1 1.3 collective-permute-start.3
  81.4 1.3 collective-permute-start.4
  82.7 1.4 %collective-permute-done.refs_2_.refs_4_.refs_8_ = bf16[1024,1152]{1,0:T(8,128)(2,1)S(1)} collective-permute-done((bf16[1024,1152]{1,0:T(8,128)(2,1)S(1)}, bf16[1024,1152]{1,0:T(8,128)(2,1)S(1)}, u32[]{:S(2)}, u32[]{:S(2)}) %collective-permute-start) | collective-permute-done | bytes 2359328 | tf_op jit(solution)/shard_map/ppermute | solution.py:225
  84.1 3.5 %compare_near.1 = (f32[1,1024]{1,0:T(1,128)S(1)}, f32[1,1024]{1,0:T(1,128)S(1)}) custom-call(s32[1]{0:T(128)} %bitcast.refs_0_, bf16[1024,1152]{1,0:T(8,128)(2,1)S(1)} %bitcast.20, bf16[1024,1152]{1,0:T(8,128)(2,1)S(1)} %collective-permute-done.refs_2_.refs_4_.refs_8_), custom_call_target="tpu_custom_call" | custom-call | flops 3019898880 | bytes 4718592 | tf_op jit(solution)/shard_map/compare_near/pallas_call | solution.py:166
  87.6 1.3 collective-permute-start.1
  88.9 1.3 collective-permute-start.2
  90.2 2.0 %collective-permute-done.3.refs_1_.refs_3_ = bf16[256,1152]{1,0:T(8,128)(2,1)S(1)} collective-permute-done((bf16[256,1152]{1,0:T(8,128)(2,1)S(1)}, bf16[256,1152]{1,0:T(8,128)(2,1)S(1)}, u32[]{:S(2)}, u32[]{:S(2)}) %collective-permute-start.3) | collective-permute-done | bytes 589856 | tf_op jit(solution)/shard_map/ppermute | solution.py:221
  92.2 0.1 collective-permute-done.4.refs_2_.refs_4_
  92.3 0.9 collective-permute-start.5
  93.2 0.0 collective-permute-start.6
  93.2 3.7 %compare_first.1 = (f32[1,512]{1,0:T(1,128)S(1)}, f32[1,1024]{1,0:T(1,128)S(1)}, f32[1,1024]{1,0:T(1,128)S(1)}) custom-call(s32[1]{0:T(128)} %bitcast.refs_0_, bf16[256,1152]{1,0:T(8,128)(2,1)S(1)} %collective-permute-done.3.refs_1_.refs_3_, bf16[256,1152]{1,0:T(8,128)(2,1)S(1)} %collective-permute-done.4.refs_2_.refs_4_, bf16[1024,1152]{1,0:T(8,128)(2,1)S(1)} %bitcast.21, ...), custom_call_target="tpu_custom_call" | custom-call | flops 3019898880 | bytes 5898240 | tf_op jit(solution)/shard_map/compare_first/pallas_call | solution.py:166
  96.9 2.9 %collective-permute-done.1.refs_1_.refs_3_ = bf16[256,1152]{1,0:T(8,128)(2,1)S(1)} collective-permute-done((bf16[256,1152]{1,0:T(8,128)(2,1)S(1)}, bf16[256,1152]{1,0:T(8,128)(2,1)S(1)}, u32[]{:S(2)}, u32[]{:S(2)}) %collective-permute-start.1) | collective-permute-done | bytes 589856 | tf_op jit(solution)/shard_map/ppermute | solution.py:221
  99.7 0.1 collective-permute-done.2.refs_2_.refs_4_
  99.8 1.2 collective-permute-start.8
  101.0 0.0 collective-permute-start.9
  101.0 0.0 collective-permute-done.5.refs_5_
  101.1 0.0 collective-permute-done.6.refs_6_
  101.1 5.0 %compare_second.1 = (f32[1,512]{1,0:T(1,128)S(1)}, f32[1,512]{1,0:T(1,128)S(1)}, f32[1,512]{1,0:T(1,128)S(1)}, f32[1,1024]{1,0:T(1,128)S(1)}, f32[1,1024]{1,0:T(1,128)S(1)}) custom-call(s32[1]{0:T(128)} %bitcast.refs_0_, bf16[256,1152]{1,0:T(8,128)(2,1)S(1)} %collective-permute-done.1.refs_1_.refs_3_, ...), custom_call_target="tpu_custom_call" | custom-call | flops 4227858432 | bytes 8257536 | tf_op jit(solution)/shard_map/compare_second/pallas_call | solution.py:166
  106.1 0.6 collective-permute-start.7
  106.7 1.7 %compare_cores.1 = (f32[1,512]{1,0:T(1,128)S(1)}, f32[1,512]{1,0:T(1,128)S(1)}) custom-call(s32[1]{0:T(128)} %bitcast.refs_0_, bf16[256,1152]{1,0:T(8,128)(2,1)S(1)} %collective-permute-done.3.refs_1_.refs_3_, bf16[256,1152]{1,0:T(8,128)(2,1)S(1)} %collective-permute-done.4.refs_2_.refs_4_, bf16[256,1152]{1,0:T(8,128)(2,1)S(1)} %collective-permute-done.1.refs_1_.refs_3_, ...), custom_call_target="tpu_custom_call" | custom-call | flops 1207959552 | bytes 4718592 | tf_op jit(solution)/shard_map/compare_cores/pallas_call | solution.py:166
  108.5 0.1 reshape.24
  108.5 0.1 reshape.23
  108.6 0.1 pad_maximum_fusion
  108.7 19.1 %all_to_all.17 = f32[128,1,16]{2,1,0:T(1,128)} all-to-all(f32[128,1,16]{2,1,0:T(1,128)S(1)} %bitcast.24), channel_id=1, replica_groups=mesh['z'=8,'y'=4,'core'=2,'x'=4] {'z','y','x'}, dimensions={0} | all-to-all | bytes 16384 | tf_op jit(solution)/shard_map/all_to_all | solution.py:229
  127.9 1.7 %unpack.1 = f32[1,512]{1,0:T(1,128)} custom-call(f32[128,16]{1,0:T(8,128)} %bitcast.25, s32[1,512]{1,0:T(1,128)} %copy-done.1, s32[1,512]{1,0:T(1,128)} %copy-done.2), custom_call_target="tpu_custom_call" | custom-call | tf_op jit(solution)/shard_map/unpack/pallas_call | solution.py:202
  (13 shorter events, 0.1 us)
Async XLA Ops:
  0.8 1.2 copy-start
  4.5 71.0 %copy-start.1 = (s32[1,512]{1,0:T(1,128)}, s32[1,512]{1,0:T(1,128)S(1)}, u32[]{:S(2)}) copy-start(s32[1,512]{1,0:T(1,128)S(1)} %get-tuple-element.59.home_ref) | copy-start | bytes 6148
  4.5 71.0 %copy-start.2 = (s32[1,512]{1,0:T(1,128)}, s32[1,512]{1,0:T(1,128)S(1)}, u32[]{:S(2)}) copy-start(s32[1,512]{1,0:T(1,128)S(1)} %get-tuple-element.60.slot_ref) | copy-start | bytes 6148
  75.5 8.6 %collective-permute-start = (bf16[1024,1152]{1,0:T(8,128)(2,1)S(1)}, bf16[1024,1152]{1,0:T(8,128)(2,1)S(1)}, u32[]{:S(2)}, u32[]{:S(2)}) collective-permute-start(bf16[1024,1152]{1,0:T(8,128)(2,1)S(1)} %bitcast.19), channel_id=1, source_target_pairs={{0,4},{4,0},{1,5},{5,1},{2,6},{6,2},{3,7},{7,3},{8,12},{12,8},{9,1... | collective-permute-start | bytes 7077896 | tf_op jit(solution)/shard_map/ppermute | solution.py:225
  80.1 12.1 %collective-permute-start.3 = (bf16[256,1152]{1,0:T(8,128)(2,1)S(1)}, bf16[256,1152]{1,0:T(8,128)(2,1)S(1)}, u32[]{:S(2)}, u32[]{:S(2)}) collective-permute-start(bf16[256,1152]{1,0:T(8,128)(2,1)S(1)} %get-tuple-element.63), channel_id=1, source_target_pairs={{1,2},{3,0},{5,13},{7,15},{8,9},{10,11},{12,20},{14,22},{17,18},{1... | collective-permute-start | bytes 1769480 | tf_op jit(solution)/shard_map/ppermute | solution.py:221
  81.4 10.9 %collective-permute-start.4 = (bf16[256,1152]{1,0:T(8,128)(2,1)S(1)}, bf16[256,1152]{1,0:T(8,128)(2,1)S(1)}, u32[]{:S(2)}, u32[]{:S(2)}) collective-permute-start(bf16[256,1152]{1,0:T(8,128)(2,1)S(1)} %get-tuple-element.62), channel_id=1, source_target_pairs={{1,0},{3,2},{5,29},{7,31},{8,11},{10,9},{12,4},{14,6},{17,16},{19,... | collective-permute-start | bytes 1769480 | tf_op jit(solution)/shard_map/ppermute | solution.py:221
  87.6 12.1 %collective-permute-start.1 = (bf16[256,1152]{1,0:T(8,128)(2,1)S(1)}, bf16[256,1152]{1,0:T(8,128)(2,1)S(1)}, u32[]{:S(2)}, u32[]{:S(2)}) collective-permute-start(bf16[256,1152]{1,0:T(8,128)(2,1)S(1)} %get-tuple-element.36), channel_id=1, source_target_pairs={{1,2},{3,0},{5,13},{7,15},{8,9},{10,11},{12,20},{14,22},{17,18},{1... | collective-permute-start | bytes 1769480 | tf_op jit(solution)/shard_map/ppermute | solution.py:221
  88.9 10.9 %collective-permute-start.2 = (bf16[256,1152]{1,0:T(8,128)(2,1)S(1)}, bf16[256,1152]{1,0:T(8,128)(2,1)S(1)}, u32[]{:S(2)}, u32[]{:S(2)}) collective-permute-start(bf16[256,1152]{1,0:T(8,128)(2,1)S(1)} %get-tuple-element.37), channel_id=1, source_target_pairs={{1,0},{3,2},{5,29},{7,31},{8,11},{10,9},{12,4},{14,6},{17,16},{19,... | collective-permute-start | bytes 1769480 | tf_op jit(solution)/shard_map/ppermute | solution.py:221
  92.3 8.7 %collective-permute-start.5 = (bf16[256,1152]{1,0:T(8,128)(2,1)S(1)}, bf16[256,1152]{1,0:T(8,128)(2,1)S(1)}, u32[]{:S(2)}, u32[]{:S(2)}) collective-permute-start(bf16[256,1152]{1,0:T(8,128)(2,1)S(1)} %collective-permute-done.3.refs_1_.refs_3_), channel_id=1, source_target_pairs={{0,4},{4,0},{1,5},{5,1},{2,6},{6,2},{3,7},{7,3},{8,12},{12,8},{9,1... | collective-permute-start | bytes 1769480 | tf_op jit(solution)/shard_map/ppermute | solution.py:225
  93.2 7.9 %collective-permute-start.6 = (bf16[256,1152]{1,0:T(8,128)(2,1)S(1)}, bf16[256,1152]{1,0:T(8,128)(2,1)S(1)}, u32[]{:S(2)}, u32[]{:S(2)}) collective-permute-start(bf16[256,1152]{1,0:T(8,128)(2,1)S(1)} %collective-permute-done.4.refs_2_.refs_4_), channel_id=1, source_target_pairs={{0,4},{4,0},{1,5},{5,1},{2,6},{6,2},{3,7},{7,3},{8,12},{12,8},{9,1... | collective-permute-start | bytes 1769480 | tf_op jit(solution)/shard_map/ppermute | solution.py:225
  99.8 6.9 %collective-permute-start.8 = (bf16[256,1152]{1,0:T(8,128)(2,1)S(1)}, bf16[256,1152]{1,0:T(8,128)(2,1)S(1)}, u32[]{:S(2)}, u32[]{:S(2)}) collective-permute-start(bf16[256,1152]{1,0:T(8,128)(2,1)S(1)} %collective-permute-done.1.refs_1_.refs_3_), channel_id=1, source_target_pairs={{0,4},{4,0},{1,5},{5,1},{2,6},{6,2},{3,7},{7,3},{8,12},{12,8},{9,1... | collective-permute-start | bytes 1769480 | tf_op jit(solution)/shard_map/ppermute | solution.py:225
  101.0 5.6 %collective-permute-start.9 = (bf16[256,1152]{1,0:T(8,128)(2,1)S(1)}, bf16[256,1152]{1,0:T(8,128)(2,1)S(1)}, u32[]{:S(2)}, u32[]{:S(2)}) collective-permute-start(bf16[256,1152]{1,0:T(8,128)(2,1)S(1)} %collective-permute-done.2.refs_2_.refs_4_), channel_id=1, source_target_pairs={{0,4},{4,0},{1,5},{5,1},{2,6},{6,2},{3,7},{7,3},{8,12},{12,8},{9,1... | collective-permute-start | bytes 1769480 | tf_op jit(solution)/shard_map/ppermute | solution.py:225
  106.1 2.3 %collective-permute-start.7 = (f32[1,1536]{1,0:T(1,128)S(1)}, f32[1,1536]{1,0:T(1,128)S(1)}, u32[]{:S(2)}, u32[]{:S(2)}) collective-permute-start(f32[1,1536]{1,0:T(1,128)S(1)} %pad_maximum_fusion.1), channel_id=1, source_target_pairs={{0,4},{4,0},{1,5},{5,1},{2,6},{6,2},{3,7},{7,3},{8,12},{12,8},{9,1... | collective-permute-start | bytes 18440 | tf_op jit(solution)/shard_map/ppermute | solution.py:225

commit v7 on v5

v7 whole, which is shorter than its diff:
```python
import functools

import jax
import jax.numpy as jnp
from jax import lax
from jax.experimental import pallas as pl
from jax.experimental.pallas import tpu as pltpu
from jax.sharding import Mesh, PartitionSpec as P

NZ, NY, NC, NX = 8, 4, 2, 4
CHIPS = NZ * NY * NX
SLOTS = 16
HALF = 8
NO_RANK = 1 << 20
TORUS = ("z", "y", "x")
ALL = ("z", "y", "core", "x")
MIB = 2**20
TILE = 512


def dot(a, b, dims):
    return lax.dot_general(a, b, (dims, ((), ())), preferred_element_type=jnp.float32)


def pack_kernel(place_ref, emb_ref, labels_ref, rows_ref, ranks_ref, home_ref, slot_ref):
    docs, features = emb_ref.shape
    wide = emb_ref[...].astype(jnp.float32)
    squares = jnp.sum(wide * wide, axis=1, keepdims=True) + 1e-06
    unit = (wide * lax.rsqrt(squares)).astype(jnp.bfloat16)
    clu = labels_ref[0:1, :]
    z, y, xh = clu // 8, (clu // 2) % 4, clu % 2
    x = 2 * xh + (y + z) % 2
    home = (z * NY + y) * NX + x
    on_home = lax.broadcasted_iota(jnp.int32, (CHIPS, docs), 0) == home
    member = on_home.astype(jnp.bfloat16)
    ahead = lax.broadcasted_iota(jnp.int32, (docs, docs), 0) < lax.broadcasted_iota(
        jnp.int32, (docs, docs), 1
    )
    before = dot(member, ahead.astype(jnp.bfloat16), ((1,), (0,)))
    slot = jnp.sum(jnp.where(on_home, before, 0.0), axis=0, keepdims=True).astype(jnp.int32)
    home_ref[...] = home
    slot_ref[...] = slot
    rank = labels_ref[1:2, :]
    in_slot = lax.broadcasted_iota(jnp.int32, (SLOTS, docs), 0) == slot
    digits = (rank & 255, (rank >> 8) & 255, rank >> 16, jnp.ones_like(rank))
    cols = jnp.concatenate(
        [jnp.where(in_slot, d.astype(jnp.float32), 0.0) for d in digits], axis=0
    ).astype(jnp.bfloat16)
    placed = dot(cols, member, ((1,), (1,))).astype(jnp.int32)
    low, mid, high, there = (placed[i * SLOTS : (i + 1) * SLOTS, :] for i in range(4))
    ranks_ref[...] = jnp.where(there > 0, low + 256 * mid + 65536 * high, NO_RANK)
    core, upper = place_ref[0], place_ref[1]
    side = jnp.where(upper == 0, -1, 1)
    dy, dx = side * core, side * (1 - core)
    via = (z * NY + ((y + dy) & 3)) * NX + ((x + dx) & 3)
    at = jnp.where(slot < HALF, home * HALF + slot, via * HALF + slot - HALF)
    pick = lax.broadcasted_iota(jnp.int32, (CHIPS * HALF, docs), 0) == at
    pick = jnp.where(pick, 1.0, 0.0).astype(jnp.bfloat16)
    rows_ref[...] = dot(pick, unit, ((1,), (0,))).astype(jnp.bfloat16)


def pack(place, embeddings, labels):
    docs, features = embeddings.shape
    vmem = pl.BlockSpec(memory_space=pltpu.VMEM)
    return pl.pallas_call(
        pack_kernel,
        out_shape=(
            jax.ShapeDtypeStruct((CHIPS * HALF, features), jnp.bfloat16),
            jax.ShapeDtypeStruct((SLOTS, CHIPS), jnp.int32),
            jax.ShapeDtypeStruct((1, docs), jnp.int32),
            jax.ShapeDtypeStruct((1, docs), jnp.int32),
        ),
        in_specs=[pl.BlockSpec(memory_space=pltpu.SMEM), vmem, vmem],
        out_specs=(vmem,) * 4,
        compiler_params=pltpu.CompilerParams(vmem_limit_bytes=24 * MIB),
        name="pack",
    )(place, embeddings, labels)


def spread_kernel(here_ref, there_ref, *outs):
    outs = list(outs)
    for ref in (here_ref, there_ref):
        ranks = ref[...]
        digits = [ranks & 255, (ranks >> 8) & 255, ranks >> 16]
        digits = jnp.concatenate(digits, axis=0).astype(jnp.float32).astype(jnp.bfloat16)
        for first_slot, skip, count in ((0, 0, 1024), (HALF, 0, 512), (HALF, 32, 512)):
            row = lax.broadcasted_iota(jnp.int32, (count, CHIPS), 0)
            chip = row // HALF if count == 1024 else row // HALF + row // 256 * 32 + skip
            of_chip = lax.broadcasted_iota(jnp.int32, (count, CHIPS), 1) == chip
            found = dot(jnp.where(of_chip, 1.0, 0.0).astype(jnp.bfloat16), digits, ((1,), (1,)))
            column = lax.broadcasted_iota(jnp.int32, found.shape, 1)
            own_slot = lax.broadcasted_iota(jnp.int32, found.shape, 0) % HALF + first_slot
            weight = jnp.where(column < SLOTS, 1.0, jnp.where(column < 2 * SLOTS, 256.0, 65536.0))
            found = jnp.where(column % SLOTS == own_slot, found * weight, 0.0)
            wide = jnp.broadcast_to(jnp.sum(found, axis=1, keepdims=True), (count, 128))
            outs.pop(0)[...] = jnp.transpose(wide)[0:1, :]
            if ref is here_ref:
                outs.pop(0)[...] = wide


def spread(here, there):
    vmem = pl.BlockSpec(memory_space=pltpu.VMEM)
    sizes = (1024, 512, 512)
    shapes = [shape for n in sizes for shape in ((1, n), (n, 128))] + [(1, n) for n in sizes]
    outs = pl.pallas_call(
        spread_kernel,
        out_shape=tuple(jax.ShapeDtypeStruct(shape, jnp.float32) for shape in shapes),
        in_specs=[vmem] * 2,
        out_specs=(vmem,) * len(shapes),
        compiler_params=pltpu.CompilerParams(vmem_limit_bytes=16 * MIB),
        name="spread",
    )(here, there)
    return outs[0:6:2], outs[1:6:2], outs[6:]


def swap_kernel(bit, mine_ref, kept_ref, came_ref, out_ref):
    kept, came = kept_ref[...], came_ref[...]
    mine = mine_ref[0]
    lane_bit = (lax.broadcasted_iota(jnp.int32, kept.shape, 1) // bit) & 1
    down, up = pltpu.roll(came, bit, 1), pltpu.roll(came, kept.shape[1] - bit, 1)
    out_ref[...] = jnp.where(lane_bit == mine, kept, jnp.where(mine == 0, down, up))


def swap(kept, came, bit, mine):
    vmem = pl.BlockSpec(memory_space=pltpu.VMEM)
    return pl.pallas_call(
        functools.partial(swap_kernel, bit),
        out_shape=jax.ShapeDtypeStruct(kept.shape, kept.dtype),
        in_specs=[pl.BlockSpec(memory_space=pltpu.SMEM), vmem, vmem],
        out_specs=vmem,
        name="swap",
    )(mine, kept, came)


def compare_kernel(plan, sets, *refs):
    core_ref, refs = refs[0], list(refs[1:])
    take = lambda flags: [refs.pop(0) if flag else None for flag in flags]
    pieces = [[refs.pop(0) for _ in range(n)] for n, _, _, _ in sets]
    col_rank = take([True for _ in sets])
    row_rank = take([by_row for _, by_row, _, _ in sets])
    start = take([has for _, _, has, _ in sets])
    outs = take([wanted for _, _, _, wanted in sets])
    by_row = take([True for _ in sets])
    by_col = take([True for _ in sets])
    joined = []
    for i, (n, _, _, _) in enumerate(sets):
        whole = pieces[i][0]
        if n > 1:
            whole = refs.pop(0)
            part = pieces[i][0].shape[0]
            for p, piece in enumerate(pieces[i]):
                whole[p * part : (p + 1) * part, :] = piece[...]
        joined.append(whole)
        by_row[i][...] = jnp.full(by_row[i].shape, -1.0, jnp.float32)
        by_col[i][...] = jnp.full(by_col[i].shape, -1.0, jnp.float32)
    core = core_ref[0]
    for (q, qb), (k, kb), both in plan:
        q_at = pl.ds(pl.multiple_of((core if qb is None else qb) * TILE, TILE), TILE)
        k_at = pl.ds(pl.multiple_of((core if kb is None else kb) * TILE, TILE), TILE)
        scores = dot(joined[q][q_at, :], joined[k][k_at, :], ((1,), (1,)))
        q_rank = row_rank[q][q_at, :]
        top = by_row[q][q_at, :]
        k_rank = col_rank[k][:, k_at]
        side = []
        for c in range(TILE // 128):
            cols = slice(c * 128, (c + 1) * 128)
            part = scores[:, cols]
            earlier = k_rank[:, cols] < q_rank
            top = jnp.maximum(top, jnp.where(earlier, part, -1.0))
            if both:
                other = jnp.where(earlier, -1.0, part)
                side.append(jnp.max(other.reshape(TILE // 8, 8, 128), axis=0))
        by_row[q][q_at, :] = top
        if both:
            by_col[k][:, k_at] = jnp.maximum(by_col[k][:, k_at], jnp.concatenate(side, axis=1))
    as_query = {q for (q, _), _, _ in plan}
    as_key = {k for _, (k, _), both in plan if both}
    for i, out in enumerate(outs):
        if out is None:
            continue
        best = None if start[i] is None else start[i][...]
        if i in as_query:
            found = jnp.max(jnp.transpose(by_row[i][...]), axis=0, keepdims=True)
            best = found if best is None else jnp.maximum(best, found)
        if i in as_key:
            found = jnp.max(by_col[i][...], axis=0, keepdims=True)
            best = found if best is None else jnp.maximum(best, found)
        out[...] = best


def compare(core, sets, plan, name):
    wide = sets[0][0][0].shape[1]
    rows = [sum(a.shape[0] for a in s[0]) for s in sets]
    vmem = pl.BlockSpec(memory_space=pltpu.VMEM)
    args = [a for s in sets for a in s[0]] + [s[1] for s in sets]
    args += [s[2] for s in sets if s[2] is not None] + [s[3] for s in sets if s[3] is not None]
    wanted = [n for n, s in zip(rows, sets) if s[4]]
    scratch = [pltpu.VMEM((n, 128), jnp.float32) for n in rows]
    scratch += [pltpu.VMEM((8, n), jnp.float32) for n in rows]
    scratch += [pltpu.VMEM((n, wide), jnp.bfloat16) for n, s in zip(rows, sets) if len(s[0]) > 1]
    return pl.pallas_call(
        functools.partial(
            compare_kernel,
            plan,
            [(len(s[0]), s[2] is not None, s[3] is not None, s[4]) for s in sets],
        ),
        out_shape=tuple(jax.ShapeDtypeStruct((1, n), jnp.float32) for n in wanted),
        in_specs=[pl.BlockSpec(memory_space=pltpu.SMEM)] + [vmem] * len(args),
        out_specs=(vmem,) * len(wanted),
        scratch_shapes=scratch,
        compiler_params=pltpu.CompilerParams(vmem_limit_bytes=24 * MIB),
        cost_estimate=pl.CostEstimate(
            flops=2 * len(plan) * TILE * TILE * wide,
            bytes_accessed=2 * wide * sum(rows),
            transcendentals=0,
        ),
        name=name,
    )(core, *args)


def unpack_kernel(back_ref, home_ref, slot_ref, out_ref):
    docs = home_ref.shape[1]
    on_home = lax.broadcasted_iota(jnp.int32, (CHIPS, docs), 0) == home_ref[...]
    found = lax.dot_general(
        back_ref[...],
        on_home.astype(jnp.float32),
        (((0,), (0,)), ((), ())),
        precision=lax.Precision.HIGHEST,
        preferred_element_type=jnp.float32,
    )
    in_slot = lax.broadcasted_iota(jnp.int32, (SLOTS, docs), 0) == slot_ref[...]
    out_ref[...] = jnp.sum(jnp.where(in_slot, found, 0.0), axis=0, keepdims=True)


def unpack(back, home, slot):
    vmem = pl.BlockSpec(memory_space=pltpu.VMEM)
    return pl.pallas_call(
        unpack_kernel,
        out_shape=jax.ShapeDtypeStruct(home.shape, jnp.float32),
        in_specs=[vmem] * 3,
        out_specs=vmem,
        name="unpack",
    )(back, home, slot)


def to_home(a, step):
    place = lambda z, y, c, x: ((z * NY + y) * NC + c) * NX + x
    pairs = [
        (place(z, y, c, x), place(z, (y + step * c) % NY, c, (x + step * (1 - c)) % NX))
        for z in range(NZ)
        for y in range(NY)
        for c in range(NC)
        for x in range(NX)
        if (x + y + z) % 2
    ]
    return lax.ppermute(a, ALL, pairs)


def other_core(a):
    return lax.ppermute(a, "core", [(0, 1), (1, 0)])


def exchange(a):
    return lax.all_to_all(a, TORUS, split_axis=0, concat_axis=0, tiled=True)


def exchange_small(a):
    span = CHIPS
    for axis, size in zip(TORUS, (NZ, NY, NX)):
        bit = size // 2
        while bit:
            span //= 2
            mine = (lax.axis_index(axis) // bit % 2).astype(jnp.int32).reshape(1)
            came = lax.ppermute(a, axis, [(i, i ^ bit) for i in range(size)])
            a = swap(a, came, span, mine)
            bit //= 2
    return a


def per_device(embeddings, cluster, doc_rank):
    docs, features = embeddings.shape
    place = jnp.stack([lax.axis_index("core"), lax.axis_index("z") // (NZ // 2)]).astype(jnp.int32)
    core = place[:1]
    rows, ranks, home, slot = pack(place, embeddings, jnp.stack([cluster, doc_rank]))
    near = exchange(rows.reshape(CHIPS, HALF, features)).reshape(CHIPS * HALF, features)
    ranks = exchange_small(ranks)
    cols, rank_rows, cols_there = spread(ranks, other_core(ranks))
    near, cols, rank_rows, cols_there = lax.optimization_barrier((near, cols, rank_rows, cols_there))
    near_col, *wave_col = cols
    near_col_there, *wave_col_there = cols_there
    near_row, *wave_row = rank_rows
    part = near.shape[0] // 4
    quarter = [near[i * part : (i + 1) * part] for i in range(4)]
    far = [[to_home(quarter[i], 1), to_home(quarter[i + 2], -1)] for i in (0, 1)]
    near_there = other_core(near)

    def near_sets(best, rows_too):
        return [
            ([near], near_col, near_row if rows_too else None, best[0], True),
            ([near_there], near_col_there, None, best[1], True),
        ]

    plan = (
        ((0, 0), (0, 0), False),
        ((0, 1), (0, 1), False),
        ((0, 0), (0, 1), True),
        ((0, 0), (1, 1), True),
        ((0, None), (1, None), True),
    )
    best = compare(core, near_sets((None, None), True), plan, "compare_near")
    far[0], best = lax.optimization_barrier((far[0], best))
    far_there = [[other_core(a) for a in far[0]]]
    plan = (
        ((0, 0), (0, 0), False),
        *(((0, 0), (k, b), True) for k in (1, 2) for b in (0, 1)),
    )
    best_first, *best = compare(
        core,
        [(far[0], wave_col[0], wave_row[0], None, True), *near_sets(best, False)],
        plan,
        "compare_first",
    )
    far[1], best_first, best = lax.optimization_barrier((far[1], best_first, best))
    far_there.append([other_core(a) for a in far[1]])
    plan = (
        ((0, 0), (0, 0), False),
        *(((0, 0), (k, b), True) for k, b in ((1, 0), (2, 0), (3, 0), (3, 1), (4, 0), (4, 1))),
    )
    best_second, best_first, best_first_there, *best = compare(
        core,
        [
            (far[1], wave_col[1], wave_row[1], None, True),
            (far[0], wave_col[0], None, best_first, True),
            (far_there[0], wave_col_there[0], None, None, True),
            *near_sets(best, False),
        ],
        plan,
        "compare_second",
    )
    theirs = other_core(jnp.concatenate([best[1], best_first_there], axis=1))
    best_first, best_second = compare(
        core,
        [
            (far[0], wave_col[0], wave_row[0], best_first, True),
            (far[1], wave_col[1], wave_row[1], best_second, True),
            (far_there[0], wave_col_there[0], None, None, False),
            (far_there[1], wave_col_there[1], None, None, False),
        ],
        (((0, 0), (2, 0), False), ((1, 0), (3, 0), False)),
        "compare_cores",
    )
    count = near.shape[0]
    best_near = jnp.maximum(best[0], theirs[:, :count])
    best_first = jnp.maximum(best_first, theirs[:, count:])
    best_far = [b[:, i : i + part] for i in (0, part) for b in (best_first, best_second)]
    best_far = jnp.concatenate(best_far, axis=1)
    result = [b.reshape(CHIPS, HALF) for b in (best_near, best_far)]
    return unpack(exchange(jnp.concatenate(result, axis=1)), home, slot).reshape(docs)


def solution(mesh):
    torus = Mesh(mesh.devices.reshape(NZ, NY, NC, NX), ALL)
    placed = (P(ALL, None), P(ALL), P(ALL))
    return jax.shard_map(
        per_device, mesh=torus, in_specs=placed, out_specs=P(ALL), check_vma=False
    )
```

time: 128 us -> 167 us (1.30)
  blocking collectives: 90.1 us -> 19.6 us
  waiting for transfers between devices: 5.28 us -> 64 us
  starting transfers between devices: 11.9 us -> 45.2 us
  Pallas kernels: 18.1 us -> 26.8 us
  local copies, waits for them, and re-layouts: 1.58 us -> 9 us
    all_to_all x2 -> x1, blocking collectives: 90.1 us -> 19.6 us  [exchange(): return lax.all_to_all(a, TORUS, split_axis=0, concat_axis=0, tiled=True)]
    ppermute x0 -> x7, waiting for transfers between devices: none -> 57.5 us  [exchange_small(): came = lax.ppermute(a, axis, [(i, i ^ bit) for i in range(size)])]
    all_to_all x0 -> x1, starting transfers between devices: none -> 16.3 us  [exchange(): return lax.all_to_all(a, TORUS, split_axis=0, concat_axis=0, tiled=True)]
    ppermute x0 -> x7, starting transfers between devices: none -> 12 us  [exchange_small(): came = lax.ppermute(a, axis, [(i, i ^ bit) for i in range(size)])]
    pallas_call x4 -> x12, Pallas kernels: 13.9 us -> 23 us  [the longest x4 12 us: compare(): pl.pallas_call(functools.partial(compare_kernel, plan, [(len(s[0]), s[2]...]
    unnamed x6 -> x26, local copies, waits for them, and re-layouts: 1.23 us -> 8.62 us
    ppermute x6 -> x7, starting transfers between devices: 6.77 us -> 11.5 us  [other_core(): return lax.ppermute(a, 'core', [(0, 1), (1, 0)])]
  transfers between devices with their start and end apart: 10 -> 19, of which waited for: 4 -> 12; matrix products, arithmetic and copies ran while one was open for 0% -> 0% of each run, Pallas kernels for 11% -> 14%
where the time goes in v7:
time: 167 us; the launch traced here: 166 us
  waiting for transfers between devices  64 us (38%)
  starting transfers between devices  45.2 us (27%)
  Pallas kernels  26.8 us (16%)
  blocking collectives  19.6 us (12%)
  local copies, waits for them, and re-layouts  9 us (5%)
    ppermute x7, waiting for transfers between devices, exchange_small(): came = lax.ppermute(a, axis, [(i, i ^ bit) for i in range(size)])  57.5 us
    all_to_all x1, blocking collectives, exchange(): return lax.all_to_all(a, TORUS, split_axis=0, concat_axis=0, tiled=True)  19.6 us
    all_to_all x1, starting transfers between devices, exchange(): return lax.all_to_all(a, TORUS, split_axis=0, concat_axis=0, tiled=True)  16.3 us
    pallas_call x4, Pallas kernels, compare(): pl.pallas_call(functools.partial(compare_kernel, plan, [(len(s[0]), s[2]...  12 us
    ppermute x7, starting transfers between devices, exchange_small(): came = lax.ppermute(a, axis, [(i, i ^ bit) for i in range(size)])  12 us
    ppermute x7, starting transfers between devices, other_core(): return lax.ppermute(a, 'core', [(0, 1), (1, 0)])  11.5 us
    pallas_call x7, Pallas kernels, swap(): pl.pallas_call(functools.partial(swap_kernel, bit), out_shape=jax.ShapeDt...  9.68 us
    unnamed x26, local copies, waits for them, and re-layouts  8.62 us
  transfers between devices with their start and end apart: 19, of which 12 were waited for; matrix products, arithmetic and copies ran while one was open for 0% of the time, Pallas kernels for 14%

profile of v7, /device:TPU:1, one launch (start us, length us, event | category | flops | bytes accessed | tf_op | source)
XLA Modules:
  0.0 165.8 jit_solution(6137886565053050346)
XLA Ops:
  2.0 2.1 %pack.1 = (bf16[1024,1024]{1,0:T(8,128)(2,1)S(1)}, s32[16,128]{1,0:T(8,128)S(1)}, s32[1,512]{1,0:T(1,128)S(1)}, s32[1,512]{1,0:T(1,128)S(1)}) custom-call(s32[2]{0:T(128)S(1)} %pad_add_fusion.1.place_ref, bf16[512,1024]{1,0:T(8,128)(2,1)S(1)} %copy-done.1, s32[2,512]{1,0:T(2,128)S(1)} %pad_add_fusion.labels_ref), custom_call_target="tpu_custom_call" | custom-call | tf_op jit(solution)/shard_map/pack/pallas_call | solution.py:65
  4.2 1.3 copy-done
  6.7 16.3 %all-to-all-start = ((bf16[128,8,1024]{2,1,0:T(8,128)(2,1)}), bf16[128,8,1024]{2,1,0:T(8,128)(2,1)S(1)}, u32[]{:S(2)}, u32[]{:S(2)}) async-start(bf16[128,8,1024]{2,1,0:T(8,128)(2,1)} %bitcast.23), calls=%async_computation | async-start | bytes 4194304 | tf_op jit(solution)/shard_map/all_to_all | solution.py:264
  23.1 4.9 %collective-permute-start = (s32[16,128]{1,0:T(8,128)S(1)}, s32[16,128]{1,0:T(8,128)S(1)}, u32[]{:S(2)}, u32[]{:S(2)}) collective-permute-start(s32[16,128]{1,0:T(8,128)S(1)} %get-tuple-element.50.kept_ref), channel_id=1, source_target_pairs={{0,128},{32,160},{64,192},{96,224},{128,0},{160,32},{192,64},{224,... | collective-permute-start | bytes 24584 | tf_op jit(solution)/shard_map/ppermute | solution.py:274
  27.9 44.3 %collective-permute-done.came_ref = s32[16,128]{1,0:T(8,128)S(1)} collective-permute-done((s32[16,128]{1,0:T(8,128)S(1)}, s32[16,128]{1,0:T(8,128)S(1)}, u32[]{:S(2)}, u32[]{:S(2)}) %collective-permute-start) | collective-permute-done | bytes 8224 | tf_op jit(solution)/shard_map/ppermute | solution.py:274
  72.8 1.4 swap.7.kept_ref
  74.2 3.6 %collective-permute-done.1.came_ref = s32[16,128]{1,0:T(8,128)S(1)} collective-permute-done((s32[16,128]{1,0:T(8,128)}, s32[16,128]{1,0:T(8,128)S(1)}, u32[]{:S(2)}, u32[]{:S(2)}) %collective-permute-start.1) | collective-permute-done | bytes 8224 | tf_op jit(solution)/shard_map/ppermute | solution.py:274
  78.4 1.4 swap.8.kept_ref
  79.8 2.7 %collective-permute-done.2.came_ref = s32[16,128]{1,0:T(8,128)S(1)} collective-permute-done((s32[16,128]{1,0:T(8,128)}, s32[16,128]{1,0:T(8,128)S(1)}, u32[]{:S(2)}, u32[]{:S(2)}) %collective-permute-start.2) | collective-permute-done | bytes 8224 | tf_op jit(solution)/shard_map/ppermute | solution.py:274
  83.1 1.4 swap.9.kept_ref
  84.5 2.3 %collective-permute-start.3 = (s32[16,128]{1,0:T(8,128)}, s32[16,128]{1,0:T(8,128)S(1)}, u32[]{:S(2)}, u32[]{:S(2)}) collective-permute-start(s32[16,128]{1,0:T(8,128)} %swap.9.kept_ref), channel_id=1, source_target_pairs={{0,16},{8,24},{16,0},{24,8},{1,17},{9,25},{17,1},{25,9},{2,18},{10... | collective-permute-start | bytes 24584 | tf_op jit(solution)/shard_map/ppermute | solution.py:274
  86.8 1.9 %collective-permute-done.3.came_ref = s32[16,128]{1,0:T(8,128)S(1)} collective-permute-done((s32[16,128]{1,0:T(8,128)}, s32[16,128]{1,0:T(8,128)S(1)}, u32[]{:S(2)}, u32[]{:S(2)}) %collective-permute-start.3) | collective-permute-done | bytes 8224 | tf_op jit(solution)/shard_map/ppermute | solution.py:274
  89.3 1.4 swap.10.kept_ref
  91.5 2.0 %collective-permute-done.4.came_ref = s32[16,128]{1,0:T(8,128)S(1)} collective-permute-done((s32[16,128]{1,0:T(8,128)}, s32[16,128]{1,0:T(8,128)S(1)}, u32[]{:S(2)}, u32[]{:S(2)}) %collective-permute-start.4) | collective-permute-done | bytes 8224 | tf_op jit(solution)/shard_map/ppermute | solution.py:274
  94.1 1.4 swap.11.kept_ref
  95.5 2.7 %collective-permute-start.5 = (s32[16,128]{1,0:T(8,128)}, s32[16,128]{1,0:T(8,128)S(1)}, u32[]{:S(2)}, u32[]{:S(2)}) collective-permute-start(s32[16,128]{1,0:T(8,128)} %swap.11.kept_ref), channel_id=1, source_target_pairs={{0,2},{1,3},{2,0},{3,1},{4,6},{5,7},{6,4},{7,5},{8,10},{9,11},{10,... | collective-permute-start | bytes 24584 | tf_op jit(solution)/shard_map/ppermute | solution.py:274
  98.2 1.5 collective-permute-done.5.came_ref
  100.3 1.4 swap.12.kept_ref
  103.0 1.5 collective-permute-done.6.came_ref
  105.0 1.4 swap.13.here_ref
  106.4 8.5 %collective-permute-start.7 = (s32[16,128]{1,0:T(8,128)}, s32[16,128]{1,0:T(8,128)S(1)}, u32[]{:S(2)}, u32[]{:S(2)}) collective-permute-start(s32[16,128]{1,0:T(8,128)} %swap.13.here_ref), channel_id=1, source_target_pairs={{0,4},{4,0},{1,5},{5,1},{2,6},{6,2},{3,7},{7,3},{8,12},{12,8},{9,1... | collective-permute-start | bytes 24584 | tf_op jit(solution)/shard_map/ppermute | solution.py:260
  116.7 1.3 spread.1
  118.6 1.3 collective-permute-start.10
  119.9 1.3 collective-permute-start.11
  122.5 1.5 collective-permute-start.9
  124.0 3.3 %compare_near.1 = (f32[1,1024]{1,0:T(1,128)S(1)}, f32[1,1024]{1,0:T(1,128)S(1)}) custom-call(s32[1]{0:T(128)} %bitcast.refs_0_, bf16[1024,1024]{1,0:T(8,128)(2,1)S(1)} %bitcast.20, bf16[1024,1024]{1,0:T(8,128)(2,1)S(1)} %collective-permute-done.12.refs_2_.refs_4_.refs_8_, f32[1,1024]{1,0:T(1,128)S(1)} %get-tuple-element.61.refs_3_.refs_6_.refs_12_, ...), custom_call_target="tpu_custom_call" | custom-call | flops 2684354560 | bytes 4194304 | tf_op jit(solution)/shard_map/compare_near/pallas_call | solution.py:201
  127.3 2.8 %collective-permute-done.10.refs_1_.refs_3_ = bf16[256,1024]{1,0:T(8,128)(2,1)S(1)} collective-permute-done((bf16[256,1024]{1,0:T(8,128)(2,1)S(1)}, bf16[256,1024]{1,0:T(8,128)(2,1)S(1)}, u32[]{:S(2)}, u32[]{:S(2)}) %collective-permute-start.10) | collective-permute-done | bytes 524320 | tf_op jit(solution)/shard_map/ppermute | solution.py:256
  132.2 3.1 %compare_first.1 = (f32[1,512]{1,0:T(1,128)S(1)}, f32[1,1024]{1,0:T(1,128)S(1)}, f32[1,1024]{1,0:T(1,128)S(1)}) custom-call(s32[1]{0:T(128)} %bitcast.refs_0_, bf16[256,1024]{1,0:T(8,128)(2,1)S(1)} %collective-permute-done.10.refs_1_.refs_3_, bf16[256,1024]{1,0:T(8,128)(2,1)S(1)} %collective-permute-done.11.refs_2_.refs_4_, bf16[1024,1024]{1,0:T(8,128)(2,1)S(1)} %bitcast.21, ...), custom_call_target="tpu_custom_call" | custom-call | flops 2684354560 | bytes 5242880 | tf_op jit(solution)/shard_map/compare_first/pallas_call | solution.py:201
  137.8 4.2 %compare_second.1 = (f32[1,512]{1,0:T(1,128)S(1)}, f32[1,512]{1,0:T(1,128)S(1)}, f32[1,512]{1,0:T(1,128)S(1)}, f32[1,1024]{1,0:T(1,128)S(1)}, f32[1,1024]{1,0:T(1,128)S(1)}) custom-call(s32[1]{0:T(128)} %bitcast.refs_0_, bf16[256,1024]{1,0:T(8,128)(2,1)S(1)} %collective-permute-done.8.refs_1_.refs_3_, ...), custom_call_target="tpu_custom_call" | custom-call | flops 3758096384 | bytes 7340032 | tf_op jit(solution)/shard_map/compare_second/pallas_call | solution.py:201
  142.7 1.4 compare_cores.1
  144.4 19.6 %all_to_all.16 = f32[128,1,16]{2,1,0:T(1,128)} all-to-all(f32[128,1,16]{2,1,0:T(1,128)S(1)} %bitcast.24), channel_id=1, replica_groups=mesh['z'=8,'y'=4,'core'=2,'x'=4] {'z','y','x'}, dimensions={0} | all-to-all | bytes 16384 | tf_op jit(solution)/shard_map/all_to_all | solution.py:264
  164.1 1.7 %unpack.1 = f32[1,512]{1,0:T(1,128)} custom-call(f32[128,16]{1,0:T(8,128)} %bitcast.25, s32[1,512]{1,0:T(1,128)} %copy-done.4, s32[1,512]{1,0:T(1,128)} %copy-done.5), custom_call_target="tpu_custom_call" | custom-call | tf_op jit(solution)/shard_map/unpack/pallas_call | solution.py:237
  (58 shorter events, 18.7 us)
Async XLA Ops:
  0.8 1.2 copy-start.1
  4.2 1.4 copy-start
  5.5 0.6 copy-start.4
  6.1 0.6 copy-start.5
  6.7 16.3 %copy-start.3 = (s32[16,128]{1,0:T(8,128)}, s32[16,128]{1,0:T(8,128)S(1)}, u32[]{:S(2)}) copy-start(s32[16,128]{1,0:T(8,128)S(1)} %get-tuple-element.50.kept_ref) | copy-start | bytes 24580
  6.7 111.3 %all-to-all-start = ((bf16[128,8,1024]{2,1,0:T(8,128)(2,1)}), bf16[128,8,1024]{2,1,0:T(8,128)(2,1)S(1)}, u32[]{:S(2)}, u32[]{:S(2)}) async-start(bf16[128,8,1024]{2,1,0:T(8,128)(2,1)} %bitcast.23), calls=%async_computation | async-start | bytes 4194304 | tf_op jit(solution)/shard_map/all_to_all | solution.py:264
  23.1 49.2 %collective-permute-start = (s32[16,128]{1,0:T(8,128)S(1)}, s32[16,128]{1,0:T(8,128)S(1)}, u32[]{:S(2)}, u32[]{:S(2)}) collective-permute-start(s32[16,128]{1,0:T(8,128)S(1)} %get-tuple-element.50.kept_ref), channel_id=1, source_target_pairs={{0,128},{32,160},{64,192},{96,224},{128,0},{160,32},{192,64},{224,... | collective-permute-start | bytes 24584 | tf_op jit(solution)/shard_map/ppermute | solution.py:274
  72.2 0.6 copy-start.9
  74.2 3.6 %collective-permute-start.1 = (s32[16,128]{1,0:T(8,128)}, s32[16,128]{1,0:T(8,128)S(1)}, u32[]{:S(2)}, u32[]{:S(2)}) collective-permute-start(s32[16,128]{1,0:T(8,128)} %swap.7.kept_ref), channel_id=1, source_target_pairs={{0,64},{32,96},{64,0},{96,32},{128,192},{160,224},{192,128},{224,1... | collective-permute-start | bytes 24584 | tf_op jit(solution)/shard_map/ppermute | solution.py:274
  77.8 0.6 copy-start.8
  79.8 2.7 %collective-permute-start.2 = (s32[16,128]{1,0:T(8,128)}, s32[16,128]{1,0:T(8,128)S(1)}, u32[]{:S(2)}, u32[]{:S(2)}) collective-permute-start(s32[16,128]{1,0:T(8,128)} %swap.8.kept_ref), channel_id=1, source_target_pairs={{0,32},{32,0},{64,96},{96,64},{128,160},{160,128},{192,224},{224,1... | collective-permute-start | bytes 24584 | tf_op jit(solution)/shard_map/ppermute | solution.py:274
  82.5 0.6 copy-start.11
  84.5 4.2 %collective-permute-start.3 = (s32[16,128]{1,0:T(8,128)}, s32[16,128]{1,0:T(8,128)S(1)}, u32[]{:S(2)}, u32[]{:S(2)}) collective-permute-start(s32[16,128]{1,0:T(8,128)} %swap.9.kept_ref), channel_id=1, source_target_pairs={{0,16},{8,24},{16,0},{24,8},{1,17},{9,25},{17,1},{25,9},{2,18},{10... | collective-permute-start | bytes 24584 | tf_op jit(solution)/shard_map/ppermute | solution.py:274
  88.7 0.6 copy-start.7
  90.7 2.8 %collective-permute-start.4 = (s32[16,128]{1,0:T(8,128)}, s32[16,128]{1,0:T(8,128)S(1)}, u32[]{:S(2)}, u32[]{:S(2)}) collective-permute-start(s32[16,128]{1,0:T(8,128)} %swap.10.kept_ref), channel_id=1, source_target_pairs={{0,8},{8,0},{16,24},{24,16},{1,9},{9,1},{17,25},{25,17},{2,10},{10... | collective-permute-start | bytes 24584 | tf_op jit(solution)/shard_map/ppermute | solution.py:274
  93.5 0.6 copy-start.12
  95.5 4.2 %collective-permute-start.5 = (s32[16,128]{1,0:T(8,128)}, s32[16,128]{1,0:T(8,128)S(1)}, u32[]{:S(2)}, u32[]{:S(2)}) collective-permute-start(s32[16,128]{1,0:T(8,128)} %swap.11.kept_ref), channel_id=1, source_target_pairs={{0,2},{1,3},{2,0},{3,1},{4,6},{5,7},{6,4},{7,5},{8,10},{9,11},{10,... | collective-permute-start | bytes 24584 | tf_op jit(solution)/shard_map/ppermute | solution.py:274
  99.7 0.6 copy-start.6
  101.7 2.7 %collective-permute-start.6 = (s32[16,128]{1,0:T(8,128)}, s32[16,128]{1,0:T(8,128)S(1)}, u32[]{:S(2)}, u32[]{:S(2)}) collective-permute-start(s32[16,128]{1,0:T(8,128)} %swap.12.kept_ref), channel_id=1, source_target_pairs={{0,1},{1,0},{2,3},{3,2},{4,5},{5,4},{6,7},{7,6},{8,9},{9,8},{10,11... | collective-permute-start | bytes 24584 | tf_op jit(solution)/shard_map/ppermute | solution.py:274
  104.4 0.6 copy-start.10
  106.4 9.6 %collective-permute-start.7 = (s32[16,128]{1,0:T(8,128)}, s32[16,128]{1,0:T(8,128)S(1)}, u32[]{:S(2)}, u32[]{:S(2)}) collective-permute-start(s32[16,128]{1,0:T(8,128)} %swap.13.here_ref), channel_id=1, source_target_pairs={{0,4},{4,0},{1,5},{5,1},{2,6},{6,2},{3,7},{7,3},{8,12},{12,8},{9,1... | collective-permute-start | bytes 24584 | tf_op jit(solution)/shard_map/ppermute | solution.py:260
  116.0 0.7 copy-start.2
  118.0 6.0 %collective-permute-start.12 = (bf16[1024,1024]{1,0:T(8,128)(2,1)S(1)}, bf16[1024,1024]{1,0:T(8,128)(2,1)S(1)}, u32[]{:S(2)}, u32[]{:S(2)}) collective-permute-start(bf16[1024,1024]{1,0:T(8,128)(2,1)S(1)} %bitcast.18), channel_id=1, source_target_pairs={{0,4},{4,0},{1,5},{5,1},{2,6},{6,2},{3,7},{7,3},{8,12},{12,8},{9,1... | collective-permute-start | bytes 6291464 | tf_op jit(solution)/shard_map/ppermute | solution.py:260
  118.6 11.4 %collective-permute-start.10 = (bf16[256,1024]{1,0:T(8,128)(2,1)S(1)}, bf16[256,1024]{1,0:T(8,128)(2,1)S(1)}, u32[]{:S(2)}, u32[]{:S(2)}) collective-permute-start(bf16[256,1024]{1,0:T(8,128)(2,1)S(1)} %get-tuple-element.95), channel_id=1, source_target_pairs={{1,2},{3,0},{5,13},{7,15},{8,9},{10,11},{12,20},{14,22},{17,18},{1... | collective-permute-start | bytes 1572872 | tf_op jit(solution)/shard_map/ppermute | solution.py:256
  119.9 11.3 %collective-permute-start.11 = (bf16[256,1024]{1,0:T(8,128)(2,1)S(1)}, bf16[256,1024]{1,0:T(8,128)(2,1)S(1)}, u32[]{:S(2)}, u32[]{:S(2)}) collective-permute-start(bf16[256,1024]{1,0:T(8,128)(2,1)S(1)} %get-tuple-element.94), channel_id=1, source_target_pairs={{1,0},{3,2},{5,29},{7,31},{8,11},{10,9},{12,4},{14,6},{17,16},{19,... | collective-permute-start | bytes 1572872 | tf_op jit(solution)/shard_map/ppermute | solution.py:256
  121.2 14.4 %collective-permute-start.8 = (bf16[256,1024]{1,0:T(8,128)(2,1)S(1)}, bf16[256,1024]{1,0:T(8,128)(2,1)S(1)}, u32[]{:S(2)}, u32[]{:S(2)}) collective-permute-start(bf16[256,1024]{1,0:T(8,128)(2,1)S(1)} %get-tuple-element.96), channel_id=1, source_target_pairs={{1,2},{3,0},{5,13},{7,15},{8,9},{10,11},{12,20},{14,22},{17,18},{1... | collective-permute-start | bytes 1572872 | tf_op jit(solution)/shard_map/ppermute | solution.py:256
  122.5 14.3 %collective-permute-start.9 = (bf16[256,1024]{1,0:T(8,128)(2,1)S(1)}, bf16[256,1024]{1,0:T(8,128)(2,1)S(1)}, u32[]{:S(2)}, u32[]{:S(2)}) collective-permute-start(bf16[256,1024]{1,0:T(8,128)(2,1)S(1)} %get-tuple-element.93), channel_id=1, source_target_pairs={{1,0},{3,2},{5,29},{7,31},{8,11},{10,9},{12,4},{14,6},{17,16},{19,... | collective-permute-start | bytes 1572872 | tf_op jit(solution)/shard_map/ppermute | solution.py:256
  131.2 6.6 %collective-permute-start.13 = (bf16[256,1024]{1,0:T(8,128)(2,1)S(1)}, bf16[256,1024]{1,0:T(8,128)(2,1)S(1)}, u32[]{:S(2)}, u32[]{:S(2)}) collective-permute-start(bf16[256,1024]{1,0:T(8,128)(2,1)S(1)} %collective-permute-done.10.refs_1_.refs_3_), channel_id=1, source_target_pairs={{0,4},{4,0},{1,5},{5,1},{2,6},{6,2},{3,7},{7,3},{8,12},{12,8},{9,1... | collective-permute-start | bytes 1572872 | tf_op jit(solution)/shard_map/ppermute | solution.py:260
  132.2 5.6 %collective-permute-start.14 = (bf16[256,1024]{1,0:T(8,128)(2,1)S(1)}, bf16[256,1024]{1,0:T(8,128)(2,1)S(1)}, u32[]{:S(2)}, u32[]{:S(2)}) collective-permute-start(bf16[256,1024]{1,0:T(8,128)(2,1)S(1)} %collective-permute-done.11.refs_2_.refs_4_), channel_id=1, source_target_pairs={{0,4},{4,0},{1,5},{5,1},{2,6},{6,2},{3,7},{7,3},{8,12},{12,8},{9,1... | collective-permute-start | bytes 1572872 | tf_op jit(solution)/shard_map/ppermute | solution.py:260
  136.8 5.8 %collective-permute-start.16 = (bf16[256,1024]{1,0:T(8,128)(2,1)S(1)}, bf16[256,1024]{1,0:T(8,128)(2,1)S(1)}, u32[]{:S(2)}, u32[]{:S(2)}) collective-permute-start(bf16[256,1024]{1,0:T(8,128)(2,1)S(1)} %collective-permute-done.8.refs_1_.refs_3_), channel_id=1, source_target_pairs={{0,4},{4,0},{1,5},{5,1},{2,6},{6,2},{3,7},{7,3},{8,12},{12,8},{9,1... | collective-permute-start | bytes 1572872 | tf_op jit(solution)/shard_map/ppermute | solution.py:260
  137.8 4.9 %collective-permute-start.17 = (bf16[256,1024]{1,0:T(8,128)(2,1)S(1)}, bf16[256,1024]{1,0:T(8,128)(2,1)S(1)}, u32[]{:S(2)}, u32[]{:S(2)}) collective-permute-start(bf16[256,1024]{1,0:T(8,128)(2,1)S(1)} %collective-permute-done.9.refs_2_.refs_4_), channel_id=1, source_target_pairs={{0,4},{4,0},{1,5},{5,1},{2,6},{6,2},{3,7},{7,3},{8,12},{12,8},{9,1... | collective-permute-start | bytes 1572872 | tf_op jit(solution)/shard_map/ppermute | solution.py:260
  142.1 2.0 %collective-permute-start.15 = (f32[1,1536]{1,0:T(1,128)S(1)}, f32[1,1536]{1,0:T(1,128)S(1)}, u32[]{:S(2)}, u32[]{:S(2)}) collective-permute-start(f32[1,1536]{1,0:T(1,128)S(1)} %pad_maximum_fusion.1), channel_id=1, source_target_pairs={{0,4},{4,0},{1,5},{5,1},{2,6},{6,2},{3,7},{7,3},{8,12},{12,8},{9,1... | collective-permute-start | bytes 18440 | tf_op jit(solution)/shard_map/ppermute | solution.py:260

commit v8 on v5

--- a/solution.py
+++ b/solution.py
@@ -9,11 +9,13 @@
 
 NZ, NY, NC, NX = 8, 4, 2, 4
 CHIPS = NZ * NY * NX
+CLUSTERS = CHIPS // 2
 SLOTS = 16
 HALF = 8
 NO_RANK = 1 << 20
-TORUS = ("z", "y", "x")
-ALL = ("z", "y", "core", "x")
+TORUS = ("z", "y", "xh", "xl")
+PAIRS = ("z", "y", "xh")
+ALL = ("z", "y", "core", "xh", "xl")
 MIB = 2**20
 TILE = 512
 
@@ -30,25 +32,19 @@
     return jnp.where(which < 4, weight, 0).astype(jnp.float32).astype(jnp.bfloat16)
 
 
-def pack_kernel(place_ref, emb_ref, labels_ref, rows_ref, home_ref, slot_ref):
+def pack_kernel(place_ref, emb_ref, labels_ref, rows_ref, slot_ref):
     docs, features = emb_ref.shape
-    wide = emb_ref[...].astype(jnp.float32)
-    squares = jnp.sum(wide * wide, axis=1, keepdims=True) + 1e-06
-    unit = (wide * lax.rsqrt(squares)).astype(jnp.bfloat16)
-    clu = labels_ref[0:1, :]
+    clu, rank = labels_ref[0:1, :], labels_ref[1:2, :]
     z, y, xh = clu // 8, (clu // 2) % 4, clu % 2
     x = 2 * xh + (y + z) % 2
     home = (z * NY + y) * NX + x
-    on_home = lax.broadcasted_iota(jnp.int32, (CHIPS, docs), 0) == home
-    member = on_home.astype(jnp.bfloat16)
+    in_cluster = lax.broadcasted_iota(jnp.int32, (CLUSTERS, docs), 0) == clu
     ahead = lax.broadcasted_iota(jnp.int32, (docs, docs), 0) < lax.broadcasted_iota(
         jnp.int32, (docs, docs), 1
     )
-    before = dot(member, ahead.astype(jnp.bfloat16), ((1,), (0,)))
-    slot = jnp.sum(jnp.where(on_home, before, 0.0), axis=0, keepdims=True).astype(jnp.int32)
-    home_ref[...] = home
+    before = dot(in_cluster.astype(jnp.bfloat16), ahead.astype(jnp.bfloat16), ((1,), (0,)))
+    slot = jnp.sum(jnp.where(in_cluster, before, 0.0), axis=0, keepdims=True).astype(jnp.int32)
     slot_ref[...] = slot
-    rank = labels_ref[1:2, :]
     which = lax.broadcasted_iota(jnp.int32, (128, docs), 0)
     digits = jnp.where(
         which == 0,
@@ -63,8 +59,11 @@
     at = jnp.where(slot < HALF, home * HALF + slot, via * HALF + slot - HALF)
     pick = lax.broadcasted_iota(jnp.int32, (CHIPS * HALF, docs), 0) == at
     pick = jnp.where(pick, 1.0, 0.0).astype(jnp.bfloat16)
+    rows_ref[:, features:] = dot(pick, digits, ((1,), (1,))).astype(jnp.bfloat16)
+    wide = emb_ref[...].astype(jnp.float32)
+    squares = jnp.sum(wide * wide, axis=1, keepdims=True) + 1e-06
+    unit = (wide * lax.rsqrt(squares)).astype(jnp.bfloat16)
     rows_ref[:, :features] = dot(pick, unit, ((1,), (0,))).astype(jnp.bfloat16)
-    rows_ref[:, features:] = dot(pick, digits, ((1,), (1,))).astype(jnp.bfloat16)
 
 
 def pack(place, embeddings, labels):
@@ -75,10 +74,9 @@
         out_shape=(
             jax.ShapeDtypeStruct((CHIPS * HALF, features + 128), jnp.bfloat16),
             jax.ShapeDtypeStruct((1, docs), jnp.int32),
-            jax.ShapeDtypeStruct((1, docs), jnp.int32),
         ),
         in_specs=[pl.BlockSpec(memory_space=pltpu.SMEM), vmem, vmem],
-        out_specs=(vmem,) * 3,
+        out_specs=(vmem,) * 2,
         compiler_params=pltpu.CompilerParams(vmem_limit_bytes=24 * MIB),
         name="pack",
     )(place, embeddings, labels)
@@ -100,6 +98,9 @@
         col_rank.append(refs.pop(0))
     weights = digit_weights()
     features = pieces[0][0].shape[1] - 128
+    as_query = {q for (q, _), _, _ in plan}
+    as_key = {k for _, (k, _), _ in plan}
+    maximum_of_key = {k for _, (k, _), both in plan if both}
     for i, (n, _, _) in enumerate(sets):
         if n > 1:
             whole = refs.pop(0)
@@ -110,10 +111,12 @@
             whole = pieces[i][0]
         joined.append(whole)
         tail = whole[:, features:]
-        row_rank[i][...] = dot(tail, weights, ((1,), (0,))) + float(NO_RANK)
-        col_rank[i][...] = dot(weights[:, :8], tail, ((0,), (1,))) + float(NO_RANK)
-        by_row[i][...] = jnp.full(by_row[i].shape, -1.0, jnp.float32)
-        by_col[i][...] = jnp.full(by_col[i].shape, -1.0, jnp.float32)
+        if i in as_query:
+            row_rank[i][...] = dot(tail, weights, ((1,), (0,))) + float(NO_RANK)
+            by_row[i][...] = jnp.full(by_row[i].shape, -1.0, jnp.float32)
+        if i in as_key:
+            col_rank[i][...] = dot(weights[:, :8], tail, ((0,), (1,))) + float(NO_RANK)
+            by_col[i][...] = jnp.full(by_col[i].shape, -1.0, jnp.float32)
     core = core_ref[0]
     for (q, qb), (k, kb), both in plan:
         q_at = pl.ds(pl.multiple_of((core if qb is None else qb) * TILE, TILE), TILE)
@@ -135,12 +138,16 @@
         if both:
             by_col[k][:, k_at] = jnp.maximum(by_col[k][:, k_at], jnp.concatenate(side, axis=1))
     for i, out in enumerate(outs):
-        if out is not None:
-            best = jnp.max(jnp.transpose(by_row[i][...]), axis=0, keepdims=True)
-            best = jnp.maximum(best, jnp.max(by_col[i][...], axis=0, keepdims=True))
-            if start[i] is not None:
-                best = jnp.maximum(best, start[i][...])
-            out[...] = best
+        if out is None:
+            continue
+        best = None if start[i] is None else start[i][...]
+        if i in as_query:
+            found = jnp.max(jnp.transpose(by_row[i][...]), axis=0, keepdims=True)
+            best = found if best is None else jnp.maximum(best, found)
+        if i in maximum_of_key:
+            found = jnp.max(by_col[i][...], axis=0, keepdims=True)
+            best = found if best is None else jnp.maximum(best, found)
+        out[...] = best
 
 
 def compare(core, sets, plan, name):
@@ -183,12 +190,12 @@
     )(core, *args)
 
 
-def unpack_kernel(back_ref, home_ref, slot_ref, out_ref):
-    docs = home_ref.shape[1]
-    on_home = lax.broadcasted_iota(jnp.int32, (CHIPS, docs), 0) == home_ref[...]
+def unpack_kernel(back_ref, clu_ref, slot_ref, out_ref):
+    docs = clu_ref.shape[1]
+    in_cluster = lax.broadcasted_iota(jnp.int32, (CLUSTERS, docs), 0) == clu_ref[...]
     found = lax.dot_general(
         back_ref[...],
-        on_home.astype(jnp.float32),
+        in_cluster.astype(jnp.float32),
         (((0,), (0,)), ((), ())),
         precision=lax.Precision.HIGHEST,
         preferred_element_type=jnp.float32,
@@ -197,15 +204,15 @@
     out_ref[...] = jnp.sum(jnp.where(in_slot, found, 0.0), axis=0, keepdims=True)
 
 
-def unpack(back, home, slot):
+def unpack(back, cluster, slot):
     vmem = pl.BlockSpec(memory_space=pltpu.VMEM)
     return pl.pallas_call(
         unpack_kernel,
-        out_shape=jax.ShapeDtypeStruct(home.shape, jnp.float32),
+        out_shape=jax.ShapeDtypeStruct(slot.shape, jnp.float32),
         in_specs=[vmem] * 3,
         out_specs=vmem,
         name="unpack",
-    )(back, home, slot)
+    )(back, cluster, slot)
 
 
 def to_home(a, step):
@@ -225,17 +232,17 @@
     return lax.ppermute(a, "core", [(0, 1), (1, 0)])
 
 
-def exchange(a):
-    return lax.all_to_all(a, TORUS, split_axis=0, concat_axis=0, tiled=True)
+def exchange(a, axes):
+    return lax.all_to_all(a, axes, split_axis=0, concat_axis=0, tiled=True)
 
 
 def per_device(embeddings, cluster, doc_rank):
     docs, features = embeddings.shape
     place = jnp.stack([lax.axis_index("core"), lax.axis_index("z") // (NZ // 2)]).astype(jnp.int32)
     core = place[:1]
-    rows, home, slot = pack(place, embeddings, jnp.stack([cluster, doc_rank]))
+    rows, slot = pack(place, embeddings, jnp.stack([cluster, doc_rank]))
     wide = features + 128
-    near = exchange(rows.reshape(CHIPS, HALF, wide)).reshape(CHIPS * HALF, wide)
+    near = exchange(rows.reshape(CHIPS, HALF, wide), TORUS).reshape(CHIPS * HALF, wide)
     part = near.shape[0] // 4
     quarter = [near[i * part : (i + 1) * part] for i in range(4)]
     far = [[to_home(quarter[i], 1), to_home(quarter[i + 2], -1)] for i in (0, 1)]
@@ -295,12 +302,16 @@
     best_first = jnp.maximum(best_first, theirs[:, count:])
     best_far = [b[:, i : i + part] for i in (0, part) for b in (best_first, best_second)]
     best_far = jnp.concatenate(best_far, axis=1)
-    result = [b.reshape(CHIPS, HALF) for b in (best_near, best_far)]
-    return unpack(exchange(jnp.concatenate(result, axis=1)), home, slot).reshape(docs)
+    result = jnp.concatenate([b.reshape(CHIPS, HALF) for b in (best_near, best_far)], axis=1)
+    passed = lax.ppermute(result, "xl", [(0, 1), (1, 0)])
+    at_home = (lax.axis_index("xl") + lax.axis_index("y") + lax.axis_index("z")) % 2 == 0
+    result = jnp.where(at_home, result, passed).reshape(CLUSTERS, 2, SLOTS)
+    result = jnp.where(lax.axis_index("xl") == 0, result[:, 0], result[:, 1])
+    return unpack(exchange(result, PAIRS), cluster.reshape(1, docs), slot).reshape(docs)
 
 
 def solution(mesh):
-    torus = Mesh(mesh.devices.reshape(NZ, NY, NC, NX), ALL)
+    torus = Mesh(mesh.devices.reshape(NZ, NY, NC, NX // 2, 2), ALL)
     placed = (P(ALL, None), P(ALL), P(ALL))
     return jax.shard_map(
         per_device, mesh=torus, in_specs=placed, out_specs=P(ALL), check_vma=False

time: 128 us -> 130 us (1.016); the launches traced: 128 us -> 128 us
  waiting for transfers between devices: 5.28 us -> 8.03 us
  blocking collectives: 90.1 us -> 88.3 us
    ppermute x0 -> x1, waiting for transfers between devices: none -> 2.47 us  [per_device(): passed = lax.ppermute(result, 'xl', [(0, 1), (1, 0)])]
    all_to_all x2, blocking collectives: 90.1 us -> 88.3 us  [exchange(): return lax.all_to_all(a, axes, split_axis=0, concat_axis=0, tiled=True)]
  transfers between devices with their start and end apart: 10 -> 11, of which waited for: 4 -> 5; matrix products, arithmetic and copies ran while one was open for 0% -> 0% of each run, Pallas kernels for 11% -> 10%
where the time goes in v8:
time: 130 us; the launch traced here: 128 us
  blocking collectives  88.3 us (68%)
  Pallas kernels  17.3 us (13%)
  starting transfers between devices  12 us (9%)
  waiting for transfers between devices  8.03 us (6%)
  local copies, waits for them, and re-layouts  1.8 us (1%)
    all_to_all x2, blocking collectives, exchange(): return lax.all_to_all(a, axes, split_axis=0, concat_axis=0, tiled=True)  88.3 us
    pallas_call x4, Pallas kernels, compare(): pl.pallas_call(functools.partial(compare_kernel, plan, [(len(arrays), bes...  13.2 us
    ppermute x6, starting transfers between devices, other_core(): return lax.ppermute(a, 'core', [(0, 1), (1, 0)])  6.76 us
    ppermute x4, waiting for transfers between devices, to_home(): return lax.ppermute(a, ALL, pairs)  5.55 us
    ppermute x4, starting transfers between devices, to_home(): return lax.ppermute(a, ALL, pairs)  5.17 us
  transfers between devices with their start and end apart: 11, of which 5 were waited for; matrix products, arithmetic and copies ran while one was open for 0% of the time, Pallas kernels for 10%

profile of v8, /device:TPU:1, one launch (start us, length us, event | category | flops | bytes accessed | tf_op | source)
XLA Modules:
  0.0 128.5 jit_solution(9506663225347850074)
XLA Ops:
  0.0 0.1 pad_add_fusion.1.place_ref
  0.1 0.7 pad_add_fusion.labels_ref
  0.8 1.2 copy-done
  2.0 2.4 %pack.1 = (bf16[1024,1152]{1,0:T(8,128)(2,1)S(1)}, s32[1,512]{1,0:T(1,128)S(1)}) custom-call(s32[2]{0:T(128)S(1)} %pad_add_fusion.1.place_ref, bf16[512,1024]{1,0:T(8,128)(2,1)S(1)} %copy-done, s32[2,512]{1,0:T(2,128)S(1)} %pad_add_fusion.labels_ref), custom_call_target="tpu_custom_call" | custom-call | tf_op jit(solution)/shard_map/pack/pallas_call | solution.py:72
  4.5 71.0 %all_to_all.13 = bf16[128,8,1152]{2,1,0:T(8,128)(2,1)S(1)} all-to-all(bf16[128,8,1152]{2,1,0:T(8,128)(2,1)S(1)} %bitcast.21), channel_id=1, replica_groups=mesh['z'=8,'y'=4,'core'=2,'xh'=2,'xl'=2] {'z','y','xh','xl'}, dimensions={0} | all-to-all | bytes 4718592 | tf_op jit(solution)/shard_map/all_to_all | solution.py:236
  75.4 4.4 %collective-permute-start.4 = (bf16[1024,1152]{1,0:T(8,128)(2,1)S(1)}, bf16[1024,1152]{1,0:T(8,128)(2,1)S(1)}, u32[]{:S(2)}, u32[]{:S(2)}) collective-permute-start(bf16[1024,1152]{1,0:T(8,128)(2,1)S(1)} %bitcast.17), channel_id=1, source_target_pairs={{0,4},{4,0},{1,5},{5,1},{2,6},{6,2},{3,7},{7,3},{8,12},{12,8},{9,1... | collective-permute-start | bytes 7077896 | tf_op jit(solution)/shard_map/ppermute | solution.py:232
  79.9 0.2 slice_bitcast_fusion.2
  80.0 1.3 %collective-permute-start.2 = (bf16[256,1152]{1,0:T(8,128)(2,1)S(1)}, bf16[256,1152]{1,0:T(8,128)(2,1)S(1)}, u32[]{:S(2)}, u32[]{:S(2)}) collective-permute-start(bf16[256,1152]{1,0:T(8,128)(2,1)S(1)} %get-tuple-element.53), channel_id=1, source_target_pairs={{1,2},{3,0},{5,13},{7,15},{8,9},{10,11},{12,20},{14,22},{17,18},{1... | collective-permute-start | bytes 1769480 | tf_op jit(solution)/shard_map/ppermute | solution.py:228
  81.3 1.3 %collective-permute-start.3 = (bf16[256,1152]{1,0:T(8,128)(2,1)S(1)}, bf16[256,1152]{1,0:T(8,128)(2,1)S(1)}, u32[]{:S(2)}, u32[]{:S(2)}) collective-permute-start(bf16[256,1152]{1,0:T(8,128)(2,1)S(1)} %get-tuple-element.52), channel_id=1, source_target_pairs={{1,0},{3,2},{5,29},{7,31},{8,11},{10,9},{12,4},{14,6},{17,16},{19,... | collective-permute-start | bytes 1769480 | tf_op jit(solution)/shard_map/ppermute | solution.py:228
  82.6 1.3 %collective-permute-start = (bf16[256,1152]{1,0:T(8,128)(2,1)S(1)}, bf16[256,1152]{1,0:T(8,128)(2,1)S(1)}, u32[]{:S(2)}, u32[]{:S(2)}) collective-permute-start(bf16[256,1152]{1,0:T(8,128)(2,1)S(1)} %get-tuple-element.54), channel_id=1, source_target_pairs={{1,2},{3,0},{5,13},{7,15},{8,9},{10,11},{12,20},{14,22},{17,18},{1... | collective-permute-start | bytes 1769480 | tf_op jit(solution)/shard_map/ppermute | solution.py:228
  83.9 1.3 %collective-permute-start.1 = (bf16[256,1152]{1,0:T(8,128)(2,1)S(1)}, bf16[256,1152]{1,0:T(8,128)(2,1)S(1)}, u32[]{:S(2)}, u32[]{:S(2)}) collective-permute-start(bf16[256,1152]{1,0:T(8,128)(2,1)S(1)} %get-tuple-element.51), channel_id=1, source_target_pairs={{1,0},{3,2},{5,29},{7,31},{8,11},{10,9},{12,4},{14,6},{17,16},{19,... | collective-permute-start | bytes 1769480 | tf_op jit(solution)/shard_map/ppermute | solution.py:228
  85.2 0.0 collective-permute-done.4.refs_2_.refs_4_.refs_8_
  85.2 3.5 %compare_near.1 = (f32[1,1024]{1,0:T(1,128)S(1)}, f32[1,1024]{1,0:T(1,128)S(1)}) custom-call(s32[1]{0:T(128)} %bitcast.refs_0_, bf16[1024,1152]{1,0:T(8,128)(2,1)S(1)} %bitcast.18, bf16[1024,1152]{1,0:T(8,128)(2,1)S(1)} %collective-permute-done.4.refs_2_.refs_4_.refs_8_), custom_call_target="tpu_custom_call" | custom-call | flops 3019898880 | bytes 4718592 | tf_op jit(solution)/shard_map/compare_near/pallas_call | solution.py:173
  88.7 3.5 %collective-permute-done.2.refs_1_.refs_3_ = bf16[256,1152]{1,0:T(8,128)(2,1)S(1)} collective-permute-done((bf16[256,1152]{1,0:T(8,128)(2,1)S(1)}, bf16[256,1152]{1,0:T(8,128)(2,1)S(1)}, u32[]{:S(2)}, u32[]{:S(2)}) %collective-permute-start.2) | collective-permute-done | bytes 589856 | tf_op jit(solution)/shard_map/ppermute | solution.py:228
  92.2 0.1 collective-permute-done.3.refs_2_.refs_4_
  92.3 0.9 collective-permute-start.5
  93.1 0.0 collective-permute-start.6
  93.1 3.5 %compare_first.1 = (f32[1,512]{1,0:T(1,128)S(1)}, f32[1,1024]{1,0:T(1,128)S(1)}, f32[1,1024]{1,0:T(1,128)S(1)}) custom-call(s32[1]{0:T(128)} %bitcast.refs_0_, bf16[256,1152]{1,0:T(8,128)(2,1)S(1)} %collective-permute-done.2.refs_1_.refs_3_, bf16[256,1152]{1,0:T(8,128)(2,1)S(1)} %collective-permute-done.3.refs_2_.refs_4_, bf16[1024,1152]{1,0:T(8,128)(2,1)S(1)} %bitcast.19, ...), custom_call_target="tpu_custom_call" | custom-call | flops 3019898880 | bytes 5898240 | tf_op jit(solution)/shard_map/compare_first/pallas_call | solution.py:173
  96.6 1.9 %collective-permute-done.refs_1_.refs_3_ = bf16[256,1152]{1,0:T(8,128)(2,1)S(1)} collective-permute-done((bf16[256,1152]{1,0:T(8,128)(2,1)S(1)}, bf16[256,1152]{1,0:T(8,128)(2,1)S(1)}, u32[]{:S(2)}, u32[]{:S(2)}) %collective-permute-start) | collective-permute-done | bytes 589856 | tf_op jit(solution)/shard_map/ppermute | solution.py:228
  98.5 0.1 collective-permute-done.1.refs_2_.refs_4_
  98.6 0.9 collective-permute-start.8
  99.4 0.0 collective-permute-start.9
  99.5 4.8 %compare_second.1 = (f32[1,512]{1,0:T(1,128)S(1)}, f32[1,512]{1,0:T(1,128)S(1)}, f32[1,512]{1,0:T(1,128)S(1)}, f32[1,1024]{1,0:T(1,128)S(1)}, f32[1,1024]{1,0:T(1,128)S(1)}) custom-call(s32[1]{0:T(128)} %bitcast.refs_0_, bf16[256,1152]{1,0:T(8,128)(2,1)S(1)} %collective-permute-done.refs_1_.refs_3_, ...), custom_call_target="tpu_custom_call" | custom-call | flops 4227858432 | bytes 8257536 | tf_op jit(solution)/shard_map/compare_second/pallas_call | solution.py:173
  104.3 0.6 collective-permute-start.7
  104.8 1.6 %compare_cores.1 = (f32[1,512]{1,0:T(1,128)S(1)}, f32[1,512]{1,0:T(1,128)S(1)}) custom-call(s32[1]{0:T(128)} %bitcast.refs_0_, bf16[256,1152]{1,0:T(8,128)(2,1)S(1)} %collective-permute-done.2.refs_1_.refs_3_, bf16[256,1152]{1,0:T(8,128)(2,1)S(1)} %collective-permute-done.3.refs_2_.refs_4_, bf16[256,1152]{1,0:T(8,128)(2,1)S(1)} %collective-permute-done.refs_1_.refs_3_, ...), custom_call_target="tpu_custom_call" | custom-call | flops 1207959552 | bytes 4718592 | tf_op jit(solution)/shard_map/compare_cores/pallas_call | solution.py:173
  106.5 0.1 reshape.28
  106.6 0.1 reshape.27
  106.8 0.1 collective-permute-start.10
  106.9 2.5 %collective-permute-done.10 = f32[128,16]{0,1:T(8,128)S(1)} collective-permute-done((f32[128,16]{0,1:T(8,128)S(1)}, f32[128,16]{0,1:T(8,128)S(1)}, u32[]{:S(2)}, u32[]{:S(2)}) %collective-permute-start.10) | collective-permute-done | bytes 8224 | tf_op jit(solution)/shard_map/ppermute | solution.py:306
  109.4 0.1 copy.8
  109.5 17.4 %all_to_all.14 = f32[64,1,16]{2,1,0:T(1,128)} all-to-all(f32[64,1,16]{2,1,0:T(1,128)S(1)} %broadcast_select_fusion), channel_id=1, replica_groups=mesh['z'=8,'y'=4,'core'=2,'xh'=2,'xl'=2] {'z','y','xh'}, dimensions={0} | all-to-all | bytes 8192 | tf_op jit(solution)/shard_map/all_to_all | solution.py:236
  126.9 1.6 %unpack.1 = f32[1,512]{1,0:T(1,128)} custom-call(f32[64,16]{1,0:T(8,128)} %bitcast.23, s32[1,512]{1,0:T(1,128)} %bitcast.25, s32[1,512]{1,0:T(1,128)} %copy-done.1), custom_call_target="tpu_custom_call" | custom-call | tf_op jit(solution)/shard_map/unpack/pallas_call | solution.py:209
  (18 shorter events, 0.2 us)
Async XLA Ops:
  0.8 1.2 copy-start
  4.4 71.0 %copy-start.1 = (s32[1,512]{1,0:T(1,128)}, s32[1,512]{1,0:T(1,128)S(1)}, u32[]{:S(2)}) copy-start(s32[1,512]{1,0:T(1,128)S(1)} %get-tuple-element.50.slot_ref) | copy-start | bytes 6148
  75.4 9.8 %collective-permute-start.4 = (bf16[1024,1152]{1,0:T(8,128)(2,1)S(1)}, bf16[1024,1152]{1,0:T(8,128)(2,1)S(1)}, u32[]{:S(2)}, u32[]{:S(2)}) collective-permute-start(bf16[1024,1152]{1,0:T(8,128)(2,1)S(1)} %bitcast.17), channel_id=1, source_target_pairs={{0,4},{4,0},{1,5},{5,1},{2,6},{6,2},{3,7},{7,3},{8,12},{12,8},{9,1... | collective-permute-start | bytes 7077896 | tf_op jit(solution)/shard_map/ppermute | solution.py:232
  80.0 12.1 %collective-permute-start.2 = (bf16[256,1152]{1,0:T(8,128)(2,1)S(1)}, bf16[256,1152]{1,0:T(8,128)(2,1)S(1)}, u32[]{:S(2)}, u32[]{:S(2)}) collective-permute-start(bf16[256,1152]{1,0:T(8,128)(2,1)S(1)} %get-tuple-element.53), channel_id=1, source_target_pairs={{1,2},{3,0},{5,13},{7,15},{8,9},{10,11},{12,20},{14,22},{17,18},{1... | collective-permute-start | bytes 1769480 | tf_op jit(solution)/shard_map/ppermute | solution.py:228
  81.3 10.9 %collective-permute-start.3 = (bf16[256,1152]{1,0:T(8,128)(2,1)S(1)}, bf16[256,1152]{1,0:T(8,128)(2,1)S(1)}, u32[]{:S(2)}, u32[]{:S(2)}) collective-permute-start(bf16[256,1152]{1,0:T(8,128)(2,1)S(1)} %get-tuple-element.52), channel_id=1, source_target_pairs={{1,0},{3,2},{5,29},{7,31},{8,11},{10,9},{12,4},{14,6},{17,16},{19,... | collective-permute-start | bytes 1769480 | tf_op jit(solution)/shard_map/ppermute | solution.py:228
  82.6 15.9 %collective-permute-start = (bf16[256,1152]{1,0:T(8,128)(2,1)S(1)}, bf16[256,1152]{1,0:T(8,128)(2,1)S(1)}, u32[]{:S(2)}, u32[]{:S(2)}) collective-permute-start(bf16[256,1152]{1,0:T(8,128)(2,1)S(1)} %get-tuple-element.54), channel_id=1, source_target_pairs={{1,2},{3,0},{5,13},{7,15},{8,9},{10,11},{12,20},{14,22},{17,18},{1... | collective-permute-start | bytes 1769480 | tf_op jit(solution)/shard_map/ppermute | solution.py:228
  83.9 14.6 %collective-permute-start.1 = (bf16[256,1152]{1,0:T(8,128)(2,1)S(1)}, bf16[256,1152]{1,0:T(8,128)(2,1)S(1)}, u32[]{:S(2)}, u32[]{:S(2)}) collective-permute-start(bf16[256,1152]{1,0:T(8,128)(2,1)S(1)} %get-tuple-element.51), channel_id=1, source_target_pairs={{1,0},{3,2},{5,29},{7,31},{8,11},{10,9},{12,4},{14,6},{17,16},{19,... | collective-permute-start | bytes 1769480 | tf_op jit(solution)/shard_map/ppermute | solution.py:228
  92.3 7.2 %collective-permute-start.5 = (bf16[256,1152]{1,0:T(8,128)(2,1)S(1)}, bf16[256,1152]{1,0:T(8,128)(2,1)S(1)}, u32[]{:S(2)}, u32[]{:S(2)}) collective-permute-start(bf16[256,1152]{1,0:T(8,128)(2,1)S(1)} %collective-permute-done.2.refs_1_.refs_3_), channel_id=1, source_target_pairs={{0,4},{4,0},{1,5},{5,1},{2,6},{6,2},{3,7},{7,3},{8,12},{12,8},{9,1... | collective-permute-start | bytes 1769480 | tf_op jit(solution)/shard_map/ppermute | solution.py:232
  93.1 6.3 %collective-permute-start.6 = (bf16[256,1152]{1,0:T(8,128)(2,1)S(1)}, bf16[256,1152]{1,0:T(8,128)(2,1)S(1)}, u32[]{:S(2)}, u32[]{:S(2)}) collective-permute-start(bf16[256,1152]{1,0:T(8,128)(2,1)S(1)} %collective-permute-done.3.refs_2_.refs_4_), channel_id=1, source_target_pairs={{0,4},{4,0},{1,5},{5,1},{2,6},{6,2},{3,7},{7,3},{8,12},{12,8},{9,1... | collective-permute-start | bytes 1769480 | tf_op jit(solution)/shard_map/ppermute | solution.py:232
  98.6 6.3 %collective-permute-start.8 = (bf16[256,1152]{1,0:T(8,128)(2,1)S(1)}, bf16[256,1152]{1,0:T(8,128)(2,1)S(1)}, u32[]{:S(2)}, u32[]{:S(2)}) collective-permute-start(bf16[256,1152]{1,0:T(8,128)(2,1)S(1)} %collective-permute-done.refs_1_.refs_3_), channel_id=1, source_target_pairs={{0,4},{4,0},{1,5},{5,1},{2,6},{6,2},{3,7},{7,3},{8,12},{12,8},{9,1... | collective-permute-start | bytes 1769480 | tf_op jit(solution)/shard_map/ppermute | solution.py:232
  99.4 5.4 %collective-permute-start.9 = (bf16[256,1152]{1,0:T(8,128)(2,1)S(1)}, bf16[256,1152]{1,0:T(8,128)(2,1)S(1)}, u32[]{:S(2)}, u32[]{:S(2)}) collective-permute-start(bf16[256,1152]{1,0:T(8,128)(2,1)S(1)} %collective-permute-done.1.refs_2_.refs_4_), channel_id=1, source_target_pairs={{0,4},{4,0},{1,5},{5,1},{2,6},{6,2},{3,7},{7,3},{8,12},{12,8},{9,1... | collective-permute-start | bytes 1769480 | tf_op jit(solution)/shard_map/ppermute | solution.py:232
  104.3 2.2 %collective-permute-start.7 = (f32[1,1536]{1,0:T(1,128)S(1)}, f32[1,1536]{1,0:T(1,128)S(1)}, u32[]{:S(2)}, u32[]{:S(2)}) collective-permute-start(f32[1,1536]{1,0:T(1,128)S(1)} %pad_maximum_fusion.1), channel_id=1, source_target_pairs={{0,4},{4,0},{1,5},{5,1},{2,6},{6,2},{3,7},{7,3},{8,12},{12,8},{9,1... | collective-permute-start | bytes 18440 | tf_op jit(solution)/shard_map/ppermute | solution.py:232
  106.8 2.6 %collective-permute-start.10 = (f32[128,16]{0,1:T(8,128)S(1)}, f32[128,16]{0,1:T(8,128)S(1)}, u32[]{:S(2)}, u32[]{:S(2)}) collective-permute-start(f32[128,16]{0,1:T(8,128)S(1)} %pad_maximum_fusion), channel_id=1, source_target_pairs={{0,1},{1,0},{2,3},{3,2},{4,5},{5,4},{6,7},{7,6},{8,9},{9,8},{10,11... | collective-permute-start | bytes 24584 | tf_op jit(solution)/shard_map/ppermute | solution.py:306

commit v9 on v5

--- a/solution.py
+++ b/solution.py
@@ -30,22 +30,18 @@
     return jnp.where(which < 4, weight, 0).astype(jnp.float32).astype(jnp.bfloat16)
 
 
-def pack_kernel(place_ref, emb_ref, labels_ref, rows_ref, home_ref, slot_ref):
-    docs, features = emb_ref.shape
-    wide = emb_ref[...].astype(jnp.float32)
-    squares = jnp.sum(wide * wide, axis=1, keepdims=True) + 1e-06
-    unit = (wide * lax.rsqrt(squares)).astype(jnp.bfloat16)
+def place_kernel(place_ref, labels_ref, at_ref, digits_ref, home_ref, slot_ref):
+    docs = labels_ref.shape[1]
     clu = labels_ref[0:1, :]
     z, y, xh = clu // 8, (clu // 2) % 4, clu % 2
     x = 2 * xh + (y + z) % 2
     home = (z * NY + y) * NX + x
-    on_home = lax.broadcasted_iota(jnp.int32, (CHIPS, docs), 0) == home
-    member = on_home.astype(jnp.bfloat16)
+    in_cluster = lax.broadcasted_iota(jnp.int32, (CHIPS // 2, docs), 0) == clu
     ahead = lax.broadcasted_iota(jnp.int32, (docs, docs), 0) < lax.broadcasted_iota(
         jnp.int32, (docs, docs), 1
     )
-    before = dot(member, ahead.astype(jnp.bfloat16), ((1,), (0,)))
-    slot = jnp.sum(jnp.where(on_home, before, 0.0), axis=0, keepdims=True).astype(jnp.int32)
+    before = dot(in_cluster.astype(jnp.bfloat16), ahead.astype(jnp.bfloat16), ((1,), (0,)))
+    slot = jnp.sum(jnp.where(in_cluster, before, 0.0), axis=0, keepdims=True).astype(jnp.int32)
     home_ref[...] = home
     slot_ref[...] = slot
     rank = labels_ref[1:2, :]
@@ -55,33 +51,48 @@
         rank & 255,
         jnp.where(which == 1, (rank >> 8) & 255, jnp.where(which == 2, rank >> 16, 1)),
     )
-    digits = jnp.where(which < 4, digits, 0).astype(jnp.float32).astype(jnp.bfloat16)
+    digits_ref[...] = jnp.where(which < 4, digits, 0).astype(jnp.float32).astype(jnp.bfloat16)
     core, upper = place_ref[0], place_ref[1]
     side = jnp.where(upper == 0, -1, 1)
     dy, dx = side * core, side * (1 - core)
     via = (z * NY + ((y + dy) & 3)) * NX + ((x + dx) & 3)
-    at = jnp.where(slot < HALF, home * HALF + slot, via * HALF + slot - HALF)
-    pick = lax.broadcasted_iota(jnp.int32, (CHIPS * HALF, docs), 0) == at
+    at_ref[...] = jnp.where(slot < HALF, home * HALF + slot, via * HALF + slot - HALF)
+
+
+def pack_kernel(emb_ref, at_ref, digits_ref, rows_ref):
+    docs, features = emb_ref.shape
+    wide = emb_ref[...].astype(jnp.float32)
+    squares = jnp.sum(wide * wide, axis=1, keepdims=True) + 1e-06
+    unit = (wide * lax.rsqrt(squares)).astype(jnp.bfloat16)
+    pick = lax.broadcasted_iota(jnp.int32, (CHIPS * HALF, docs), 0) == at_ref[...]
     pick = jnp.where(pick, 1.0, 0.0).astype(jnp.bfloat16)
     rows_ref[:, :features] = dot(pick, unit, ((1,), (0,))).astype(jnp.bfloat16)
-    rows_ref[:, features:] = dot(pick, digits, ((1,), (1,))).astype(jnp.bfloat16)
+    rows_ref[:, features:] = dot(pick, digits_ref[...], ((1,), (1,))).astype(jnp.bfloat16)
 
 
 def pack(place, embeddings, labels):
     docs, features = embeddings.shape
     vmem = pl.BlockSpec(memory_space=pltpu.VMEM)
-    return pl.pallas_call(
+    limit = pltpu.CompilerParams(vmem_limit_bytes=24 * MIB)
+    line = jax.ShapeDtypeStruct((1, docs), jnp.int32)
+    at, digits, home, slot = pl.pallas_call(
+        place_kernel,
+        out_shape=(line, jax.ShapeDtypeStruct((128, docs), jnp.bfloat16), line, line),
+        in_specs=[pl.BlockSpec(memory_space=pltpu.SMEM), vmem],
+        out_specs=(vmem,) * 4,
+        compiler_params=limit,
+        cost_estimate=pl.CostEstimate(flops=2 * 10**9, bytes_accessed=MIB, transcendentals=0),
+        name="place",
+    )(place, labels)
+    rows = pl.pallas_call(
         pack_kernel,
-        out_shape=(
-            jax.ShapeDtypeStruct((CHIPS * HALF, features + 128), jnp.bfloat16),
-            jax.ShapeDtypeStruct((1, docs), jnp.int32),
-            jax.ShapeDtypeStruct((1, docs), jnp.int32),
-        ),
-        in_specs=[pl.BlockSpec(memory_space=pltpu.SMEM), vmem, vmem],
-        out_specs=(vmem,) * 3,
-        compiler_params=pltpu.CompilerParams(vmem_limit_bytes=24 * MIB),
+        out_shape=jax.ShapeDtypeStruct((CHIPS * HALF, features + 128), jnp.bfloat16),
+        in_specs=[vmem] * 3,
+        out_specs=vmem,
+        compiler_params=limit,
         name="pack",
-    )(place, embeddings, labels)
+    )(embeddings, at, digits)
+    return rows, home, slot
 
 
 def compare_kernel(plan, sets, *refs):
@@ -100,6 +111,9 @@
         col_rank.append(refs.pop(0))
     weights = digit_weights()
     features = pieces[0][0].shape[1] - 128
+    as_query = {q for (q, _), _, _ in plan}
+    as_key = {k for _, (k, _), _ in plan}
+    maximum_of_key = {k for _, (k, _), both in plan if both}
     for i, (n, _, _) in enumerate(sets):
         if n > 1:
             whole = refs.pop(0)
@@ -110,10 +124,12 @@
             whole = pieces[i][0]
         joined.append(whole)
         tail = whole[:, features:]
-        row_rank[i][...] = dot(tail, weights, ((1,), (0,))) + float(NO_RANK)
-        col_rank[i][...] = dot(weights[:, :8], tail, ((0,), (1,))) + float(NO_RANK)
-        by_row[i][...] = jnp.full(by_row[i].shape, -1.0, jnp.float32)
-        by_col[i][...] = jnp.full(by_col[i].shape, -1.0, jnp.float32)
+        if i in as_query:
+            row_rank[i][...] = dot(tail, weights, ((1,), (0,))) + float(NO_RANK)
+            by_row[i][...] = jnp.full(by_row[i].shape, -1.0, jnp.float32)
+        if i in as_key:
+            col_rank[i][...] = dot(weights[:, :8], tail, ((0,), (1,))) + float(NO_RANK)
+            by_col[i][...] = jnp.full(by_col[i].shape, -1.0, jnp.float32)
     core = core_ref[0]
     for (q, qb), (k, kb), both in plan:
         q_at = pl.ds(pl.multiple_of((core if qb is None else qb) * TILE, TILE), TILE)
@@ -135,12 +151,16 @@
         if both:
             by_col[k][:, k_at] = jnp.maximum(by_col[k][:, k_at], jnp.concatenate(side, axis=1))
     for i, out in enumerate(outs):
-        if out is not None:
-            best = jnp.max(jnp.transpose(by_row[i][...]), axis=0, keepdims=True)
-            best = jnp.maximum(best, jnp.max(by_col[i][...], axis=0, keepdims=True))
-            if start[i] is not None:
-                best = jnp.maximum(best, start[i][...])
-            out[...] = best
+        if out is None:
+            continue
+        best = None if start[i] is None else start[i][...]
+        if i in as_query:
+            found = jnp.max(jnp.transpose(by_row[i][...]), axis=0, keepdims=True)
+            best = found if best is None else jnp.maximum(best, found)
+        if i in maximum_of_key:
+            found = jnp.max(by_col[i][...], axis=0, keepdims=True)
+            best = found if best is None else jnp.maximum(best, found)
+        out[...] = best
 
 
 def compare(core, sets, plan, name):

time: 128 us -> 127 us (level)
  transfers between devices with their start and end apart: 10 -> 10, of which waited for: 4 -> 4; matrix products, arithmetic and copies ran while one was open for 0% -> 0% of each run, Pallas kernels for 11% -> 10%
where the time goes in v9:
time: 127 us
  blocking collectives  90.1 us (71%)
  Pallas kernels  17.5 us (14%)
  starting transfers between devices  11.9 us (9%)
  waiting for transfers between devices  5.56 us (4%)
    all_to_all x2, blocking collectives, exchange(): return lax.all_to_all(a, TORUS, split_axis=0, concat_axis=0, tiled=True)  90.1 us
    pallas_call x4, Pallas kernels, compare(): pl.pallas_call(functools.partial(compare_kernel, plan, [(len(arrays), bes...  13.2 us
    ppermute x6, starting transfers between devices, other_core(): return lax.ppermute(a, 'core', [(0, 1), (1, 0)])  6.78 us
    ppermute x4, waiting for transfers between devices, to_home(): return lax.ppermute(a, ALL, pairs)  5.54 us
    ppermute x4, starting transfers between devices, to_home(): return lax.ppermute(a, ALL, pairs)  5.17 us
  transfers between devices with their start and end apart: 10, of which 4 were waited for; matrix products, arithmetic and copies ran while one was open for 0% of the time, Pallas kernels for 10%

profile of v9, /device:TPU:1, one launch (start us, length us, event | category | flops | bytes accessed | tf_op | source)
XLA Modules:
  0.0 126.9 jit_solution(13445976104618377942)
XLA Ops:
  0.0 0.1 pad_add_fusion.1.place_ref
  0.1 0.7 pad_add_fusion.labels_ref
  0.8 0.8 place.1
  1.6 0.4 copy-done
  2.0 1.8 %pack.1 = bf16[1024,1152]{1,0:T(8,128)(2,1)S(1)} custom-call(bf16[512,1024]{1,0:T(8,128)(2,1)S(1)} %copy-done, s32[1,512]{1,0:T(1,128)S(1)} %get-tuple-element.30.at_ref, bf16[128,512]{1,0:T(8,128)(2,1)S(1)} %get-tuple-element.31.digits_ref), custom_call_target="tpu_custom_call" | custom-call | tf_op jit(solution)/shard_map/pack/pallas_call | solution.py:87
  3.8 70.9 %all_to_all.16 = bf16[128,8,1152]{2,1,0:T(8,128)(2,1)S(1)} all-to-all(bf16[128,8,1152]{2,1,0:T(8,128)(2,1)S(1)} %bitcast.23), channel_id=1, replica_groups=mesh['z'=8,'y'=4,'core'=2,'x'=4] {'z','y','x'}, dimensions={0} | all-to-all | bytes 4718592 | tf_op jit(solution)/shard_map/all_to_all | solution.py:249
  74.8 4.5 %collective-permute-start.4 = (bf16[1024,1152]{1,0:T(8,128)(2,1)S(1)}, bf16[1024,1152]{1,0:T(8,128)(2,1)S(1)}, u32[]{:S(2)}, u32[]{:S(2)}) collective-permute-start(bf16[1024,1152]{1,0:T(8,128)(2,1)S(1)} %bitcast.19), channel_id=1, source_target_pairs={{0,4},{4,0},{1,5},{5,1},{2,6},{6,2},{3,7},{7,3},{8,12},{12,8},{9,1... | collective-permute-start | bytes 7077896 | tf_op jit(solution)/shard_map/ppermute | solution.py:245
  79.2 0.2 slice_bitcast_fusion.2
  79.4 1.3 %collective-permute-start.2 = (bf16[256,1152]{1,0:T(8,128)(2,1)S(1)}, bf16[256,1152]{1,0:T(8,128)(2,1)S(1)}, u32[]{:S(2)}, u32[]{:S(2)}) collective-permute-start(bf16[256,1152]{1,0:T(8,128)(2,1)S(1)} %get-tuple-element.57), channel_id=1, source_target_pairs={{1,2},{3,0},{5,13},{7,15},{8,9},{10,11},{12,20},{14,22},{17,18},{1... | collective-permute-start | bytes 1769480 | tf_op jit(solution)/shard_map/ppermute | solution.py:241
  80.7 1.3 %collective-permute-start.3 = (bf16[256,1152]{1,0:T(8,128)(2,1)S(1)}, bf16[256,1152]{1,0:T(8,128)(2,1)S(1)}, u32[]{:S(2)}, u32[]{:S(2)}) collective-permute-start(bf16[256,1152]{1,0:T(8,128)(2,1)S(1)} %get-tuple-element.56), channel_id=1, source_target_pairs={{1,0},{3,2},{5,29},{7,31},{8,11},{10,9},{12,4},{14,6},{17,16},{19,... | collective-permute-start | bytes 1769480 | tf_op jit(solution)/shard_map/ppermute | solution.py:241
  82.0 1.3 %collective-permute-start = (bf16[256,1152]{1,0:T(8,128)(2,1)S(1)}, bf16[256,1152]{1,0:T(8,128)(2,1)S(1)}, u32[]{:S(2)}, u32[]{:S(2)}) collective-permute-start(bf16[256,1152]{1,0:T(8,128)(2,1)S(1)} %get-tuple-element.58), channel_id=1, source_target_pairs={{1,2},{3,0},{5,13},{7,15},{8,9},{10,11},{12,20},{14,22},{17,18},{1... | collective-permute-start | bytes 1769480 | tf_op jit(solution)/shard_map/ppermute | solution.py:241
  83.3 1.3 %collective-permute-start.1 = (bf16[256,1152]{1,0:T(8,128)(2,1)S(1)}, bf16[256,1152]{1,0:T(8,128)(2,1)S(1)}, u32[]{:S(2)}, u32[]{:S(2)}) collective-permute-start(bf16[256,1152]{1,0:T(8,128)(2,1)S(1)} %get-tuple-element.55), channel_id=1, source_target_pairs={{1,0},{3,2},{5,29},{7,31},{8,11},{10,9},{12,4},{14,6},{17,16},{19,... | collective-permute-start | bytes 1769480 | tf_op jit(solution)/shard_map/ppermute | solution.py:241
  84.6 0.0 collective-permute-done.4.refs_2_.refs_4_.refs_8_
  84.6 3.5 %compare_near.1 = (f32[1,1024]{1,0:T(1,128)S(1)}, f32[1,1024]{1,0:T(1,128)S(1)}) custom-call(s32[1]{0:T(128)} %bitcast.refs_0_, bf16[1024,1152]{1,0:T(8,128)(2,1)S(1)} %bitcast.20, bf16[1024,1152]{1,0:T(8,128)(2,1)S(1)} %collective-permute-done.4.refs_2_.refs_4_.refs_8_), custom_call_target="tpu_custom_call" | custom-call | flops 3019898880 | bytes 4718592 | tf_op jit(solution)/shard_map/compare_near/pallas_call | solution.py:186
  88.1 3.5 %collective-permute-done.2.refs_1_.refs_3_ = bf16[256,1152]{1,0:T(8,128)(2,1)S(1)} collective-permute-done((bf16[256,1152]{1,0:T(8,128)(2,1)S(1)}, bf16[256,1152]{1,0:T(8,128)(2,1)S(1)}, u32[]{:S(2)}, u32[]{:S(2)}) %collective-permute-start.2) | collective-permute-done | bytes 589856 | tf_op jit(solution)/shard_map/ppermute | solution.py:241
  91.5 0.1 collective-permute-done.3.refs_2_.refs_4_
  91.6 0.9 collective-permute-start.5
  92.5 0.0 collective-permute-start.6
  92.5 3.5 %compare_first.1 = (f32[1,512]{1,0:T(1,128)S(1)}, f32[1,1024]{1,0:T(1,128)S(1)}, f32[1,1024]{1,0:T(1,128)S(1)}) custom-call(s32[1]{0:T(128)} %bitcast.refs_0_, bf16[256,1152]{1,0:T(8,128)(2,1)S(1)} %collective-permute-done.2.refs_1_.refs_3_, bf16[256,1152]{1,0:T(8,128)(2,1)S(1)} %collective-permute-done.3.refs_2_.refs_4_, bf16[1024,1152]{1,0:T(8,128)(2,1)S(1)} %bitcast.21, ...), custom_call_target="tpu_custom_call" | custom-call | flops 3019898880 | bytes 5898240 | tf_op jit(solution)/shard_map/compare_first/pallas_call | solution.py:186
  95.9 1.9 %collective-permute-done.refs_1_.refs_3_ = bf16[256,1152]{1,0:T(8,128)(2,1)S(1)} collective-permute-done((bf16[256,1152]{1,0:T(8,128)(2,1)S(1)}, bf16[256,1152]{1,0:T(8,128)(2,1)S(1)}, u32[]{:S(2)}, u32[]{:S(2)}) %collective-permute-start) | collective-permute-done | bytes 589856 | tf_op jit(solution)/shard_map/ppermute | solution.py:241
  97.8 0.1 collective-permute-done.1.refs_2_.refs_4_
  97.9 0.9 collective-permute-start.8
  98.8 0.0 collective-permute-start.9
  98.8 4.8 %compare_second.1 = (f32[1,512]{1,0:T(1,128)S(1)}, f32[1,512]{1,0:T(1,128)S(1)}, f32[1,512]{1,0:T(1,128)S(1)}, f32[1,1024]{1,0:T(1,128)S(1)}, f32[1,1024]{1,0:T(1,128)S(1)}) custom-call(s32[1]{0:T(128)} %bitcast.refs_0_, bf16[256,1152]{1,0:T(8,128)(2,1)S(1)} %collective-permute-done.refs_1_.refs_3_, ...), custom_call_target="tpu_custom_call" | custom-call | flops 4227858432 | bytes 8257536 | tf_op jit(solution)/shard_map/compare_second/pallas_call | solution.py:186
  103.6 0.6 collective-permute-start.7
  104.2 1.5 %compare_cores.1 = (f32[1,512]{1,0:T(1,128)S(1)}, f32[1,512]{1,0:T(1,128)S(1)}) custom-call(s32[1]{0:T(128)} %bitcast.refs_0_, bf16[256,1152]{1,0:T(8,128)(2,1)S(1)} %collective-permute-done.2.refs_1_.refs_3_, bf16[256,1152]{1,0:T(8,128)(2,1)S(1)} %collective-permute-done.3.refs_2_.refs_4_, bf16[256,1152]{1,0:T(8,128)(2,1)S(1)} %collective-permute-done.refs_1_.refs_3_, ...), custom_call_target="tpu_custom_call" | custom-call | flops 1207959552 | bytes 4718592 | tf_op jit(solution)/shard_map/compare_cores/pallas_call | solution.py:186
  105.8 0.0 collective-permute-done.7
  105.8 0.1 reshape.24
  105.9 0.1 reshape.23
  106.0 0.1 pad_maximum_fusion
  106.1 19.1 %all_to_all.17 = f32[128,1,16]{2,1,0:T(1,128)} all-to-all(f32[128,1,16]{2,1,0:T(1,128)S(1)} %bitcast.24), channel_id=1, replica_groups=mesh['z'=8,'y'=4,'core'=2,'x'=4] {'z','y','x'}, dimensions={0} | all-to-all | bytes 16384 | tf_op jit(solution)/shard_map/all_to_all | solution.py:249
  125.2 1.7 %unpack.1 = f32[1,512]{1,0:T(1,128)} custom-call(f32[128,16]{1,0:T(8,128)} %bitcast.25, s32[1,512]{1,0:T(1,128)} %copy-done.1, s32[1,512]{1,0:T(1,128)} %copy-done.2), custom_call_target="tpu_custom_call" | custom-call | tf_op jit(solution)/shard_map/unpack/pallas_call | solution.py:222
  (14 shorter events, 0.1 us)
Async XLA Ops:
  0.8 1.2 copy-start
  1.6 73.2 %copy-start.1 = (s32[1,512]{1,0:T(1,128)}, s32[1,512]{1,0:T(1,128)S(1)}, u32[]{:S(2)}) copy-start(s32[1,512]{1,0:T(1,128)S(1)} %get-tuple-element.53.home_ref) | copy-start | bytes 6148
  1.6 73.2 %copy-start.2 = (s32[1,512]{1,0:T(1,128)}, s32[1,512]{1,0:T(1,128)S(1)}, u32[]{:S(2)}) copy-start(s32[1,512]{1,0:T(1,128)S(1)} %get-tuple-element.54.slot_ref) | copy-start | bytes 6148
  74.8 9.8 %collective-permute-start.4 = (bf16[1024,1152]{1,0:T(8,128)(2,1)S(1)}, bf16[1024,1152]{1,0:T(8,128)(2,1)S(1)}, u32[]{:S(2)}, u32[]{:S(2)}) collective-permute-start(bf16[1024,1152]{1,0:T(8,128)(2,1)S(1)} %bitcast.19), channel_id=1, source_target_pairs={{0,4},{4,0},{1,5},{5,1},{2,6},{6,2},{3,7},{7,3},{8,12},{12,8},{9,1... | collective-permute-start | bytes 7077896 | tf_op jit(solution)/shard_map/ppermute | solution.py:245
  79.4 12.1 %collective-permute-start.2 = (bf16[256,1152]{1,0:T(8,128)(2,1)S(1)}, bf16[256,1152]{1,0:T(8,128)(2,1)S(1)}, u32[]{:S(2)}, u32[]{:S(2)}) collective-permute-start(bf16[256,1152]{1,0:T(8,128)(2,1)S(1)} %get-tuple-element.57), channel_id=1, source_target_pairs={{1,2},{3,0},{5,13},{7,15},{8,9},{10,11},{12,20},{14,22},{17,18},{1... | collective-permute-start | bytes 1769480 | tf_op jit(solution)/shard_map/ppermute | solution.py:241
  80.7 10.9 %collective-permute-start.3 = (bf16[256,1152]{1,0:T(8,128)(2,1)S(1)}, bf16[256,1152]{1,0:T(8,128)(2,1)S(1)}, u32[]{:S(2)}, u32[]{:S(2)}) collective-permute-start(bf16[256,1152]{1,0:T(8,128)(2,1)S(1)} %get-tuple-element.56), channel_id=1, source_target_pairs={{1,0},{3,2},{5,29},{7,31},{8,11},{10,9},{12,4},{14,6},{17,16},{19,... | collective-permute-start | bytes 1769480 | tf_op jit(solution)/shard_map/ppermute | solution.py:241
  82.0 15.9 %collective-permute-start = (bf16[256,1152]{1,0:T(8,128)(2,1)S(1)}, bf16[256,1152]{1,0:T(8,128)(2,1)S(1)}, u32[]{:S(2)}, u32[]{:S(2)}) collective-permute-start(bf16[256,1152]{1,0:T(8,128)(2,1)S(1)} %get-tuple-element.58), channel_id=1, source_target_pairs={{1,2},{3,0},{5,13},{7,15},{8,9},{10,11},{12,20},{14,22},{17,18},{1... | collective-permute-start | bytes 1769480 | tf_op jit(solution)/shard_map/ppermute | solution.py:241
  83.3 14.6 %collective-permute-start.1 = (bf16[256,1152]{1,0:T(8,128)(2,1)S(1)}, bf16[256,1152]{1,0:T(8,128)(2,1)S(1)}, u32[]{:S(2)}, u32[]{:S(2)}) collective-permute-start(bf16[256,1152]{1,0:T(8,128)(2,1)S(1)} %get-tuple-element.55), channel_id=1, source_target_pairs={{1,0},{3,2},{5,29},{7,31},{8,11},{10,9},{12,4},{14,6},{17,16},{19,... | collective-permute-start | bytes 1769480 | tf_op jit(solution)/shard_map/ppermute | solution.py:241
  91.6 7.2 %collective-permute-start.5 = (bf16[256,1152]{1,0:T(8,128)(2,1)S(1)}, bf16[256,1152]{1,0:T(8,128)(2,1)S(1)}, u32[]{:S(2)}, u32[]{:S(2)}) collective-permute-start(bf16[256,1152]{1,0:T(8,128)(2,1)S(1)} %collective-permute-done.2.refs_1_.refs_3_), channel_id=1, source_target_pairs={{0,4},{4,0},{1,5},{5,1},{2,6},{6,2},{3,7},{7,3},{8,12},{12,8},{9,1... | collective-permute-start | bytes 1769480 | tf_op jit(solution)/shard_map/ppermute | solution.py:245
  92.5 6.3 %collective-permute-start.6 = (bf16[256,1152]{1,0:T(8,128)(2,1)S(1)}, bf16[256,1152]{1,0:T(8,128)(2,1)S(1)}, u32[]{:S(2)}, u32[]{:S(2)}) collective-permute-start(bf16[256,1152]{1,0:T(8,128)(2,1)S(1)} %collective-permute-done.3.refs_2_.refs_4_), channel_id=1, source_target_pairs={{0,4},{4,0},{1,5},{5,1},{2,6},{6,2},{3,7},{7,3},{8,12},{12,8},{9,1... | collective-permute-start | bytes 1769480 | tf_op jit(solution)/shard_map/ppermute | solution.py:245
  97.9 6.3 %collective-permute-start.8 = (bf16[256,1152]{1,0:T(8,128)(2,1)S(1)}, bf16[256,1152]{1,0:T(8,128)(2,1)S(1)}, u32[]{:S(2)}, u32[]{:S(2)}) collective-permute-start(bf16[256,1152]{1,0:T(8,128)(2,1)S(1)} %collective-permute-done.refs_1_.refs_3_), channel_id=1, source_target_pairs={{0,4},{4,0},{1,5},{5,1},{2,6},{6,2},{3,7},{7,3},{8,12},{12,8},{9,1... | collective-permute-start | bytes 1769480 | tf_op jit(solution)/shard_map/ppermute | solution.py:245
  98.8 5.4 %collective-permute-start.9 = (bf16[256,1152]{1,0:T(8,128)(2,1)S(1)}, bf16[256,1152]{1,0:T(8,128)(2,1)S(1)}, u32[]{:S(2)}, u32[]{:S(2)}) collective-permute-start(bf16[256,1152]{1,0:T(8,128)(2,1)S(1)} %collective-permute-done.1.refs_2_.refs_4_), channel_id=1, source_target_pairs={{0,4},{4,0},{1,5},{5,1},{2,6},{6,2},{3,7},{7,3},{8,12},{12,8},{9,1... | collective-permute-start | bytes 1769480 | tf_op jit(solution)/shard_map/ppermute | solution.py:245
  103.6 2.2 %collective-permute-start.7 = (f32[1,1536]{1,0:T(1,128)S(1)}, f32[1,1536]{1,0:T(1,128)S(1)}, u32[]{:S(2)}, u32[]{:S(2)}) collective-permute-start(f32[1,1536]{1,0:T(1,128)S(1)} %pad_maximum_fusion.1), channel_id=1, source_target_pairs={{0,4},{4,0},{1,5},{5,1},{2,6},{6,2},{3,7},{7,3},{8,12},{12,8},{9,1... | collective-permute-start | bytes 18440 | tf_op jit(solution)/shard_map/ppermute | solution.py:245

commit v10 on v9

--- a/solution.py
+++ b/solution.py
@@ -12,7 +12,7 @@
 SLOTS = 16
 HALF = 8
 NO_RANK = 1 << 20
-TORUS = ("z", "y", "x")
+TORUS = ("y", "z", "x")
 ALL = ("z", "y", "core", "x")
 MIB = 2**20
 TILE = 512
@@ -35,7 +35,7 @@
     clu = labels_ref[0:1, :]
     z, y, xh = clu // 8, (clu // 2) % 4, clu % 2
     x = 2 * xh + (y + z) % 2
-    home = (z * NY + y) * NX + x
+    home = (y * NZ + z) * NX + x
     in_cluster = lax.broadcasted_iota(jnp.int32, (CHIPS // 2, docs), 0) == clu
     ahead = lax.broadcasted_iota(jnp.int32, (docs, docs), 0) < lax.broadcasted_iota(
         jnp.int32, (docs, docs), 1
@@ -55,7 +55,7 @@
     core, upper = place_ref[0], place_ref[1]
     side = jnp.where(upper == 0, -1, 1)
     dy, dx = side * core, side * (1 - core)
-    via = (z * NY + ((y + dy) & 3)) * NX + ((x + dx) & 3)
+    via = (((y + dy) & 3) * NZ + z) * NX + ((x + dx) & 3)
     at_ref[...] = jnp.where(slot < HALF, home * HALF + slot, via * HALF + slot - HALF)
 
 
@@ -251,7 +251,7 @@
 
 def per_device(embeddings, cluster, doc_rank):
     docs, features = embeddings.shape
-    place = jnp.stack([lax.axis_index("core"), lax.axis_index("z") // (NZ // 2)]).astype(jnp.int32)
+    place = jnp.stack([lax.axis_index("core"), lax.axis_index("y") // (NY // 2)]).astype(jnp.int32)
     core = place[:1]
     rows, home, slot = pack(place, embeddings, jnp.stack([cluster, doc_rank]))
     wide = features + 128

time: 127 us -> 127 us (level)
  no operation moved by 1% of the time
where the time goes in v10:
time: 127 us; the launch traced here: 126 us
  blocking collectives  89.7 us (71%)
  Pallas kernels  17.5 us (14%)
  starting transfers between devices  11.8 us (9%)
  waiting for transfers between devices  5.56 us (4%)
    all_to_all x2, blocking collectives, exchange(): return lax.all_to_all(a, TORUS, split_axis=0, concat_axis=0, tiled=True)  89.7 us
    pallas_call x4, Pallas kernels, compare(): pl.pallas_call(functools.partial(compare_kernel, plan, [(len(arrays), bes...  13.2 us
    ppermute x6, starting transfers between devices, other_core(): return lax.ppermute(a, 'core', [(0, 1), (1, 0)])  6.6 us
    ppermute x4, waiting for transfers between devices, to_home(): return lax.ppermute(a, ALL, pairs)  5.54 us
    ppermute x4, starting transfers between devices, to_home(): return lax.ppermute(a, ALL, pairs)  5.17 us
  transfers between devices with their start and end apart: 10, of which 4 were waited for; matrix products, arithmetic and copies ran while one was open for 0% of the time, Pallas kernels for 10%

profile of v10, /device:TPU:1, one launch (start us, length us, event | category | flops | bytes accessed | tf_op | source)
XLA Modules:
  0.0 126.4 jit_solution(4647032766884639090)
XLA Ops:
  0.0 0.1 pad_add_fusion.1.place_ref
  0.1 0.7 pad_add_fusion.labels_ref
  0.8 0.8 place.1
  1.6 0.4 copy-done
  2.0 1.8 %pack.1 = bf16[1024,1152]{1,0:T(8,128)(2,1)S(1)} custom-call(bf16[512,1024]{1,0:T(8,128)(2,1)S(1)} %copy-done, s32[1,512]{1,0:T(1,128)S(1)} %get-tuple-element.30.at_ref, bf16[128,512]{1,0:T(8,128)(2,1)S(1)} %get-tuple-element.31.digits_ref), custom_call_target="tpu_custom_call" | custom-call | tf_op jit(solution)/shard_map/pack/pallas_call | solution.py:87
  3.8 70.9 %all_to_all.16 = bf16[128,8,1152]{2,1,0:T(8,128)(2,1)S(1)} all-to-all(bf16[128,8,1152]{2,1,0:T(8,128)(2,1)S(1)} %bitcast.23), channel_id=1, replica_groups=mesh['z'=8,'y'=4,'core'=2,'x'=4] {'y','z','x'}, dimensions={0} | all-to-all | bytes 4718592 | tf_op jit(solution)/shard_map/all_to_all | solution.py:249
  74.7 4.3 %collective-permute-start.4 = (bf16[1024,1152]{1,0:T(8,128)(2,1)S(1)}, bf16[1024,1152]{1,0:T(8,128)(2,1)S(1)}, u32[]{:S(2)}, u32[]{:S(2)}) collective-permute-start(bf16[1024,1152]{1,0:T(8,128)(2,1)S(1)} %bitcast.19), channel_id=1, source_target_pairs={{0,4},{4,0},{1,5},{5,1},{2,6},{6,2},{3,7},{7,3},{8,12},{12,8},{9,1... | collective-permute-start | bytes 7077896 | tf_op jit(solution)/shard_map/ppermute | solution.py:245
  79.0 0.2 slice_bitcast_fusion.2
  79.2 1.3 %collective-permute-start.2 = (bf16[256,1152]{1,0:T(8,128)(2,1)S(1)}, bf16[256,1152]{1,0:T(8,128)(2,1)S(1)}, u32[]{:S(2)}, u32[]{:S(2)}) collective-permute-start(bf16[256,1152]{1,0:T(8,128)(2,1)S(1)} %get-tuple-element.57), channel_id=1, source_target_pairs={{1,2},{3,0},{5,13},{7,15},{8,9},{10,11},{12,20},{14,22},{17,18},{1... | collective-permute-start | bytes 1769480 | tf_op jit(solution)/shard_map/ppermute | solution.py:241
  80.5 1.3 %collective-permute-start.3 = (bf16[256,1152]{1,0:T(8,128)(2,1)S(1)}, bf16[256,1152]{1,0:T(8,128)(2,1)S(1)}, u32[]{:S(2)}, u32[]{:S(2)}) collective-permute-start(bf16[256,1152]{1,0:T(8,128)(2,1)S(1)} %get-tuple-element.56), channel_id=1, source_target_pairs={{1,0},{3,2},{5,29},{7,31},{8,11},{10,9},{12,4},{14,6},{17,16},{19,... | collective-permute-start | bytes 1769480 | tf_op jit(solution)/shard_map/ppermute | solution.py:241
  81.8 1.3 %collective-permute-start = (bf16[256,1152]{1,0:T(8,128)(2,1)S(1)}, bf16[256,1152]{1,0:T(8,128)(2,1)S(1)}, u32[]{:S(2)}, u32[]{:S(2)}) collective-permute-start(bf16[256,1152]{1,0:T(8,128)(2,1)S(1)} %get-tuple-element.58), channel_id=1, source_target_pairs={{1,2},{3,0},{5,13},{7,15},{8,9},{10,11},{12,20},{14,22},{17,18},{1... | collective-permute-start | bytes 1769480 | tf_op jit(solution)/shard_map/ppermute | solution.py:241
  83.1 1.3 %collective-permute-start.1 = (bf16[256,1152]{1,0:T(8,128)(2,1)S(1)}, bf16[256,1152]{1,0:T(8,128)(2,1)S(1)}, u32[]{:S(2)}, u32[]{:S(2)}) collective-permute-start(bf16[256,1152]{1,0:T(8,128)(2,1)S(1)} %get-tuple-element.55), channel_id=1, source_target_pairs={{1,0},{3,2},{5,29},{7,31},{8,11},{10,9},{12,4},{14,6},{17,16},{19,... | collective-permute-start | bytes 1769480 | tf_op jit(solution)/shard_map/ppermute | solution.py:241
  84.4 3.5 %compare_near.1 = (f32[1,1024]{1,0:T(1,128)S(1)}, f32[1,1024]{1,0:T(1,128)S(1)}) custom-call(s32[1]{0:T(128)} %bitcast.refs_0_, bf16[1024,1152]{1,0:T(8,128)(2,1)S(1)} %bitcast.20, bf16[1024,1152]{1,0:T(8,128)(2,1)S(1)} %collective-permute-done.4.refs_2_.refs_4_.refs_8_), custom_call_target="tpu_custom_call" | custom-call | flops 3019898880 | bytes 4718592 | tf_op jit(solution)/shard_map/compare_near/pallas_call | solution.py:186
  87.8 3.5 %collective-permute-done.2.refs_1_.refs_3_ = bf16[256,1152]{1,0:T(8,128)(2,1)S(1)} collective-permute-done((bf16[256,1152]{1,0:T(8,128)(2,1)S(1)}, bf16[256,1152]{1,0:T(8,128)(2,1)S(1)}, u32[]{:S(2)}, u32[]{:S(2)}) %collective-permute-start.2) | collective-permute-done | bytes 589856 | tf_op jit(solution)/shard_map/ppermute | solution.py:241
  91.3 0.1 collective-permute-done.3.refs_2_.refs_4_
  91.4 0.9 collective-permute-start.5
  92.2 0.0 collective-permute-start.6
  92.3 3.5 %compare_first.1 = (f32[1,512]{1,0:T(1,128)S(1)}, f32[1,1024]{1,0:T(1,128)S(1)}, f32[1,1024]{1,0:T(1,128)S(1)}) custom-call(s32[1]{0:T(128)} %bitcast.refs_0_, bf16[256,1152]{1,0:T(8,128)(2,1)S(1)} %collective-permute-done.2.refs_1_.refs_3_, bf16[256,1152]{1,0:T(8,128)(2,1)S(1)} %collective-permute-done.3.refs_2_.refs_4_, bf16[1024,1152]{1,0:T(8,128)(2,1)S(1)} %bitcast.21, ...), custom_call_target="tpu_custom_call" | custom-call | flops 3019898880 | bytes 5898240 | tf_op jit(solution)/shard_map/compare_first/pallas_call | solution.py:186
  95.7 1.9 %collective-permute-done.refs_1_.refs_3_ = bf16[256,1152]{1,0:T(8,128)(2,1)S(1)} collective-permute-done((bf16[256,1152]{1,0:T(8,128)(2,1)S(1)}, bf16[256,1152]{1,0:T(8,128)(2,1)S(1)}, u32[]{:S(2)}, u32[]{:S(2)}) %collective-permute-start) | collective-permute-done | bytes 589856 | tf_op jit(solution)/shard_map/ppermute | solution.py:241
  97.6 0.1 collective-permute-done.1.refs_2_.refs_4_
  97.7 0.9 collective-permute-start.8
  98.6 0.0 collective-permute-start.9
  98.6 4.8 %compare_second.1 = (f32[1,512]{1,0:T(1,128)S(1)}, f32[1,512]{1,0:T(1,128)S(1)}, f32[1,512]{1,0:T(1,128)S(1)}, f32[1,1024]{1,0:T(1,128)S(1)}, f32[1,1024]{1,0:T(1,128)S(1)}) custom-call(s32[1]{0:T(128)} %bitcast.refs_0_, bf16[256,1152]{1,0:T(8,128)(2,1)S(1)} %collective-permute-done.refs_1_.refs_3_, ...), custom_call_target="tpu_custom_call" | custom-call | flops 4227858432 | bytes 8257536 | tf_op jit(solution)/shard_map/compare_second/pallas_call | solution.py:186
  103.4 0.6 collective-permute-start.7
  104.0 0.0 collective-permute-done.8.refs_7_
  104.0 0.0 collective-permute-done.9.refs_8_
  104.0 1.6 %compare_cores.1 = (f32[1,512]{1,0:T(1,128)S(1)}, f32[1,512]{1,0:T(1,128)S(1)}) custom-call(s32[1]{0:T(128)} %bitcast.refs_0_, bf16[256,1152]{1,0:T(8,128)(2,1)S(1)} %collective-permute-done.2.refs_1_.refs_3_, bf16[256,1152]{1,0:T(8,128)(2,1)S(1)} %collective-permute-done.3.refs_2_.refs_4_, bf16[256,1152]{1,0:T(8,128)(2,1)S(1)} %collective-permute-done.refs_1_.refs_3_, ...), custom_call_target="tpu_custom_call" | custom-call | flops 1207959552 | bytes 4718592 | tf_op jit(solution)/shard_map/compare_cores/pallas_call | solution.py:186
  105.6 0.1 reshape.24
  105.7 0.1 reshape.23
  105.8 0.1 pad_maximum_fusion
  105.9 18.8 %all_to_all.17 = f32[128,1,16]{2,1,0:T(1,128)} all-to-all(f32[128,1,16]{2,1,0:T(1,128)S(1)} %bitcast.24), channel_id=1, replica_groups=mesh['z'=8,'y'=4,'core'=2,'x'=4] {'y','z','x'}, dimensions={0} | all-to-all | bytes 16384 | tf_op jit(solution)/shard_map/all_to_all | solution.py:249
  124.6 1.7 %unpack.1 = f32[1,512]{1,0:T(1,128)} custom-call(f32[128,16]{1,0:T(8,128)} %bitcast.25, s32[1,512]{1,0:T(1,128)} %copy-done.1, s32[1,512]{1,0:T(1,128)} %copy-done.2), custom_call_target="tpu_custom_call" | custom-call | tf_op jit(solution)/shard_map/unpack/pallas_call | solution.py:222
  (14 shorter events, 0.1 us)
Async XLA Ops:
  0.8 1.2 copy-start
  1.6 73.1 %copy-start.1 = (s32[1,512]{1,0:T(1,128)}, s32[1,512]{1,0:T(1,128)S(1)}, u32[]{:S(2)}) copy-start(s32[1,512]{1,0:T(1,128)S(1)} %get-tuple-element.53.home_ref) | copy-start | bytes 6148
  1.6 73.1 %copy-start.2 = (s32[1,512]{1,0:T(1,128)}, s32[1,512]{1,0:T(1,128)S(1)}, u32[]{:S(2)}) copy-start(s32[1,512]{1,0:T(1,128)S(1)} %get-tuple-element.54.slot_ref) | copy-start | bytes 6148
  74.7 9.7 %collective-permute-start.4 = (bf16[1024,1152]{1,0:T(8,128)(2,1)S(1)}, bf16[1024,1152]{1,0:T(8,128)(2,1)S(1)}, u32[]{:S(2)}, u32[]{:S(2)}) collective-permute-start(bf16[1024,1152]{1,0:T(8,128)(2,1)S(1)} %bitcast.19), channel_id=1, source_target_pairs={{0,4},{4,0},{1,5},{5,1},{2,6},{6,2},{3,7},{7,3},{8,12},{12,8},{9,1... | collective-permute-start | bytes 7077896 | tf_op jit(solution)/shard_map/ppermute | solution.py:245
  79.2 12.1 %collective-permute-start.2 = (bf16[256,1152]{1,0:T(8,128)(2,1)S(1)}, bf16[256,1152]{1,0:T(8,128)(2,1)S(1)}, u32[]{:S(2)}, u32[]{:S(2)}) collective-permute-start(bf16[256,1152]{1,0:T(8,128)(2,1)S(1)} %get-tuple-element.57), channel_id=1, source_target_pairs={{1,2},{3,0},{5,13},{7,15},{8,9},{10,11},{12,20},{14,22},{17,18},{1... | collective-permute-start | bytes 1769480 | tf_op jit(solution)/shard_map/ppermute | solution.py:241
  80.5 10.9 %collective-permute-start.3 = (bf16[256,1152]{1,0:T(8,128)(2,1)S(1)}, bf16[256,1152]{1,0:T(8,128)(2,1)S(1)}, u32[]{:S(2)}, u32[]{:S(2)}) collective-permute-start(bf16[256,1152]{1,0:T(8,128)(2,1)S(1)} %get-tuple-element.56), channel_id=1, source_target_pairs={{1,0},{3,2},{5,29},{7,31},{8,11},{10,9},{12,4},{14,6},{17,16},{19,... | collective-permute-start | bytes 1769480 | tf_op jit(solution)/shard_map/ppermute | solution.py:241
  81.8 15.9 %collective-permute-start = (bf16[256,1152]{1,0:T(8,128)(2,1)S(1)}, bf16[256,1152]{1,0:T(8,128)(2,1)S(1)}, u32[]{:S(2)}, u32[]{:S(2)}) collective-permute-start(bf16[256,1152]{1,0:T(8,128)(2,1)S(1)} %get-tuple-element.58), channel_id=1, source_target_pairs={{1,2},{3,0},{5,13},{7,15},{8,9},{10,11},{12,20},{14,22},{17,18},{1... | collective-permute-start | bytes 1769480 | tf_op jit(solution)/shard_map/ppermute | solution.py:241
  83.1 14.6 %collective-permute-start.1 = (bf16[256,1152]{1,0:T(8,128)(2,1)S(1)}, bf16[256,1152]{1,0:T(8,128)(2,1)S(1)}, u32[]{:S(2)}, u32[]{:S(2)}) collective-permute-start(bf16[256,1152]{1,0:T(8,128)(2,1)S(1)} %get-tuple-element.55), channel_id=1, source_target_pairs={{1,0},{3,2},{5,29},{7,31},{8,11},{10,9},{12,4},{14,6},{17,16},{19,... | collective-permute-start | bytes 1769480 | tf_op jit(solution)/shard_map/ppermute | solution.py:241
  91.4 7.2 %collective-permute-start.5 = (bf16[256,1152]{1,0:T(8,128)(2,1)S(1)}, bf16[256,1152]{1,0:T(8,128)(2,1)S(1)}, u32[]{:S(2)}, u32[]{:S(2)}) collective-permute-start(bf16[256,1152]{1,0:T(8,128)(2,1)S(1)} %collective-permute-done.2.refs_1_.refs_3_), channel_id=1, source_target_pairs={{0,4},{4,0},{1,5},{5,1},{2,6},{6,2},{3,7},{7,3},{8,12},{12,8},{9,1... | collective-permute-start | bytes 1769480 | tf_op jit(solution)/shard_map/ppermute | solution.py:245
  92.2 6.3 %collective-permute-start.6 = (bf16[256,1152]{1,0:T(8,128)(2,1)S(1)}, bf16[256,1152]{1,0:T(8,128)(2,1)S(1)}, u32[]{:S(2)}, u32[]{:S(2)}) collective-permute-start(bf16[256,1152]{1,0:T(8,128)(2,1)S(1)} %collective-permute-done.3.refs_2_.refs_4_), channel_id=1, source_target_pairs={{0,4},{4,0},{1,5},{5,1},{2,6},{6,2},{3,7},{7,3},{8,12},{12,8},{9,1... | collective-permute-start | bytes 1769480 | tf_op jit(solution)/shard_map/ppermute | solution.py:245
  97.7 6.3 %collective-permute-start.8 = (bf16[256,1152]{1,0:T(8,128)(2,1)S(1)}, bf16[256,1152]{1,0:T(8,128)(2,1)S(1)}, u32[]{:S(2)}, u32[]{:S(2)}) collective-permute-start(bf16[256,1152]{1,0:T(8,128)(2,1)S(1)} %collective-permute-done.refs_1_.refs_3_), channel_id=1, source_target_pairs={{0,4},{4,0},{1,5},{5,1},{2,6},{6,2},{3,7},{7,3},{8,12},{12,8},{9,1... | collective-permute-start | bytes 1769480 | tf_op jit(solution)/shard_map/ppermute | solution.py:245
  98.6 5.4 %collective-permute-start.9 = (bf16[256,1152]{1,0:T(8,128)(2,1)S(1)}, bf16[256,1152]{1,0:T(8,128)(2,1)S(1)}, u32[]{:S(2)}, u32[]{:S(2)}) collective-permute-start(bf16[256,1152]{1,0:T(8,128)(2,1)S(1)} %collective-permute-done.1.refs_2_.refs_4_), channel_id=1, source_target_pairs={{0,4},{4,0},{1,5},{5,1},{2,6},{6,2},{3,7},{7,3},{8,12},{12,8},{9,1... | collective-permute-start | bytes 1769480 | tf_op jit(solution)/shard_map/ppermute | solution.py:245
  103.4 2.2 %collective-permute-start.7 = (f32[1,1536]{1,0:T(1,128)S(1)}, f32[1,1536]{1,0:T(1,128)S(1)}, u32[]{:S(2)}, u32[]{:S(2)}) collective-permute-start(f32[1,1536]{1,0:T(1,128)S(1)} %pad_maximum_fusion.1), channel_id=1, source_target_pairs={{0,4},{4,0},{1,5},{5,1},{2,6},{6,2},{3,7},{7,3},{8,12},{12,8},{9,1... | collective-permute-start | bytes 18440 | tf_op jit(solution)/shard_map/ppermute | solution.py:245

commit v11 on v10

--- a/solution.py
+++ b/solution.py
@@ -285,6 +285,7 @@
     plan = (
         ((0, 0), (0, 0), False),
         *(((0, 0), (k, b), True) for k, b in ((1, 0), (2, 0), (3, 0), (3, 1), (4, 0), (4, 1))),
+        ((1, 0), (2, 0), False),
     )
     best_second, best_first, best_first_there, *best = compare(
         core,
@@ -299,15 +300,10 @@
         "compare_second",
     )
     theirs = other_core(jnp.concatenate([best[1], best_first_there], axis=1))
-    best_first, best_second = compare(
+    [best_second] = compare(
         core,
-        [
-            (far[0], best_first, True),
-            (far[1], best_second, True),
-            (far_there[0], None, False),
-            (far_there[1], None, False),
-        ],
-        (((0, 0), (2, 0), False), ((1, 0), (3, 0), False)),
+        [(far[1], best_second, True), (far_there[1], None, False)],
+        (((0, 0), (1, 0), False),),
         "compare_cores",
     )
     count = near.shape[0]

time: 127 us -> 127 us (level)
  transfers between devices with their start and end apart: 10 -> 10, of which waited for: 4 -> 4; matrix products, arithmetic and copies ran while one was open for 0% -> 0% of each run, Pallas kernels for 10% -> 11%
where the time goes in v11:
time: 127 us; the launch traced here: 126 us
  blocking collectives  89.7 us (71%)
  Pallas kernels  17.6 us (14%)
  starting transfers between devices  11.8 us (9%)
  waiting for transfers between devices  5.55 us (4%)
    all_to_all x2, blocking collectives, exchange(): return lax.all_to_all(a, TORUS, split_axis=0, concat_axis=0, tiled=True)  89.7 us
    pallas_call x4, Pallas kernels, compare(): pl.pallas_call(functools.partial(compare_kernel, plan, [(len(arrays), bes...  13.3 us
    ppermute x6, starting transfers between devices, other_core(): return lax.ppermute(a, 'core', [(0, 1), (1, 0)])  6.6 us
    ppermute x4, waiting for transfers between devices, to_home(): return lax.ppermute(a, ALL, pairs)  5.54 us
    ppermute x4, starting transfers between devices, to_home(): return lax.ppermute(a, ALL, pairs)  5.17 us
  transfers between devices with their start and end apart: 10, of which 4 were waited for; matrix products, arithmetic and copies ran while one was open for 0% of the time, Pallas kernels for 11%

profile of v11, /device:TPU:1, one launch (start us, length us, event | category | flops | bytes accessed | tf_op | source)
XLA Modules:
  0.0 126.4 jit_solution(17175193897023830970)
XLA Ops:
  0.0 0.1 pad_add_fusion.1.place_ref
  0.1 0.7 pad_add_fusion.labels_ref
  0.8 0.8 place.1
  1.6 0.4 copy-done
  2.0 1.8 %pack.1 = bf16[1024,1152]{1,0:T(8,128)(2,1)S(1)} custom-call(bf16[512,1024]{1,0:T(8,128)(2,1)S(1)} %copy-done, s32[1,512]{1,0:T(1,128)S(1)} %get-tuple-element.28.at_ref, bf16[128,512]{1,0:T(8,128)(2,1)S(1)} %get-tuple-element.29.digits_ref), custom_call_target="tpu_custom_call" | custom-call | tf_op jit(solution)/shard_map/pack/pallas_call | solution.py:87
  3.8 70.9 %all_to_all.16 = bf16[128,8,1152]{2,1,0:T(8,128)(2,1)S(1)} all-to-all(bf16[128,8,1152]{2,1,0:T(8,128)(2,1)S(1)} %bitcast.23), channel_id=1, replica_groups=mesh['z'=8,'y'=4,'core'=2,'x'=4] {'y','z','x'}, dimensions={0} | all-to-all | bytes 4718592 | tf_op jit(solution)/shard_map/all_to_all | solution.py:249
  74.7 4.3 %collective-permute-start.4 = (bf16[1024,1152]{1,0:T(8,128)(2,1)S(1)}, bf16[1024,1152]{1,0:T(8,128)(2,1)S(1)}, u32[]{:S(2)}, u32[]{:S(2)}) collective-permute-start(bf16[1024,1152]{1,0:T(8,128)(2,1)S(1)} %bitcast.19), channel_id=1, source_target_pairs={{0,4},{4,0},{1,5},{5,1},{2,6},{6,2},{3,7},{7,3},{8,12},{12,8},{9,1... | collective-permute-start | bytes 7077896 | tf_op jit(solution)/shard_map/ppermute | solution.py:245
  79.0 0.2 slice_bitcast_fusion
  79.2 1.3 %collective-permute-start.2 = (bf16[256,1152]{1,0:T(8,128)(2,1)S(1)}, bf16[256,1152]{1,0:T(8,128)(2,1)S(1)}, u32[]{:S(2)}, u32[]{:S(2)}) collective-permute-start(bf16[256,1152]{1,0:T(8,128)(2,1)S(1)} %get-tuple-element.52), channel_id=1, source_target_pairs={{1,2},{3,0},{5,13},{7,15},{8,9},{10,11},{12,20},{14,22},{17,18},{1... | collective-permute-start | bytes 1769480 | tf_op jit(solution)/shard_map/ppermute | solution.py:241
  80.5 1.3 %collective-permute-start.3 = (bf16[256,1152]{1,0:T(8,128)(2,1)S(1)}, bf16[256,1152]{1,0:T(8,128)(2,1)S(1)}, u32[]{:S(2)}, u32[]{:S(2)}) collective-permute-start(bf16[256,1152]{1,0:T(8,128)(2,1)S(1)} %get-tuple-element.51), channel_id=1, source_target_pairs={{1,0},{3,2},{5,29},{7,31},{8,11},{10,9},{12,4},{14,6},{17,16},{19,... | collective-permute-start | bytes 1769480 | tf_op jit(solution)/shard_map/ppermute | solution.py:241
  81.8 1.3 %collective-permute-start = (bf16[256,1152]{1,0:T(8,128)(2,1)S(1)}, bf16[256,1152]{1,0:T(8,128)(2,1)S(1)}, u32[]{:S(2)}, u32[]{:S(2)}) collective-permute-start(bf16[256,1152]{1,0:T(8,128)(2,1)S(1)} %get-tuple-element.54), channel_id=1, source_target_pairs={{1,2},{3,0},{5,13},{7,15},{8,9},{10,11},{12,20},{14,22},{17,18},{1... | collective-permute-start | bytes 1769480 | tf_op jit(solution)/shard_map/ppermute | solution.py:241
  83.1 1.3 %collective-permute-start.1 = (bf16[256,1152]{1,0:T(8,128)(2,1)S(1)}, bf16[256,1152]{1,0:T(8,128)(2,1)S(1)}, u32[]{:S(2)}, u32[]{:S(2)}) collective-permute-start(bf16[256,1152]{1,0:T(8,128)(2,1)S(1)} %get-tuple-element.53), channel_id=1, source_target_pairs={{1,0},{3,2},{5,29},{7,31},{8,11},{10,9},{12,4},{14,6},{17,16},{19,... | collective-permute-start | bytes 1769480 | tf_op jit(solution)/shard_map/ppermute | solution.py:241
  84.4 0.0 collective-permute-done.4.refs_2_.refs_4_.refs_8_
  84.4 3.5 %compare_near.1 = (f32[1,1024]{1,0:T(1,128)S(1)}, f32[1,1024]{1,0:T(1,128)S(1)}) custom-call(s32[1]{0:T(128)} %bitcast.refs_0_, bf16[1024,1152]{1,0:T(8,128)(2,1)S(1)} %bitcast.20, bf16[1024,1152]{1,0:T(8,128)(2,1)S(1)} %collective-permute-done.4.refs_2_.refs_4_.refs_8_), custom_call_target="tpu_custom_call" | custom-call | flops 3019898880 | bytes 4718592 | tf_op jit(solution)/shard_map/compare_near/pallas_call | solution.py:186
  87.8 3.5 %collective-permute-done.2.refs_1_.refs_3_ = bf16[256,1152]{1,0:T(8,128)(2,1)S(1)} collective-permute-done((bf16[256,1152]{1,0:T(8,128)(2,1)S(1)}, bf16[256,1152]{1,0:T(8,128)(2,1)S(1)}, u32[]{:S(2)}, u32[]{:S(2)}) %collective-permute-start.2) | collective-permute-done | bytes 589856 | tf_op jit(solution)/shard_map/ppermute | solution.py:241
  91.3 0.1 collective-permute-done.3.refs_2_.refs_4_
  91.4 0.9 collective-permute-start.5
  92.2 0.0 collective-permute-start.6
  92.3 3.5 %compare_first.1 = (f32[1,512]{1,0:T(1,128)S(1)}, f32[1,1024]{1,0:T(1,128)S(1)}, f32[1,1024]{1,0:T(1,128)S(1)}) custom-call(s32[1]{0:T(128)} %bitcast.refs_0_, bf16[256,1152]{1,0:T(8,128)(2,1)S(1)} %collective-permute-done.2.refs_1_.refs_3_, bf16[256,1152]{1,0:T(8,128)(2,1)S(1)} %collective-permute-done.3.refs_2_.refs_4_, bf16[1024,1152]{1,0:T(8,128)(2,1)S(1)} %bitcast.21, ...), custom_call_target="tpu_custom_call" | custom-call | flops 3019898880 | bytes 5898240 | tf_op jit(solution)/shard_map/compare_first/pallas_call | solution.py:186
  95.7 1.9 %collective-permute-done.refs_1_ = bf16[256,1152]{1,0:T(8,128)(2,1)S(1)} collective-permute-done((bf16[256,1152]{1,0:T(8,128)(2,1)S(1)}, bf16[256,1152]{1,0:T(8,128)(2,1)S(1)}, u32[]{:S(2)}, u32[]{:S(2)}) %collective-permute-start) | collective-permute-done | bytes 589856 | tf_op jit(solution)/shard_map/ppermute | solution.py:241
  97.6 0.1 collective-permute-done.1.refs_2_
  97.7 0.9 collective-permute-start.8
  98.6 0.0 collective-permute-start.9
  98.6 0.0 collective-permute-done.6.refs_6_
  98.6 5.4 %compare_second.1 = (f32[1,512]{1,0:T(1,128)S(1)}, f32[1,512]{1,0:T(1,128)S(1)}, f32[1,512]{1,0:T(1,128)S(1)}, f32[1,1024]{1,0:T(1,128)S(1)}, f32[1,1024]{1,0:T(1,128)S(1)}) custom-call(s32[1]{0:T(128)} %bitcast.refs_0_, bf16[256,1152]{1,0:T(8,128)(2,1)S(1)} %collective-permute-done.refs_1_, bf16[256,1152]{1,0:T(8,128)(2,1)S(1)} %collective-permute-done.1.refs_2_, ...), custom_call_target="tpu_custom_call" | custom-call | flops 4831838208 | bytes 8257536 | tf_op jit(solution)/shard_map/compare_second/pallas_call | solution.py:186
  104.0 0.6 collective-permute-start.7
  104.6 1.0 compare_cores.1
  105.7 0.1 reshape.24
  105.8 0.1 reshape.23
  105.8 0.1 pad_maximum_fusion
  105.9 18.8 %all_to_all.17 = f32[128,1,16]{2,1,0:T(1,128)} all-to-all(f32[128,1,16]{2,1,0:T(1,128)S(1)} %bitcast.24), channel_id=1, replica_groups=mesh['z'=8,'y'=4,'core'=2,'x'=4] {'y','z','x'}, dimensions={0} | all-to-all | bytes 16384 | tf_op jit(solution)/shard_map/all_to_all | solution.py:249
  124.7 1.7 %unpack.1 = f32[1,512]{1,0:T(1,128)} custom-call(f32[128,16]{1,0:T(8,128)} %bitcast.25, s32[1,512]{1,0:T(1,128)} %copy-done.1, s32[1,512]{1,0:T(1,128)} %copy-done.2), custom_call_target="tpu_custom_call" | custom-call | tf_op jit(solution)/shard_map/unpack/pallas_call | solution.py:222
  (14 shorter events, 0.1 us)
Async XLA Ops:
  0.8 1.2 copy-start
  1.6 73.1 %copy-start.1 = (s32[1,512]{1,0:T(1,128)}, s32[1,512]{1,0:T(1,128)S(1)}, u32[]{:S(2)}) copy-start(s32[1,512]{1,0:T(1,128)S(1)} %get-tuple-element.49.home_ref) | copy-start | bytes 6148
  1.6 73.1 %copy-start.2 = (s32[1,512]{1,0:T(1,128)}, s32[1,512]{1,0:T(1,128)S(1)}, u32[]{:S(2)}) copy-start(s32[1,512]{1,0:T(1,128)S(1)} %get-tuple-element.50.slot_ref) | copy-start | bytes 6148
  74.7 9.7 %collective-permute-start.4 = (bf16[1024,1152]{1,0:T(8,128)(2,1)S(1)}, bf16[1024,1152]{1,0:T(8,128)(2,1)S(1)}, u32[]{:S(2)}, u32[]{:S(2)}) collective-permute-start(bf16[1024,1152]{1,0:T(8,128)(2,1)S(1)} %bitcast.19), channel_id=1, source_target_pairs={{0,4},{4,0},{1,5},{5,1},{2,6},{6,2},{3,7},{7,3},{8,12},{12,8},{9,1... | collective-permute-start | bytes 7077896 | tf_op jit(solution)/shard_map/ppermute | solution.py:245
  79.2 12.1 %collective-permute-start.2 = (bf16[256,1152]{1,0:T(8,128)(2,1)S(1)}, bf16[256,1152]{1,0:T(8,128)(2,1)S(1)}, u32[]{:S(2)}, u32[]{:S(2)}) collective-permute-start(bf16[256,1152]{1,0:T(8,128)(2,1)S(1)} %get-tuple-element.52), channel_id=1, source_target_pairs={{1,2},{3,0},{5,13},{7,15},{8,9},{10,11},{12,20},{14,22},{17,18},{1... | collective-permute-start | bytes 1769480 | tf_op jit(solution)/shard_map/ppermute | solution.py:241
  80.5 10.9 %collective-permute-start.3 = (bf16[256,1152]{1,0:T(8,128)(2,1)S(1)}, bf16[256,1152]{1,0:T(8,128)(2,1)S(1)}, u32[]{:S(2)}, u32[]{:S(2)}) collective-permute-start(bf16[256,1152]{1,0:T(8,128)(2,1)S(1)} %get-tuple-element.51), channel_id=1, source_target_pairs={{1,0},{3,2},{5,29},{7,31},{8,11},{10,9},{12,4},{14,6},{17,16},{19,... | collective-permute-start | bytes 1769480 | tf_op jit(solution)/shard_map/ppermute | solution.py:241
  81.8 15.9 %collective-permute-start = (bf16[256,1152]{1,0:T(8,128)(2,1)S(1)}, bf16[256,1152]{1,0:T(8,128)(2,1)S(1)}, u32[]{:S(2)}, u32[]{:S(2)}) collective-permute-start(bf16[256,1152]{1,0:T(8,128)(2,1)S(1)} %get-tuple-element.54), channel_id=1, source_target_pairs={{1,2},{3,0},{5,13},{7,15},{8,9},{10,11},{12,20},{14,22},{17,18},{1... | collective-permute-start | bytes 1769480 | tf_op jit(solution)/shard_map/ppermute | solution.py:241
  83.1 14.6 %collective-permute-start.1 = (bf16[256,1152]{1,0:T(8,128)(2,1)S(1)}, bf16[256,1152]{1,0:T(8,128)(2,1)S(1)}, u32[]{:S(2)}, u32[]{:S(2)}) collective-permute-start(bf16[256,1152]{1,0:T(8,128)(2,1)S(1)} %get-tuple-element.53), channel_id=1, source_target_pairs={{1,0},{3,2},{5,29},{7,31},{8,11},{10,9},{12,4},{14,6},{17,16},{19,... | collective-permute-start | bytes 1769480 | tf_op jit(solution)/shard_map/ppermute | solution.py:241
  91.4 7.2 %collective-permute-start.5 = (bf16[256,1152]{1,0:T(8,128)(2,1)S(1)}, bf16[256,1152]{1,0:T(8,128)(2,1)S(1)}, u32[]{:S(2)}, u32[]{:S(2)}) collective-permute-start(bf16[256,1152]{1,0:T(8,128)(2,1)S(1)} %collective-permute-done.2.refs_1_.refs_3_), channel_id=1, source_target_pairs={{0,4},{4,0},{1,5},{5,1},{2,6},{6,2},{3,7},{7,3},{8,12},{12,8},{9,1... | collective-permute-start | bytes 1769480 | tf_op jit(solution)/shard_map/ppermute | solution.py:245
  92.2 6.3 %collective-permute-start.6 = (bf16[256,1152]{1,0:T(8,128)(2,1)S(1)}, bf16[256,1152]{1,0:T(8,128)(2,1)S(1)}, u32[]{:S(2)}, u32[]{:S(2)}) collective-permute-start(bf16[256,1152]{1,0:T(8,128)(2,1)S(1)} %collective-permute-done.3.refs_2_.refs_4_), channel_id=1, source_target_pairs={{0,4},{4,0},{1,5},{5,1},{2,6},{6,2},{3,7},{7,3},{8,12},{12,8},{9,1... | collective-permute-start | bytes 1769480 | tf_op jit(solution)/shard_map/ppermute | solution.py:245
  97.7 6.9 %collective-permute-start.8 = (bf16[256,1152]{1,0:T(8,128)(2,1)S(1)}, bf16[256,1152]{1,0:T(8,128)(2,1)S(1)}, u32[]{:S(2)}, u32[]{:S(2)}) collective-permute-start(bf16[256,1152]{1,0:T(8,128)(2,1)S(1)} %collective-permute-done.refs_1_), channel_id=1, source_target_pairs={{0,4},{4,0},{1,5},{5,1},{2,6},{6,2},{3,7},{7,3},{8,12},{12,8},{9,1... | collective-permute-start | bytes 1769480 | tf_op jit(solution)/shard_map/ppermute | solution.py:245
  98.6 6.0 %collective-permute-start.9 = (bf16[256,1152]{1,0:T(8,128)(2,1)S(1)}, bf16[256,1152]{1,0:T(8,128)(2,1)S(1)}, u32[]{:S(2)}, u32[]{:S(2)}) collective-permute-start(bf16[256,1152]{1,0:T(8,128)(2,1)S(1)} %collective-permute-done.1.refs_2_), channel_id=1, source_target_pairs={{0,4},{4,0},{1,5},{5,1},{2,6},{6,2},{3,7},{7,3},{8,12},{12,8},{9,1... | collective-permute-start | bytes 1769480 | tf_op jit(solution)/shard_map/ppermute | solution.py:245
  104.0 1.6 %collective-permute-start.7 = (f32[1,1536]{1,0:T(1,128)S(1)}, f32[1,1536]{1,0:T(1,128)S(1)}, u32[]{:S(2)}, u32[]{:S(2)}) collective-permute-start(f32[1,1536]{1,0:T(1,128)S(1)} %pad_maximum_fusion.1), channel_id=1, source_target_pairs={{0,4},{4,0},{1,5},{5,1},{2,6},{6,2},{3,7},{7,3},{8,12},{12,8},{9,1... | collective-permute-start | bytes 18440 | tf_op jit(solution)/shard_map/ppermute | solution.py:245
